TPU v7x, 32 devices: a whole 2x2x4 slice. The times are simulated.
32 devices in a mesh: head: 2 (over y), blk: 16 (over z, x, core).
Axes of the slice: x: 2, y: 2, z: 4, core: 2. Of those that a mesh axis runs over, the one named last changes fastest.
Arguments:
- block_input: bfloat16 [2, 4096, 1024], P(None, ('blk', 'head')), may hold values from -6 to 6
- qkv_weight: bfloat16 [1024, 3072], P(('blk', 'head')), may hold values from -0.1875 to 0.1875
- q_bias: bfloat16 [1024], P(('blk', 'head')), may hold values from -3 to 3
- v_bias: bfloat16 [1024], P(('blk', 'head')), may hold values from -0.3125 to 0.3125
- out_weight: bfloat16 [1024, 1024], P(('blk', 'head')), may hold values from -3 to 3
- out_bias: bfloat16 [1024], P(('blk', 'head')), may hold values from -3 to 3
- norm1_gain: bfloat16 [1024], P(('blk', 'head')), may hold values from 0.099609375 to 1.8984375
- norm1_shift: bfloat16 [1024], P(('blk', 'head')), may hold values from -3 to 3
- norm2_gain: bfloat16 [1024], P(('blk', 'head')), may hold values from 0.099609375 to 1.8984375
- norm2_shift: bfloat16 [1024], P(('blk', 'head')), may hold values from -3 to 3
- fc_weight: bfloat16 [1024, 4096], P(('blk', 'head')), may hold values from -0.1875 to 0.1875
- fc_bias: bfloat16 [4096], P(('blk', 'head')), may hold values from -3 to 3
- proj_weight: bfloat16 [4096, 1024], P(('blk', 'head')), may hold values from -0.09375 to 0.09375
- proj_bias: bfloat16 [1024], P(('blk', 'head')), may hold values from -3 to 3
- out_grad: bfloat16 [2, 4096, 1024], P(None, ('blk', 'head')), may hold values from -6 to 6
- dealt: int32 [2, 4096], replicated, may hold values from 0 to 4095, as said below
- lengths: int32 [2, 2], replicated, may hold values from 1024 to 3072, as said below
Outputs:
- block_output: bfloat16 [2, 4096, 1024], P(None, ('blk', 'head'))
- input_grad: bfloat16 [2, 4096, 1024], P(None, ('blk', 'head'))
- grad_qkv_weight: float32 [1024, 3072], P(('blk', 'head'))
- grad_q_bias: float32 [1024], P(('blk', 'head'))
- grad_v_bias: float32 [1024], P(('blk', 'head'))
- grad_out_weight: float32 [1024, 1024], P(('blk', 'head'))
- grad_out_bias: float32 [1024], P(('blk', 'head'))
- grad_norm1_gain: float32 [1024], P(('blk', 'head'))
- grad_norm1_shift: float32 [1024], P(('blk', 'head'))
- grad_norm2_gain: float32 [1024], P(('blk', 'head'))
- grad_norm2_shift: float32 [1024], P(('blk', 'head'))
- grad_fc_weight: float32 [1024, 4096], P(('blk', 'head'))
- grad_fc_bias: float32 [4096], P(('blk', 'head'))
- grad_proj_weight: float32 [4096, 1024], P(('blk', 'head'))
- grad_proj_bias: float32 [1024], P(('blk', 'head'))
Inputs may be any that keep to these rules, and one draw needn't show every extreme that they name: `dealt`: row b is a permutation of 0 to 4095: entry j is the packed position of the j-th stored token. Cut the packed order into 64 runs of 64 positions; each consecutive group of 128 stored tokens is run t followed by run 2 * 32 - 1 - t, each ascending, for a t of its own. Row b gives the lengths of micro-batch b's two sequences in packed order (the first holds the positions below lengths[b, 0]); they add up to 4096.
All inputs are finite; a program needn't handle non-finite values.
Results may differ from a plain program's by a relative error of at most 0.024.
Values may be sent and summed in bfloat16 or wider, within the bound.
No kernel may reach another device: no remote copies, remote signals or barrier semaphores. Data moves between devices by JAX's collectives and lax.ppermute only.
A program may use at most 384 MiB of HBM per device.

v0:
```python
import functools
import math

import jax
import jax.numpy as jnp
from jax import lax
from jax.experimental import pallas as pl
from jax.experimental.pallas import tpu as pltpu
from jax.sharding import Mesh
from jax.sharding import PartitionSpec as P

DH = 64


def gelu_tanh(values):
    inner = 0.7978845608028654 * (values + 0.044715 * values * values * values)
    return 0.5 * values * (1.0 + jnp.tanh(inner))


def normalize(values):
    centred = values - jnp.mean(values, axis=-1, keepdims=True)
    inverse = lax.rsqrt(jnp.mean(centred * centred, axis=-1, keepdims=True) + 1e-05)
    return (centred * inverse, inverse)


def norm_back(grad_normed, normed, inverse):
    return inverse * (
        grad_normed
        - jnp.mean(grad_normed, axis=-1, keepdims=True)
        - normed * jnp.mean(grad_normed * normed, axis=-1, keepdims=True)
    )


def product(left, right):
    return jnp.dot(left, right, preferred_element_type=jnp.float32)


def product_tn(left, right):
    return lax.dot_general(
        left, right, (((0,), (0,)), ((), ())), preferred_element_type=jnp.float32
    )


def product_nt(left, right):
    return lax.dot_general(
        left, right, (((1,), (1,)), ((), ())), preferred_element_type=jnp.float32
    )


def visible_pairs(query_pos, key_pos, boundary):
    same_side = (query_pos[:, None] >= boundary) == (key_pos[None, :] >= boundary)
    return same_side & (key_pos[None, :] <= query_pos[:, None])


def forward_tile(current, queries3, keys3, values3, visible, scale):
    running, total, accum = current
    scores = jnp.einsum("qhd,khd->hqk", queries3, keys3, preferred_element_type=jnp.float32) * scale
    scores = jnp.where(visible[None], scores, -1000000000.0)
    highest = jnp.maximum(running, jnp.max(scores, axis=-1))
    weights = jnp.where(visible[None], jnp.exp(scores - highest[..., None]), 0.0)
    factor = jnp.exp(running - highest)
    total = total * factor + jnp.sum(weights, axis=-1)
    accum = accum * factor[..., None] + jnp.einsum(
        "hqk,khd->hqd", weights.astype(jnp.bfloat16), values3, preferred_element_type=jnp.float32
    )
    return (highest, total, accum)


def general_forward(query_parts, pos_parts, positions, boundary, keys_group, values_group, key_span):
    heads_local, head_size = (query_parts[0].shape[1], query_parts[0].shape[2])
    scale = head_size ** (-0.5)

    def fold_keys(state, pieces, start):
        key_rows, value_rows = pieces
        count_rows = key_rows.shape[0]
        block_rows = math.gcd(count_rows, key_span)
        block_count = count_rows // block_rows

        def one_step(index, inner):
            offset = index * block_rows
            keys3 = lax.dynamic_slice_in_dim(key_rows, offset, block_rows).reshape(
                block_rows, heads_local, head_size
            )
            values3 = lax.dynamic_slice_in_dim(value_rows, offset, block_rows).reshape(
                block_rows, heads_local, head_size
            )
            key_pos = lax.dynamic_slice_in_dim(positions, offset, block_rows)
            part_queries = query_parts[0]
            visible = visible_pairs(pos_parts[0], key_pos, boundary)
            current = inner[0]
            result = forward_tile(current, part_queries, keys3, values3, visible, scale)
            updated = [result]
            return tuple(updated)

        return lax.fori_loop(0, block_count, one_step, state)

    initial = tuple(
        (
            (
                jnp.full((heads_local, part.shape[0]), -1000000000.0, jnp.float32),
                jnp.zeros((heads_local, part.shape[0]), jnp.float32),
                jnp.zeros((heads_local, part.shape[0], head_size), jnp.float32),
            )
            for part in query_parts
        )
    )
    return fold_keys(
        initial,
        (
            lax.all_gather(keys_group, "blk", axis=0, tiled=True),
            lax.all_gather(values_group, "blk", axis=0, tiled=True),
        ),
        jnp.int32(0),
    )


def backward_tile(current, queries3, grad3, log_total, delta, keys3, values3, visible, scale):
    grad_query, term = current
    scores = jnp.einsum("qhd,khd->hqk", queries3, keys3, preferred_element_type=jnp.float32) * scale
    scores = jnp.where(visible[None], scores, -1000000000.0)
    exact = jnp.where(visible[None], jnp.exp(scores - log_total[..., None]), 0.0)
    grad_probs = jnp.einsum("qhd,khd->hqk", grad3, values3, preferred_element_type=jnp.float32)
    grad_scores = (exact * (grad_probs - delta[..., None])).astype(jnp.bfloat16)
    grad_query = (
        grad_query
        + jnp.einsum("hqk,khd->hqd", grad_scores, keys3, preferred_element_type=jnp.float32) * scale
    )
    rounded = exact.astype(jnp.bfloat16)
    grad_values = jnp.einsum("hqk,qhd->khd", rounded, grad3, preferred_element_type=jnp.float32)
    grad_keys = (
        jnp.einsum("hqk,qhd->khd", grad_scores, queries3, preferred_element_type=jnp.float32)
        * scale
    )
    rows = keys3.shape[0]
    term = jnp.stack([grad_keys.reshape(rows, -1), grad_values.reshape(rows, -1)], axis=1)
    return (grad_query, term)


def general_backward(
    query_parts,
    grad_parts,
    total_parts,
    delta_parts,
    pos_parts,
    positions,
    boundary,
    keys_group,
    values_group,
    key_span,
    buffer_rows,
):
    heads_local, head_size = (query_parts[0].shape[1], query_parts[0].shape[2])
    scale = head_size ** (-0.5)

    def fold_keys(state, pieces, start):
        key_rows, value_rows = pieces
        count_rows = key_rows.shape[0]
        block_rows = math.gcd(count_rows, key_span)
        block_count = count_rows // block_rows

        def one_step(index, inner):
            offset = index * block_rows
            keys3 = lax.dynamic_slice_in_dim(key_rows, offset, block_rows).reshape(
                block_rows, heads_local, head_size
            )
            values3 = lax.dynamic_slice_in_dim(value_rows, offset, block_rows).reshape(
                block_rows, heads_local, head_size
            )
            key_pos = lax.dynamic_slice_in_dim(positions, offset, block_rows)
            grads_now, buffer = inner
            term = jnp.zeros((block_rows, 2, heads_local * head_size), jnp.float32)
            part_queries = query_parts[0]
            part_grads = grad_parts[0]
            part_total = total_parts[0]
            part_delta = delta_parts[0]
            visible = visible_pairs(pos_parts[0], key_pos, boundary)
            current = (grads_now[0], term)
            result = backward_tile(
                current,
                part_queries,
                part_grads,
                part_total,
                part_delta,
                keys3,
                values3,
                visible,
                scale,
            )
            updated = [result[0]]
            term = result[1]
            buffer = lax.dynamic_update_slice(buffer, term, (offset, 0, 0))
            return (tuple(updated), buffer)

        return lax.fori_loop(0, block_count, one_step, state)

    grads_init = tuple(
        (jnp.zeros((heads_local, part.shape[0], head_size), jnp.float32) for part in query_parts)
    )
    initial = (grads_init, jnp.zeros((buffer_rows, 2, heads_local * head_size), jnp.float32))
    return fold_keys(
        initial,
        (
            lax.all_gather(keys_group, "blk", axis=0, tiled=True),
            lax.all_gather(values_group, "blk", axis=0, tiled=True),
        ),
        jnp.int32(0),
    )


def general_body(
    block_input,
    qkv_weight,
    q_bias,
    v_bias,
    out_weight,
    out_bias,
    norm1_gain,
    norm1_shift,
    norm2_gain,
    norm2_shift,
    fc_weight,
    fc_bias,
    proj_weight,
    proj_bias,
    out_grad,
    dealt,
    lengths,
):
    micro_count, local_rows, width = block_input.shape
    head_devices = lax.axis_size("head")
    blk_devices = lax.axis_size("blk")
    group = local_rows * head_devices
    blk_index = lax.axis_index("blk")
    head_size = DH
    key_span = 1024
    part_count = group // group
    shards = (
        qkv_weight,
        q_bias,
        v_bias,
        out_weight,
        out_bias,
        norm1_gain,
        norm1_shift,
        norm2_gain,
        norm2_shift,
        fc_weight,
        fc_bias,
        proj_weight,
        proj_bias,
    )
    totals = [
        jnp.zeros((shard.shape[0] * blk_devices * head_devices,) + shard.shape[1:], jnp.float32)
        for shard in shards
    ]
    outputs = []
    input_grads = []
    for micro_index in range(micro_count):
        whole = (
            lax.all_gather(shards[0], ("blk", "head"), axis=0, tiled=True),
            lax.all_gather(shards[1], ("blk", "head"), axis=0, tiled=True),
            lax.all_gather(shards[2], ("blk", "head"), axis=0, tiled=True),
            lax.all_gather(shards[3], ("blk", "head"), axis=0, tiled=True),
            lax.all_gather(shards[4], ("blk", "head"), axis=0, tiled=True),
            lax.all_gather(shards[5], ("blk", "head"), axis=0, tiled=True),
            lax.all_gather(shards[6], ("blk", "head"), axis=0, tiled=True),
            lax.all_gather(shards[7], ("blk", "head"), axis=0, tiled=True),
            lax.all_gather(shards[8], ("blk", "head"), axis=0, tiled=True),
            lax.all_gather(shards[9], ("blk", "head"), axis=0, tiled=True),
            lax.all_gather(shards[10], ("blk", "head"), axis=0, tiled=True),
            lax.all_gather(shards[11], ("blk", "head"), axis=0, tiled=True),
            lax.all_gather(shards[12], ("blk", "head"), axis=0, tiled=True),
        )
        (
            w_qkv,
            b_query,
            b_value,
            w_out,
            b_out,
            gain_one,
            shift_one,
            gain_two,
            shift_two,
            w_fc,
            b_fc,
            w_proj,
            b_proj,
        ) = whole
        b_query = b_query.astype(jnp.float32)
        b_value = b_value.astype(jnp.float32)
        b_out = b_out.astype(jnp.float32)
        gain_one = gain_one.astype(jnp.float32)
        shift_one = shift_one.astype(jnp.float32)
        gain_two = gain_two.astype(jnp.float32)
        shift_two = shift_two.astype(jnp.float32)
        b_fc = b_fc.astype(jnp.float32)
        b_proj = b_proj.astype(jnp.float32)
        positions = dealt[micro_index]
        boundary = lengths[micro_index, 0]
        query_pos = lax.dynamic_slice_in_dim(positions, blk_index * group, group)
        inputs = block_input[micro_index].astype(jnp.float32)
        normed_one, inverse_one = normalize(inputs)
        act_one = (normed_one * gain_one + shift_one).astype(jnp.bfloat16)
        mixed = product(act_one, w_qkv)
        queries = (mixed[:, :width] + b_query).astype(jnp.bfloat16)
        keys = mixed[:, width : 2 * width].astype(jnp.bfloat16)
        values = (mixed[:, 2 * width :] + b_value).astype(jnp.bfloat16)
        heads_in = lax.all_to_all(
            jnp.stack([queries, keys, values], axis=1),
            "head",
            split_axis=2,
            concat_axis=0,
            tiled=True,
        )
        local_width = heads_in.shape[2]
        heads_local = local_width // head_size
        queries3 = heads_in[:, 0].reshape(group, heads_local, head_size)
        keys_group = heads_in[:, 1]
        values_group = heads_in[:, 2]
        query_parts = tuple((queries3 for index in range(part_count)))
        pos_parts = tuple((query_pos for index in range(part_count)))
        states = general_forward(
            query_parts, pos_parts, positions, boundary, keys_group, values_group, key_span
        )
        running = jnp.concatenate([state[0] for state in states], axis=1)
        total = jnp.concatenate([state[1] for state in states], axis=1)
        accum = jnp.concatenate([state[2] for state in states], axis=1)
        log_total = running + jnp.log(total)
        attn_heads = (
            (accum / total[..., None])
            .transpose(1, 0, 2)
            .reshape(group, local_width)
            .astype(jnp.bfloat16)
        )
        attended = lax.all_to_all(attn_heads, "head", split_axis=0, concat_axis=1, tiled=True)
        resid = inputs + product(attended, w_out) + b_out
        normed_two, inverse_two = normalize(resid)
        act_two = (normed_two * gain_two + shift_two).astype(jnp.bfloat16)
        pre = product(act_two, w_fc) + b_fc
        hidden = gelu_tanh(pre).astype(jnp.bfloat16)
        outputs.append((resid + product(hidden, w_proj) + b_proj).astype(jnp.bfloat16))
        cotangent = out_grad[micro_index]
        grad_proj_w = product_tn(hidden, cotangent)
        grad_proj_b = jnp.sum(cotangent.astype(jnp.float32), axis=0)
        grad_hidden = product_nt(cotangent, w_proj)
        grad_pre = jax.vjp(gelu_tanh, pre)[1](grad_hidden)[0].astype(jnp.bfloat16)
        grad_fc_w = product_tn(act_two, grad_pre)
        grad_fc_b = jnp.sum(grad_pre.astype(jnp.float32), axis=0)
        grad_act_two = product_nt(grad_pre, w_fc)
        grad_gain_two = jnp.sum(grad_act_two * normed_two, axis=0)
        grad_shift_two = jnp.sum(grad_act_two, axis=0)
        grad_resid = cotangent.astype(jnp.float32) + norm_back(
            grad_act_two * gain_two, normed_two, inverse_two
        )
        grad_branch = grad_resid.astype(jnp.bfloat16)
        grad_out_w = product_tn(attended, grad_branch)
        grad_out_b = jnp.sum(grad_branch.astype(jnp.float32), axis=0)
        grad_attn = product_nt(grad_branch, w_out).astype(jnp.bfloat16)
        grad_heads = lax.all_to_all(grad_attn, "head", split_axis=1, concat_axis=0, tiled=True)
        grad3 = grad_heads.reshape(group, heads_local, head_size)
        attn3 = attn_heads.reshape(group, heads_local, head_size)
        delta = jnp.sum(grad3.astype(jnp.float32) * attn3.astype(jnp.float32), axis=-1).T
        grad_parts = tuple((grad3 for index in range(part_count)))
        total_parts = tuple((log_total for index in range(part_count)))
        delta_parts = tuple((delta for index in range(part_count)))
        query_grads, buffer = general_backward(
            query_parts,
            grad_parts,
            total_parts,
            delta_parts,
            pos_parts,
            positions,
            boundary,
            keys_group,
            values_group,
            key_span,
            group * blk_devices,
        )
        kv_sums = lax.psum_scatter(buffer, "blk", scatter_dimension=0, tiled=True)
        grad_k_heads = kv_sums[:, 0].astype(jnp.bfloat16)
        grad_v_heads = kv_sums[:, 1].astype(jnp.bfloat16)
        grad_query = jnp.concatenate(list(query_grads), axis=1)
        grad_q_heads = (
            grad_query.transpose(1, 0, 2).reshape(group, local_width).astype(jnp.bfloat16)
        )
        grads_heads = jnp.stack([grad_q_heads, grad_k_heads, grad_v_heads], axis=1)
        back_tokens = lax.all_to_all(grads_heads, "head", split_axis=0, concat_axis=2, tiled=True)
        grad_mixed = back_tokens.reshape(local_rows, 3 * width)
        grad_qkv_w = product_tn(act_one, grad_mixed)
        grad_q_b = jnp.sum(back_tokens[:, 0].astype(jnp.float32), axis=0)
        grad_v_b = jnp.sum(back_tokens[:, 2].astype(jnp.float32), axis=0)
        grad_act_one = product_nt(grad_mixed, w_qkv)
        grad_gain_one = jnp.sum(grad_act_one * normed_one, axis=0)
        grad_shift_one = jnp.sum(grad_act_one, axis=0)
        input_grads.append(
            (grad_resid + norm_back(grad_act_one * gain_one, normed_one, inverse_one)).astype(
                jnp.bfloat16
            )
        )
        terms = (
            grad_qkv_w,
            grad_q_b,
            grad_v_b,
            grad_out_w,
            grad_out_b,
            grad_gain_one,
            grad_shift_one,
            grad_gain_two,
            grad_shift_two,
            grad_fc_w,
            grad_fc_b,
            grad_proj_w,
            grad_proj_b,
        )
        totals = [running_sum + term for running_sum, term in zip(totals, terms)]
    final = (
        lax.psum_scatter(totals[0], ("blk", "head"), scatter_dimension=0, tiled=True),
        lax.psum_scatter(totals[1], ("blk", "head"), scatter_dimension=0, tiled=True),
        lax.psum_scatter(totals[2], ("blk", "head"), scatter_dimension=0, tiled=True),
        lax.psum_scatter(totals[3], ("blk", "head"), scatter_dimension=0, tiled=True),
        lax.psum_scatter(totals[4], ("blk", "head"), scatter_dimension=0, tiled=True),
        lax.psum_scatter(totals[5], ("blk", "head"), scatter_dimension=0, tiled=True),
        lax.psum_scatter(totals[6], ("blk", "head"), scatter_dimension=0, tiled=True),
        lax.psum_scatter(totals[7], ("blk", "head"), scatter_dimension=0, tiled=True),
        lax.psum_scatter(totals[8], ("blk", "head"), scatter_dimension=0, tiled=True),
        lax.psum_scatter(totals[9], ("blk", "head"), scatter_dimension=0, tiled=True),
        lax.psum_scatter(totals[10], ("blk", "head"), scatter_dimension=0, tiled=True),
        lax.psum_scatter(totals[11], ("blk", "head"), scatter_dimension=0, tiled=True),
        lax.psum_scatter(totals[12], ("blk", "head"), scatter_dimension=0, tiled=True),
    )
    return (
        jnp.stack(outputs),
        jnp.stack(input_grads),
        final[0],
        final[1],
        final[2],
        final[3],
        final[4],
        final[5],
        final[6],
        final[7],
        final[8],
        final[9],
        final[10],
        final[11],
        final[12],
    )


RUN = 64
BLOCK = 512
NEG = -1000000000.0
VM = pltpu.VMEM
SM = pltpu.SMEM


def dot_nt(left, right):
    return lax.dot_general(left, right, (((1,), (1,)), ((), ())), preferred_element_type=jnp.float32)


def dot_nn(left, right):
    return lax.dot_general(left, right, (((1,), (0,)), ((), ())), preferred_element_type=jnp.float32)


def rows_at(index, size):
    return pl.ds(pl.multiple_of(index * size, size), size)


def first_block(start, bound):
    return jnp.where(start >= bound, bound // BLOCK, 0)


def forward_kernel(head_size, bound_ref, inloc, outloc, qkv, out, qs, ks, vs, attn_t, lse, vt, mixed):
    tokens = qkv.shape[0]
    runs = tokens // RUN
    scale = head_size ** (-0.5)
    bound = bound_ref[0]

    @pl.loop(0, runs)
    def _(run):
        rows = qkv[rows_at(inloc[run], RUN), :]
        here = rows_at(run, RUN)
        qs[here, :] = (rows[:, :head_size].astype(jnp.float32) * scale).astype(jnp.bfloat16)
        ks[here, :] = rows[:, head_size : 2 * head_size]
        vs[here, :] = rows[:, 2 * head_size :]

    @pl.loop(0, tokens // BLOCK)
    def _(block):
        here = rows_at(block, BLOCK)
        vt[:, here] = vs[here, :].astype(jnp.float32).T.astype(jnp.bfloat16)

    @pl.loop(0, tokens // BLOCK)
    def _(block):
        start = block * BLOCK
        here = rows_at(block, BLOCK)
        queries = qs[here, :]
        query_pos = start + lax.broadcasted_iota(jnp.int32, (1, BLOCK), 1)
        floor = jnp.where(query_pos >= bound, bound, 0)

        def scores_of(index, diagonal):
            keys = ks[rows_at(index, BLOCK), :]
            scores = dot_nt(keys, queries)
            key_pos = index * BLOCK + lax.broadcasted_iota(jnp.int32, (BLOCK, BLOCK), 0)
            visible = key_pos >= floor
            if diagonal:
                visible = visible & (key_pos <= query_pos)
            return jnp.where(visible, scores, NEG)

        scores = scores_of(block, True)
        highest = jnp.max(scores, axis=0, keepdims=True)
        weights = jnp.exp(scores - highest)
        total = jnp.sum(weights, axis=0, keepdims=True)
        accum = dot_nn(vt[:, here], weights.astype(jnp.bfloat16))

        def step(index, state):
            highest, total, accum = state
            scores = scores_of(index, False)
            higher = jnp.maximum(highest, jnp.max(scores, axis=0, keepdims=True))
            weights = jnp.exp(scores - higher)
            factor = jnp.exp(highest - higher)
            total = total * factor + jnp.sum(weights, axis=0, keepdims=True)
            accum = accum * factor + dot_nn(vt[:, rows_at(index, BLOCK)], weights.astype(jnp.bfloat16))
            return higher, total, accum

        highest, total, accum = lax.fori_loop(first_block(start, bound), block, step, (highest, total, accum))
        result = accum / total
        attn_t[:, here] = result.astype(jnp.bfloat16)
        lse[:, here] = highest + jnp.log(total)
        result = result.T.astype(jnp.bfloat16)
        for part in range(BLOCK // RUN):
            mixed[rows_at(outloc[block * (BLOCK // RUN) + part], RUN), :] = result[part * RUN : (part + 1) * RUN]

    chips, _, span = out.shape

    @pl.loop(0, chips)
    def _(chip):
        out[chip] = mixed[rows_at(chip, span), :].astype(jnp.float32).T.astype(jnp.bfloat16)


def attend_forward(bound, inloc, outloc, qkv, chips, head_size):
    tokens = qkv.shape[0]
    bf16 = jnp.bfloat16
    pairs = tokens * (tokens // 2)
    return pl.pallas_call(
        functools.partial(forward_kernel, head_size),
        out_shape=(
            jax.ShapeDtypeStruct((chips, head_size, tokens // chips), bf16),
            jax.ShapeDtypeStruct((tokens, head_size), bf16),
            jax.ShapeDtypeStruct((tokens, head_size), bf16),
            jax.ShapeDtypeStruct((tokens, head_size), bf16),
            jax.ShapeDtypeStruct((head_size, tokens), bf16),
            jax.ShapeDtypeStruct((1, tokens), jnp.float32),
        ),
        in_specs=[pl.BlockSpec(memory_space=SM)] * 3 + [pl.BlockSpec(memory_space=VM)],
        out_specs=[pl.BlockSpec(memory_space=VM)] * 6,
        scratch_shapes=[VM((head_size, tokens), bf16), VM((tokens, head_size), bf16)],
        compiler_params=pltpu.CompilerParams(vmem_limit_bytes=40 * 1024 * 1024),
        cost_estimate=pl.CostEstimate(flops=4 * 4 * pairs * head_size, bytes_accessed=tokens * 2048, transcendentals=pairs),
        name="attend_forward",
    )(bound, inloc, outloc, qkv)


def backward_kernel(
    head_size, count, share, bound_ref, inloc, outloc, grad_t, qs, ks, vs, attn_t, lse, *refs
):
    pieces = refs[:count]
    send_out, normed, raw, grads, kt, dk, dv, mixed, wide, moved, sem = refs[count:]
    tokens = qs.shape[0]
    runs = tokens // RUN
    scale = head_size ** (-0.5)
    bound = bound_ref[0]
    chips, _, span = grad_t.shape
    copies, filled = [], 0
    for piece in pieces:
        copies.append(pltpu.make_async_copy(piece, normed.at[pl.ds(filled, piece.shape[0])], sem))
        filled += piece.shape[0]
    for copy in copies:
        copy.start()

    @pl.loop(0, chips)
    def _(chip):
        mixed[rows_at(chip, span), :] = grad_t[chip, :head_size, :].astype(jnp.float32).T.astype(jnp.bfloat16)

    @pl.loop(0, runs)
    def _(run):
        grads[rows_at(run, RUN), :] = mixed[rows_at(outloc[run], RUN), :]

    @pl.loop(0, tokens // BLOCK)
    def _(block):
        here = rows_at(block, BLOCK)
        kt[:, here] = ks[here, :].astype(jnp.float32).T.astype(jnp.bfloat16)

    @pl.loop(0, tokens // BLOCK)
    def _(block):
        start = block * BLOCK
        here = rows_at(block, BLOCK)
        queries = qs[here, :]
        grad = grads[here, :]
        log_total = lse[:, here]
        delta = jnp.sum(grad.astype(jnp.float32).T * attn_t[:, here].astype(jnp.float32), axis=0, keepdims=True)
        query_pos = start + lax.broadcasted_iota(jnp.int32, (1, BLOCK), 1)
        floor = jnp.where(query_pos >= bound, bound, 0)

        def one(index, diagonal):
            there = rows_at(index, BLOCK)
            scores = dot_nt(ks[there, :], queries)
            key_pos = index * BLOCK + lax.broadcasted_iota(jnp.int32, (BLOCK, BLOCK), 0)
            visible = key_pos >= floor
            if diagonal:
                visible = visible & (key_pos <= query_pos)
            probs = jnp.where(visible, jnp.exp(scores - log_total), 0.0)
            grad_probs = dot_nt(vs[there, :], grad)
            grad_scores = (probs * (grad_probs - delta)).astype(jnp.bfloat16)
            return (
                dot_nn(probs.astype(jnp.bfloat16), grad),
                dot_nn(grad_scores, queries),
                dot_nn(kt[:, there], grad_scores),
                there,
            )

        grad_v, grad_k, grad_q, there = one(block, True)
        dv[there, :] = grad_v
        dk[there, :] = grad_k

        def step(index, grad_q):
            grad_v, grad_k, term, there = one(index, False)
            dv[there, :] += grad_v
            dk[there, :] += grad_k
            return grad_q + term

        grad_q = lax.fori_loop(first_block(start, bound), block, step, grad_q)
        wide[here, :head_size] = (grad_q.T * scale).astype(jnp.bfloat16)

    wide[:, head_size : 2 * head_size] = dk[...].astype(jnp.bfloat16)
    wide[:, 2 * head_size :] = dv[...].astype(jnp.bfloat16)

    size = 3 * head_size

    @pl.loop(0, runs)
    def _(run):
        moved[rows_at(outloc[run], RUN), :] = wide[rows_at(run, RUN), :]

    @pl.loop(0, chips)
    def _(chip):
        send_out[chip, :size, :] = moved[rows_at(chip, span), :].astype(jnp.float32).T.astype(jnp.bfloat16)

    @pl.loop(0, runs)
    def _(run):
        moved[rows_at(inloc[run], RUN), :] = wide[rows_at(run, RUN), :]

    for copy in copies:
        copy.wait()
    raw[...] = jnp.zeros_like(raw)

    @pl.loop(0, tokens // BLOCK)
    def _(block):
        here = rows_at(block, BLOCK)
        turned = moved[here, :].astype(jnp.float32).T.astype(jnp.bfloat16)
        raw[...] += dot_nn(turned, normed[here, :])

    product = raw[...].T
    sums = jnp.sum(wide[...].astype(jnp.float32), axis=0, keepdims=True)
    high = sums.astype(jnp.bfloat16).astype(jnp.float32)
    tail = jnp.concatenate([high, sums - high, jnp.zeros((14, size), jnp.float32)], axis=0)
    for chip in range(chips):
        first = chip // 2 * 4 * share + chip % 2 * share
        rows = jnp.concatenate([product[first : first + share], product[first + 2 * share : first + 3 * share], tail], axis=0)
        rows = jnp.concatenate([rows, jnp.zeros((rows.shape[0], span - size), jnp.float32)], axis=1)
        send_out[chip, size:, :] = rows.astype(jnp.bfloat16)


def attend_backward(bound, inloc, outloc, grad_t, qs, ks, vs, attn_t, lse, pieces, share):
    tokens, head_size = qs.shape
    chips = grad_t.shape[0]
    width = pieces[0].shape[1]
    bf16 = jnp.bfloat16
    pairs = tokens * (tokens // 2)
    return pl.pallas_call(
        functools.partial(backward_kernel, head_size, len(pieces), share),
        out_shape=jax.ShapeDtypeStruct((chips, 3 * head_size + 2 * share + 16, tokens // chips), bf16),
        in_specs=[pl.BlockSpec(memory_space=SM)] * 3 + [pl.BlockSpec(memory_space=VM)] * 6
        + [pl.BlockSpec(memory_space=pltpu.HBM)] * len(pieces),
        out_specs=pl.BlockSpec(memory_space=VM),
        scratch_shapes=[
            VM((tokens, width), bf16),
            VM((3 * head_size, width), jnp.float32),
            VM((tokens, head_size), bf16),
            VM((head_size, tokens), bf16),
            VM((tokens, head_size), jnp.float32),
            VM((tokens, head_size), jnp.float32),
            VM((tokens, head_size), bf16),
            VM((tokens, 3 * head_size), bf16),
            VM((tokens, 3 * head_size), bf16),
            pltpu.SemaphoreType.DMA,
        ],
        compiler_params=pltpu.CompilerParams(vmem_limit_bytes=48 * 1024 * 1024),
        cost_estimate=pl.CostEstimate(flops=4 * 10 * pairs * head_size, bytes_accessed=tokens * 4096, transcendentals=pairs),
        name="attend_backward",
    )(bound, inloc, outloc, grad_t, qs, ks, vs, attn_t, lse, *pieces)


HALF_STEP = 512


def gelu_pair(values):
    cubic = values * values
    inner = 0.7978845608028654 * values * (1.0 + 0.044715 * cubic)
    bent = jnp.tanh(inner)
    slope = 0.7978845608028654 * (1.0 + 0.134145 * cubic)
    half = 0.5 * (1.0 + bent)
    return values * half, half + 0.5 * values * (1.0 - bent * bent) * slope


def load_rows(table, pieces, targets, sem, wait):
    slot = 0
    for piece in pieces:
        count = piece.shape[0]

        @pl.loop(0, count)
        def _(index, piece=piece, slot=slot):
            chip = table[0, slot + index]
            for rows, target in targets(chip):
                copy = pltpu.make_async_copy(piece.at[index, rows], target, sem)
                if wait:
                    copy.wait()
                else:
                    copy.start()

        slot += count


def project_kernel(count, table, got, *refs):
    pieces, (part_out, sent, attn_in, w_out, sem) = refs[:count], refs[count:]
    chips, size, span = got.shape
    share = w_out.shape[0] // chips
    rows = span // 2

    def targets(chip):
        return [(pl.ds(0, share), w_out.at[rows_at(chip, share)])]

    load_rows(table, pieces, targets, sem, False)
    for chip in range(chips):
        micro, head = divmod(chip, chips // 2)
        for rel in range(2):
            column = (rel * 2 + micro) * rows
            attn_in[head * size : (head + 1) * size, column : column + rows] = got[chip, :, rel * rows : (rel + 1) * rows]
    load_rows(table, pieces, targets, sem, True)
    left = attn_in[...].astype(jnp.float32).T.astype(jnp.bfloat16)
    part = dot_nn(left, w_out[...])
    part_out[...] = part
    sent[...] = part.astype(jnp.bfloat16)


def project(table, got, pieces, share):
    chips, size, span = got.shape
    width = pieces[0].shape[2]
    tokens = 2 * span
    bf16 = jnp.bfloat16
    return pl.pallas_call(
        functools.partial(project_kernel, len(pieces)),
        out_shape=(
            jax.ShapeDtypeStruct((tokens, width), jnp.float32),
            jax.ShapeDtypeStruct((tokens, width), bf16),
            jax.ShapeDtypeStruct((chips // 2 * size, tokens), bf16),
        ),
        in_specs=[pl.BlockSpec(memory_space=SM), pl.BlockSpec(memory_space=VM)]
        + [pl.BlockSpec(memory_space=pltpu.HBM)] * len(pieces),
        out_specs=[pl.BlockSpec(memory_space=VM)] * 3,
        scratch_shapes=[VM((chips * share, width), bf16), pltpu.SemaphoreType.DMA],
        compiler_params=pltpu.CompilerParams(vmem_limit_bytes=58 * 1024 * 1024),
        cost_estimate=pl.CostEstimate(
            flops=2 * tokens * chips * share * width, bytes_accessed=8 * tokens * width, transcendentals=0
        ),
        name="project",
    )(table, got, *pieces)


def middle_kernel(count, share, table, x_a, x_b, g_a, g_b, part, got_a, got_b, *refs):
    pieces = refs[:count]
    (resid, base, other, grad_act, grad_sent, fc_sums, vectors, terms) = refs[count : count + 8]
    (smalls, fc_bias, w_fc, w_proj, g_all, act, act_t, rest, proj_buf, fc_buf, small_sem, load_sem, proj_sem, fc_sem) = refs[count + 8 :]
    f32, bf16 = jnp.float32, jnp.bfloat16
    tokens, width = part.shape
    own = tokens // 2
    hidden = w_proj.shape[0]
    chips = terms.shape[0]
    each = hidden // chips
    folds = hidden // width
    fc_row = share + each

    def targets(chip):
        wanted = [(pl.ds(share, each), w_proj.at[rows_at(chip, each)])]
        for fold in range(folds):
            for core in range(2):
                first = fc_row + (fold * 2 + core) * share
                place = ((chip // 2) * 2 + core) * 2 + chip % 2
                wanted.append(
                    (pl.ds(first, share), w_fc.at[rows_at(place, share), pl.ds(fold * width, width)])
                )
        return wanted

    def small_targets(chip):
        return [(pl.ds(pieces[0].shape[1] - 16, 16), smalls.at[chip])]

    load_rows(table, pieces, small_targets, small_sem, False)
    load_rows(table, pieces, targets, load_sem, False)
    load_rows(table, pieces, small_targets, small_sem, True)
    small_sum = jnp.sum(smalls[...].astype(f32), axis=0)
    vectors[...] = small_sum[:8]
    for fold in range(folds):
        fc_bias[:, fold * width : (fold + 1) * width] = small_sum[8 + fold : 9 + fold]
    for half, (x_in, g_in, arrived) in enumerate(((x_a, g_a, got_a), (x_b, g_b, got_b))):
        here = slice(half * own, (half + 1) * own)
        g_all[here, :] = g_in[...]
        value = x_in[...].astype(f32) + part[here, :] + arrived[...].astype(f32) + vectors[2:3, :]
        resid[here, :] = value
        centred = value - jnp.mean(value, axis=-1, keepdims=True)
        inverse = lax.rsqrt(jnp.mean(centred * centred, axis=-1, keepdims=True) + 1e-05)
        rounded = (centred * inverse * vectors[0:1, :] + vectors[1:2, :]).astype(bf16)
        act[here, :] = rounded
        act_t[:, here] = rounded.astype(f32).T.astype(bf16)
    base[...] = resid[:own, :] + vectors[3:4, :]
    load_rows(table, pieces, targets, load_sem, True)

    per_step = HALF_STEP // each

    def copies(step, slot):
        made = []
        for index in range(per_step):
            made.append(
                pltpu.make_async_copy(
                    proj_buf.at[slot, pl.ds(index * each, each)],
                    terms.at[table[1, step * per_step + index], pl.ds(0, each)],
                    proj_sem.at[slot],
                )
            )
        fold = step // (width // HALF_STEP)
        column = pl.multiple_of(step % (width // HALF_STEP) * HALF_STEP, HALF_STEP)
        for chip in range(chips):
            for core in range(2):
                place = ((chip // 2) * 2 + core) * 2 + chip % 2
                made.append(
                    pltpu.make_async_copy(
                        fc_buf.at[slot, pl.ds(place * share, share)],
                        terms.at[
                            table[1, chip],
                            pl.ds(pl.multiple_of(each + share + (fold * 2 + core) * share, 16), share),
                            pl.ds(column, HALF_STEP),
                        ],
                        fc_sem.at[slot],
                    )
                )
        return made

    steps = hidden // HALF_STEP

    @pl.loop(0, steps)
    def _(step):
        slot = step % 2
        columns = pl.ds(pl.multiple_of(step * HALF_STEP, HALF_STEP), HALF_STEP)
        rows = rows_at(step, HALF_STEP)

        @pl.when(step >= 2)
        def _():
            for copy in copies(step - 2, slot):
                copy.wait()

        grads = g_all[...]
        value, slope = gelu_pair(dot_nn(act[...], w_fc[:, columns]) + fc_bias[:, columns])
        value = value.astype(bf16)
        proj_buf[slot] = dot_nn(value.astype(f32).T.astype(bf16), grads).astype(bf16)
        grad_pre = (dot_nt(grads, w_proj[rows, :]) * slope).astype(bf16)
        fc_sums[:, columns] = jnp.sum(grad_pre.astype(f32), axis=0, keepdims=True)
        fc_buf[slot] = dot_nn(act_t[...], grad_pre).astype(bf16)
        for copy in copies(step, slot):
            copy.start()
        projected = dot_nn(value, w_proj[rows, :])
        back = dot_nt(grad_pre, w_fc[:, columns])
        base[...] += projected[:own]

        @pl.when(step == 0)
        def _():
            grad_act[...] = back
            rest[...] = projected[own:]

        @pl.when(step > 0)
        def _():
            grad_act[...] += back
            rest[...] += projected[own:]

    other[...] = rest[...].astype(bf16)
    grad_sent[...] = grad_act[...].astype(bf16)
    for step in range(steps - 2, steps):
        for copy in copies(step, step % 2):
            copy.wait()


def middle(table, x_a, x_b, g_a, g_b, part, got_a, got_b, pieces, share, hidden):
    tokens, width = part.shape
    f32, bf16 = jnp.float32, jnp.bfloat16
    chips = table.shape[1]
    each = hidden // chips
    rows = share + each + 2 * share * (hidden // width)
    shape = jax.ShapeDtypeStruct
    return pl.pallas_call(
        functools.partial(middle_kernel, len(pieces), share),
        out_shape=(
            shape((tokens, width), f32),
            shape((tokens // 2, width), f32),
            shape((tokens // 2, width), bf16),
            shape((tokens, width), f32),
            shape((tokens, width), bf16),
            shape((1, hidden), f32),
            shape((8, width), f32),
            shape((chips, rows, width), bf16),
        ),
        in_specs=[pl.BlockSpec(memory_space=SM)]
        + [pl.BlockSpec(memory_space=VM)] * 7
        + [pl.BlockSpec(memory_space=pltpu.HBM)] * len(pieces),
        out_specs=[pl.BlockSpec(memory_space=VM)] * 7 + [pl.BlockSpec(memory_space=pltpu.HBM)],
        scratch_shapes=[
            VM((chips, 16, width), bf16),
            VM((1, hidden), f32),
            VM((width, hidden), bf16),
            VM((hidden, width), bf16),
            VM((tokens, width), bf16),
            VM((tokens, width), bf16),
            VM((width, tokens), bf16),
            VM((tokens // 2, width), f32),
            VM((2, HALF_STEP, width), bf16),
            VM((2, width, HALF_STEP), bf16),
            pltpu.SemaphoreType.DMA,
            pltpu.SemaphoreType.DMA,
            pltpu.SemaphoreType.DMA((2,)),
            pltpu.SemaphoreType.DMA((2,)),
        ],
        compiler_params=pltpu.CompilerParams(vmem_limit_bytes=56 * 1024 * 1024),
        cost_estimate=pl.CostEstimate(
            flops=12 * tokens * width * hidden, bytes_accessed=8 * width * hidden, transcendentals=tokens * hidden
        ),
        name="middle",
    )(table, x_a, x_b, g_a, g_b, part, got_a, got_b, *pieces)


def branch_kernel(share, row, table, resid, g_a, g_b, part, got_a, got_b, vectors, fc_sums, attn_in, given, grad_resid, branch, tails, terms, products, sem):
    f32, bf16 = jnp.float32, jnp.bfloat16
    tokens, width = resid.shape
    own = tokens // 2
    chips = tails.shape[0]
    gain_sum = jnp.zeros((1, width), f32)
    shift_sum = jnp.zeros((1, width), f32)
    bias_sum = jnp.zeros((1, width), f32)
    proj_sum = jnp.zeros((1, width), f32)
    for half, (g_in, arrived) in enumerate(((g_a, got_a), (g_b, got_b))):
        here = slice(half * own, (half + 1) * own)
        value = resid[here, :]
        centred = value - jnp.mean(value, axis=-1, keepdims=True)
        inverse = lax.rsqrt(jnp.mean(centred * centred, axis=-1, keepdims=True) + 1e-05)
        normed = centred * inverse
        grad = part[here, :] + arrived[...].astype(f32)
        gain_sum += jnp.sum(grad * normed, axis=0, keepdims=True)
        shift_sum += jnp.sum(grad, axis=0, keepdims=True)
        scaled = grad * vectors[0:1, :]
        given_grad = g_in[...].astype(f32)
        total = given_grad + inverse * (
            scaled
            - jnp.mean(scaled, axis=-1, keepdims=True)
            - normed * jnp.mean(scaled * normed, axis=-1, keepdims=True)
        )
        rounded = total.astype(bf16)
        bias_sum += jnp.sum(rounded.astype(f32), axis=0, keepdims=True)
        proj_sum += jnp.sum(given_grad, axis=0, keepdims=True)
        branch[here, :] = rounded
        if half == 0:
            grad_resid[...] = total
    group = width // (chips // 2)
    sums = jnp.concatenate([gain_sum, shift_sum, bias_sum, proj_sum], axis=0)
    each = fc_sums.shape[1] // chips
    for chip in range(chips):
        first = chip // 2 * group
        tail = jnp.concatenate(
            [
                sums[:, first : first + group],
                fc_sums[:, chip * each : (chip + 1) * each],
                jnp.zeros((3, group), f32),
            ],
            axis=0,
        )
        high = tail.astype(bf16)
        low = (tail - high.astype(f32)).astype(bf16)
        tails[chip] = jnp.concatenate([high, low], axis=1)
    products[...] = dot_nn(attn_in[...], branch[...]).astype(bf16)

    @pl.loop(0, chips)
    def _(chip):
        pltpu.make_async_copy(products.at[rows_at(chip, share)], terms.at[table[1, chip], pl.ds(row, share)], sem).start()

    @pl.loop(0, chips)
    def _(chip):
        pltpu.make_async_copy(products.at[rows_at(chip, share)], terms.at[table[1, chip], pl.ds(row, share)], sem).wait()


def branch_back(table, resid, g_a, g_b, part, got_a, got_b, vectors, fc_sums, attn_in, terms, share, row, span):
    tokens, width = resid.shape
    f32, bf16 = jnp.float32, jnp.bfloat16
    chips = table.shape[1]
    shape = jax.ShapeDtypeStruct
    return pl.pallas_call(
        functools.partial(branch_kernel, share, row),
        out_shape=(
            shape((tokens // 2, width), f32),
            shape((tokens, width), bf16),
            shape((chips, 8, span), bf16),
            shape(terms.shape, bf16),
        ),
        in_specs=[pl.BlockSpec(memory_space=SM)]
        + [pl.BlockSpec(memory_space=VM)] * 9
        + [pl.BlockSpec(memory_space=pltpu.HBM)],
        out_specs=[pl.BlockSpec(memory_space=VM)] * 3 + [pl.BlockSpec(memory_space=pltpu.HBM)],
        scratch_shapes=[VM((chips * share, width), bf16), pltpu.SemaphoreType.DMA],
        input_output_aliases={10: 3},
        compiler_params=pltpu.CompilerParams(vmem_limit_bytes=40 * 1024 * 1024),
        cost_estimate=pl.CostEstimate(
            flops=2 * tokens * chips * share * width, bytes_accessed=16 * tokens * width, transcendentals=0
        ),
        name="branch_back",
    )(table, resid, g_a, g_b, part, got_a, got_b, vectors, fc_sums, attn_in, terms)


def attention_back_kernel(count, table, branch, tails, *refs):
    pieces, (sent, w_out, sem) = refs[:count], refs[count:]
    chips, size, span = sent.shape
    size -= 8
    rows = span // 2
    share = w_out.shape[0] // chips

    def targets(chip):
        return [(pl.ds(0, share), w_out.at[rows_at(chip, share)])]

    load_rows(table, pieces, targets, sem, False)
    sent[:, size:, :] = tails[...]
    load_rows(table, pieces, targets, sem, True)
    grads = dot_nt(w_out[...], branch[...]).astype(jnp.bfloat16)
    for chip in range(chips):
        micro, head = divmod(chip, chips // 2)
        for rel in range(2):
            column = (rel * 2 + micro) * rows
            sent[chip, :size, rel * rows : (rel + 1) * rows] = grads[
                head * size : (head + 1) * size, column : column + rows
            ]


def attention_back(table, branch, tails, pieces, share, size):
    tokens, width = branch.shape
    chips, _, span = tails.shape
    bf16 = jnp.bfloat16
    return pl.pallas_call(
        functools.partial(attention_back_kernel, len(pieces)),
        out_shape=jax.ShapeDtypeStruct((chips, size + 8, span), bf16),
        in_specs=[pl.BlockSpec(memory_space=SM)]
        + [pl.BlockSpec(memory_space=VM)] * 2
        + [pl.BlockSpec(memory_space=pltpu.HBM)] * len(pieces),
        out_specs=pl.BlockSpec(memory_space=VM),
        scratch_shapes=[VM((chips * share, width), bf16), pltpu.SemaphoreType.DMA],
        compiler_params=pltpu.CompilerParams(vmem_limit_bytes=58 * 1024 * 1024),
        cost_estimate=pl.CostEstimate(
            flops=2 * tokens * chips * share * width, bytes_accessed=4 * tokens * width, transcendentals=0
        ),
        name="attention_back",
    )(table, branch, tails, *pieces)


def finish_kernel(order, got, weights, kept, sent, weight, grads, sem):
    chips, _, span = got.shape
    size = weight.shape[0] // len(order)
    rows = span // 2
    own = kept.shape[0]

    def copies():
        return [
            pltpu.make_async_copy(weights.at[slot], weight.at[pl.ds(head * size, size)], sem)
            for slot, head in enumerate(order)
        ]

    for copy in copies():
        copy.start()
    for chip in range(chips):
        micro, head = divmod(chip, chips // 2)
        turned = got[chip, :size, :].astype(jnp.float32).T.astype(jnp.bfloat16)
        for rel in range(2):
            row = (rel * 2 + micro) * rows
            grads[head, row : row + rows, :] = turned[rel * rows : (rel + 1) * rows]
    for copy in copies():
        copy.wait()
    left = jnp.concatenate([grads[head] for head in range(len(order))], axis=1)
    back = dot_nn(left, weight[...])
    kept[...] = back[:own]
    sent[...] = back[own:].astype(jnp.bfloat16)


def finish(got, weights, order):
    chips, _, span = got.shape
    heads, size, width = weights.shape
    bf16 = jnp.bfloat16
    return pl.pallas_call(
        functools.partial(finish_kernel, order),
        out_shape=(
            jax.ShapeDtypeStruct((span, width), jnp.float32),
            jax.ShapeDtypeStruct((span, width), bf16),
        ),
        in_specs=[pl.BlockSpec(memory_space=VM), pl.BlockSpec(memory_space=pltpu.HBM)],
        out_specs=[pl.BlockSpec(memory_space=VM)] * 2,
        scratch_shapes=[
            VM((heads * size, width), bf16),
            VM((heads, 2 * span, size), bf16),
            pltpu.SemaphoreType.DMA,
        ],
        compiler_params=pltpu.CompilerParams(vmem_limit_bytes=58 * 1024 * 1024),
        cost_estimate=pl.CostEstimate(
            flops=4 * span * width * heads * size,
            bytes_accessed=2 * width * heads * size + 8 * span * width,
            transcendentals=0,
        ),
        name="finish",
    )(got, weights)


PATHS = (("x", "z", "head"), ("head", "z", "x"))


PAIR = [(0, 1), (1, 0)]
NEAR = [(0, 1), (1, 0), (2, 3), (3, 2)]
FAR = [(0, 2), (2, 0), (1, 3), (3, 1)]


def swap(values, axis, pairs=PAIR):
    return lax.ppermute(values, axis, pairs)


def across(values, axis):
    return swap(values, axis, NEAR if axis == "z" else PAIR)


def in_order(mine, other, index, axis):
    first = jnp.where(index == 0, mine, other)
    second = jnp.where(index == 0, other, mine)
    return jnp.stack([first, second], axis=axis)


def split_float(values):
    high = values.astype(jnp.bfloat16)
    low = (values - high.astype(jnp.float32)).astype(jnp.bfloat16)
    return high, low


def run_table(order, pair_start):
    pairs = order.shape[0]
    runs = jnp.arange(2 * pairs, dtype=jnp.int32)[:, None]
    low = jnp.where(runs == order[None, :], pair_start[None, :], 0)
    high = jnp.where(runs == 2 * pairs - 1 - order[None, :], pair_start[None, :] + 1, 0)
    return jnp.sum(low + high, axis=1).astype(jnp.int32)


def ring_order(count, turn):
    half = [(z, (z + step + turn) % 2) for z in range(count) for step in range(2)]
    return [z * 4 + y for z, y in half] + [z * 4 + 2 + y for z, y in reversed(half)]


def core_groups(rings):
    return [[(chip // 2 * 2 + core) * 2 + chip % 2 for chip in ring] for core, ring in enumerate(rings)]


def cube_orders(depth):
    cycle = [0, 1, 3, 2, 6, 7, 5, 4]
    return [[chip + start for chip in cycle] for start in (0, 4 * depth)]


def fast_body(
    block_input,
    qkv_weight,
    q_bias,
    v_bias,
    out_weight,
    out_bias,
    norm1_gain,
    norm1_shift,
    norm2_gain,
    norm2_shift,
    fc_weight,
    fc_bias,
    proj_weight,
    proj_bias,
    out_grad,
    dealt,
    lengths,
):
    f32, bf16 = jnp.float32, jnp.bfloat16
    micro, rows, width = block_input.shape
    nz, nx = lax.axis_size("z"), lax.axis_size("x")
    iz, ix, ic, iy = (lax.axis_index(name) for name in ("z", "x", "core", "head"))
    zx = nz * nx
    every, chips = ("z", "x", "core", "head"), ("z", "x", "head")
    devices, chip_count = 4 * zx, 2 * zx
    heads = 2 * zx
    local = heads * DH // 2
    share = qkv_weight.shape[0]
    hidden_share = proj_weight.shape[0]
    hidden_half = hidden_share * chip_count

    inputs = block_input.astype(f32)
    normed_one, inverse_one = normalize(inputs)
    n1 = normed_one.astype(bf16)
    n1, qkv_weight, fc_weight, norm1_gain, norm2_gain = lax.optimization_barrier(
        (n1, qkv_weight, fc_weight, norm1_gain, norm2_gain)
    )
    gain_one = norm1_gain.astype(f32)
    shift_one = norm1_shift.astype(f32)
    raw_qkv = qkv_weight.astype(f32)
    scaled_qkv = (raw_qkv * gain_one[:, None]).astype(bf16)
    device = ((iz * nx + ix) * 2 + ic) * 2 + iy
    offset = jnp.sum(raw_qkv * shift_one[:, None], axis=0)
    zero = jnp.zeros((width,), f32)
    place = device * share
    offset = offset + jnp.concatenate(
        [
            lax.dynamic_update_slice(zero, q_bias.astype(f32), (place,)),
            zero,
            lax.dynamic_update_slice(zero, v_bias.astype(f32), (place,)),
        ]
    )
    high, low = split_float(offset)
    to_heads = jnp.concatenate([scaled_qkv, high[None], low[None], jnp.zeros((6, 3 * width), bf16)], axis=0)
    to_heads = to_heads.reshape(share + 8, 3, zx // 2, 2, 2, DH).transpose(2, 4, 3, 0, 1, 5)
    to_heads = to_heads.reshape(1, heads, share + 8, 3 * DH)
    to_heads = jnp.broadcast_to(to_heads, (2, heads, share + 8, 3 * DH)).reshape(devices, share + 8, 3 * DH)
    head_rows = lax.all_to_all(to_heads, every, split_axis=0, concat_axis=0, tiled=True)
    head_weight = head_rows[:, :share].reshape(width, 3 * DH)
    head_offset = jnp.sum(head_rows[:, share : share + 2].astype(f32), axis=(0, 1))

    mine = iz // 2
    near = lax.dynamic_index_in_dim(n1, mine, 0, keepdims=False)
    far = swap(lax.dynamic_index_in_dim(n1, 1 - mine, 0, keepdims=False), "z", FAR)
    paths = PATHS
    got = across(near, paths[0][0])
    far, got = lax.optimization_barrier((far, got))
    near = jnp.stack([near, got])
    near_got, far_got = across(near, paths[0][1]), across(far, paths[1][0])
    near_got, far_got = lax.optimization_barrier((near_got, far_got))
    near, far = jnp.stack([near, near_got]), jnp.stack([far, far_got])
    near_got, far_got = across(near, paths[0][2]), across(far, paths[1][1])
    far = jnp.stack([far, far_got])
    parts = [near, near_got, far, across(far, paths[1][2])]
    pieces, owners = [], []

    def add_all(flip):
        core = 1 - ic if flip else ic
        for index, part in enumerate(parts):
            pieces.append((swap(part, "core") if flip else part).reshape(-1, width))
            for second in range(2):
                for first in range(2):
                    flips = dict(zip(paths[index // 2], (first, second, index % 2)))
                    owners.append((iz ^ flips["z"] ^ (index // 2 * 2), ix ^ flips["x"], core, iy ^ flips["head"]))

    add_all(False)
    add_all(True)
    slot_device = jnp.stack([((z * nx + x) * 2 + core) * 2 + y for z, x, core, y in owners]).astype(jnp.int32)
    my_dealt = lax.dynamic_index_in_dim(dealt, mine, 0, keepdims=False)
    order = my_dealt.reshape(devices, rows)[:, 0] // RUN
    slot_of = jnp.sum(
        jnp.where(jnp.arange(devices)[:, None] == slot_device[None, :], jnp.arange(devices)[None, :], 0), axis=1
    )
    inloc = run_table(order, (slot_of * 2).astype(jnp.int32))
    ids = jnp.arange(devices, dtype=jnp.int32)
    id_y, id_c, id_zx = ids % 2, ids // 2 % 2, ids // 4
    send_pair = (id_zx * 2 + id_y) * 2 + (id_c ^ ic)
    outloc = run_table(order, (send_pair * 2).astype(jnp.int32))
    bound = lax.dynamic_index_in_dim(lengths, mine, 0, keepdims=False)[:1]

    fc_parts = fc_weight.reshape(share, zx, 2, 2, hidden_share)

    def core_columns(values, index):
        return lax.dynamic_index_in_dim(values, index, 2, keepdims=False)

    fc_mine = core_columns(fc_parts, ic).reshape(share, hidden_half)
    fc_other = swap(core_columns(fc_parts, 1 - ic).reshape(share, hidden_half), "core")
    fc_pair = in_order(fc_mine, fc_other, ic, 0).reshape(2 * share, hidden_half)
    small = jnp.stack([norm2_gain, norm2_shift, out_bias, proj_bias])
    small_rows = jnp.zeros((16, width), bf16)
    small_rows = lax.dynamic_update_slice(small_rows, small, (0, place))
    other_place = (((iz * nx + ix) * 2 + 1 - ic) * 2 + iy) * share
    small_rows = lax.dynamic_update_slice(small_rows, swap(small, "core"), (0, other_place))
    fc_place = ((iz * nx + ix) * 2 + iy) * hidden_share
    small_rows = lax.dynamic_update_slice(small_rows, fc_bias[None], (8 + fc_place // width, fc_place % width))
    folds = hidden_half // width
    fc_folded = fc_pair.reshape(2 * share, folds, width).transpose(1, 0, 2).reshape(-1, width)
    packed = jnp.concatenate([out_weight, proj_weight, fc_folded, small_rows], axis=0)
    rings = [ring_order(nz, turn) for turn in range(2)]
    places = [[ring.index(chip) for chip in range(chip_count)] for ring in rings]
    table = lax.dynamic_index_in_dim(
        jnp.array([[ring, place] for ring, place in zip(rings, places)], jnp.int32), ic, 0, keepdims=False
    )
    gathered = lax.all_gather(packed, every, axis=0, axis_index_groups=core_groups(rings))
    out_rows = share
    proj_rows = hidden_share
    fc_rows = 2 * share * folds

    mixed = [(product(piece, head_weight) + head_offset).astype(bf16) for piece in pieces]
    slots = jnp.concatenate(mixed, axis=0)
    attn_send, queries, keys, values, attn_t, lse = attend_forward(bound, inloc, outloc, slots, chip_count, DH)

    x_a, x_b = block_input.reshape(-1, width), swap(block_input, "core").reshape(-1, width)
    g_a, g_b = out_grad.reshape(-1, width), swap(out_grad, "core").reshape(-1, width)
    own = micro * rows
    attn_got = lax.all_to_all(attn_send, chips, split_axis=0, concat_axis=0, tiled=True)
    weight_turned, attn_got = lax.optimization_barrier((head_weight.T, attn_got))
    cubes = cube_orders(nz // 2)
    w_qkv = lax.all_gather(weight_turned, chips, axis=0, axis_index_groups=cubes)
    part, sent, attn_in = project(table, attn_got, [gathered], share)
    resid, base, project_other, grad_part, sent_back, fc_sums, vectors, terms = middle(
        table, x_a, x_b, g_a, g_b, part, swap(sent[own:], "core"), swap(sent[:own], "core"), [gathered], share, hidden_half
    )
    grad_resid, branch, tails, terms = branch_back(
        table,
        resid,
        g_a,
        g_b,
        grad_part,
        swap(sent_back[own:], "core"),
        swap(sent_back[:own], "core"),
        vectors,
        fc_sums,
        attn_in,
        terms,
        share,
        proj_rows,
        2 * rows,
    )
    grad_send = attention_back(table, branch, tails, [gathered], share, DH)
    output = (base + swap(project_other, "core").astype(f32)).astype(bf16)

    grad_got = lax.all_to_all(grad_send, chips, split_axis=0, concat_axis=0, tiled=True)
    vector_sums = jnp.sum(grad_got[:, DH:].astype(f32), axis=0)
    vector_sums = vector_sums[:, :rows] + vector_sums[:, rows:]
    final_vectors = lax.dynamic_slice(vector_sums, (0, (ic * 2 + iy) * share), (4, share))
    final_fc_b = vector_sums[4]

    summed = lax.psum_scatter(
        terms, every, scatter_dimension=0, tiled=True, axis_index_groups=core_groups(rings)
    )[0]
    final_proj_w = summed[:proj_rows].astype(f32)
    final_out_w = summed[proj_rows : proj_rows + out_rows].astype(f32)
    fc_sum = summed[proj_rows + out_rows :].reshape(folds, 2, share, width)
    fc_keep = lax.dynamic_index_in_dim(fc_sum, ic, 1, keepdims=False)
    fc_give = swap(lax.dynamic_index_in_dim(fc_sum, 1 - ic, 1, keepdims=False), "core")

    def by_owner(values):
        return values.transpose(1, 0, 2).reshape(share, zx, 2, hidden_share)

    final_fc_w = in_order(by_owner(fc_keep), by_owner(fc_give), ic, 2).reshape(share, 2 * hidden_half).astype(f32)

    send_grads = attend_backward(
        bound, inloc, outloc, grad_got, queries, keys, values, attn_t, lse, pieces, share
    )
    grads_got = lax.all_to_all(send_grads, chips, split_axis=0, concat_axis=0, tiled=True)
    back_own, back_other = finish(grads_got, w_qkv, cubes[0])
    raw_got = grads_got[:, 3 * DH :, : 3 * DH].astype(f32)
    raw_sum = jnp.sum(raw_got.reshape(2, zx, 2 * share + 16, 3 * DH), axis=0)
    raw_parts = raw_sum[:, : 2 * share].reshape(zx, 2, share, 3 * DH)
    sums_mine = raw_sum[:, 2 * share : 2 * share + 1] + raw_sum[:, 2 * share + 1 : 2 * share + 2]
    raw_keep = jnp.concatenate([lax.dynamic_index_in_dim(raw_parts, ic, 1, keepdims=False), sums_mine], axis=1)
    raw_give = jnp.concatenate([lax.dynamic_index_in_dim(raw_parts, 1 - ic, 1, keepdims=False), sums_mine], axis=1)
    raw_all = in_order(raw_keep, swap(raw_give, "core"), ic, 1).reshape(heads, share + 1, 3, DH)
    raw_all = raw_all.transpose(1, 2, 0, 3).reshape(share + 1, 3 * width)
    raw_grad, all_sums = raw_all[:share], raw_all[share]
    final_qkv_w = raw_grad * gain_one[:, None] + shift_one[:, None] * all_sums[None, :]
    final_gain_one = jnp.sum(raw_grad * raw_qkv, axis=1)
    final_shift_one = jnp.sum(raw_qkv * all_sums[None, :], axis=1)
    final_q_b = lax.dynamic_slice(all_sums, (place,), (share,))
    final_v_b = lax.dynamic_slice(all_sums, (2 * width + place,), (share,))

    back_own = back_own + swap(back_other, "core").astype(f32)
    back_own = back_own.reshape(micro, rows, width)
    input_grad = grad_resid.reshape(micro, rows, width) + norm_back(back_own, normed_one, inverse_one)

    return (
        output.reshape(micro, rows, width),
        input_grad.astype(bf16),
        final_qkv_w,
        final_q_b,
        final_v_b,
        final_out_w,
        final_vectors[2],
        final_gain_one,
        final_shift_one,
        final_vectors[0],
        final_vectors[1],
        final_fc_w,
        final_fc_b,
        final_proj_w,
        final_vectors[3],
    )


def specs(names):
    rows, vector, tokens = P(names, None), P(names), P(None, names, None)
    weights = (rows, vector, vector, rows, vector, vector, vector, vector, vector, rows, vector, rows, vector)
    return (tokens, *weights, tokens, P(), P()), (tokens, tokens, *weights)


def solution(mesh):
    sizes = dict(mesh.shape)
    if sizes["head"] == 2 and sizes["blk"] == 16:
        fine = Mesh(mesh.devices.reshape(2, 4, 2, 2), ("head", "z", "x", "core"))
        given, made = specs(("z", "x", "core", "head"))
        return jax.shard_map(fast_body, mesh=fine, in_specs=given, out_specs=made, check_vma=False)
    given, made = specs(("blk", "head"))
    return jax.shard_map(general_body, mesh=mesh, in_specs=given, out_specs=made, check_vma=False)
```

profile of v0, /device:TPU:11, one launch (start us, length us, event | category | flops | bytes accessed | tf_op | source)
XLA Modules:
  0.0 386.3 jit_solution(11113311328902182985)
XLA Ops:
  15.4 2.4 collective-permute-start.2
  21.3 4.6 %all-to-all-start = ((bf16[32,40,192]{2,1,0:T(8,128)(2,1)}), bf16[32,40,192]{2,1,0:T(8,128)(2,1)S(1)}, u32[]{:S(2)}, u32[]{:S(2)}) async-start(bf16[32,40,192]{2,1,0:T(8,128)(2,1)} %bitcast.6), calls=%async_computation | async-start | bytes 1310720 | tf_op jit(solution)/shard_map/all_to_all | solution.py:1236
  26.0 9.5 %collective-permute-done.2 = bf16[128,1024]{1,0:T(8,128)(2,1)S(1)} collective-permute-done((bf16[128,1024]{1,0:T(8,128)(2,1)S(1)}, bf16[128,1024]{1,0:T(8,128)(2,1)S(1)}, u32[]{:S(2)}, u32[]{:S(2)}) %collective-permute-start.2) | collective-permute-done | bytes 262176 | tf_op jit(solution)/shard_map/ppermute | solution.py:1137
  38.0 2.6 collective-permute-start.5
  40.9 13.1 %collective-permute-done.5 = bf16[128,1024]{1,0:T(8,128)(2,1)S(1)} collective-permute-done((bf16[128,1024]{1,0:T(8,128)(2,1)}, bf16[128,1024]{1,0:T(8,128)(2,1)S(1)}, u32[]{:S(2)}, u32[]{:S(2)}) %collective-permute-start.5) | collective-permute-done | bytes 262176 | tf_op jit(solution)/shard_map/ppermute | solution.py:1137
  54.0 3.9 %collective-permute-done.4 = bf16[2,128,1024]{2,1,0:T(8,128)(2,1)S(1)} collective-permute-done((bf16[2,128,1024]{2,1,0:T(8,128)(2,1)S(1)}, bf16[2,128,1024]{2,1,0:T(8,128)(2,1)S(1)}, u32[]{:S(2)}, u32[]{:S(2)}) %collective-permute-start.4) | collective-permute-done | bytes 524320 | tf_op jit(solution)/shard_map/ppermute | solution.py:1137
  59.1 2.4 collective-permute-start.7
  62.8 3.0 collective-permute-start.6
  65.8 12.5 %collective-permute-done.7 = bf16[2,128,1024]{2,1,0:T(8,128)(2,1)S(1)} collective-permute-done((bf16[2,128,1024]{2,1,0:T(8,128)(2,1)S(1)}, bf16[2,128,1024]{2,1,0:T(8,128)(2,1)S(1)}, u32[]{:S(2)}, u32[]{:S(2)}) %collective-permute-start.7) | collective-permute-done | bytes 524320 | tf_op jit(solution)/shard_map/ppermute | solution.py:1137
  83.7 27.8 %collective-permute-done.6 = bf16[2,2,128,1024]{3,2,1,0:T(8,128)(2,1)} collective-permute-done((bf16[2,2,128,1024]{3,2,1,0:T(8,128)(2,1)S(1)}, bf16[2,2,128,1024]{3,2,1,0:T(8,128)(2,1)}, u32[]{:S(2)}, u32[]{:S(2)}) %collective-permute-start.6) | collective-permute-done | bytes 1048608 | tf_op jit(solution)/shard_map/ppermute | solution.py:1137
  122.1 24.4 %attend_forward.1 = (bf16[16,64,256]{2,1,0:T(8,128)(2,1)S(1)}, bf16[4096,64]{1,0:T(8,128)(2,1)S(1)}, bf16[4096,64]{1,0:T(8,128)(2,1)S(1)}, bf16[4096,64]{1,0:T(8...) custom-call(s32[1]{0:T(128)S(1)} %bitcast.168, s32[64]{0:T(128)S(1)} %get-tuple-element.86.inloc, ...), custom_call_target="tpu_custom_call" | custom-call | flops 8589934592 | bytes 8388608 | tf_op jit(solution)/shard_map/attend_forward/pallas_call | solution.py:544
  149.4 21.2 %all_to_all.20.got = bf16[16,64,256]{2,1,0:T(8,128)(2,1)} all-to-all(bf16[16,64,256]{2,1,0:T(8,128)(2,1)S(1)} %get-tuple-element.56), channel_id=1, replica_groups=mesh['head'=2,'z'=4,'x'=2,'core'=2] {'z','x','head'}, dimensions={0} | all-to-all | bytes 1048576 | tf_op jit(solution)/shard_map/all_to_all | solution.py:1314
  171.8 2.1 collective-permute-start
  174.6 4.9 %project.1 = (f32[512,1024]{1,0:T(8,128)}, bf16[512,1024]{1,0:T(8,128)(2,1)}, bf16[512,512]{1,0:T(8,128)(2,1)}) custom-call(s32[2,16]{1,0:T(2,128)} %fusion.36.table, bf16[16,64,256]{2,1,0:T(8,128)(2,1)} %all_to_all.20.got, bf16[16,304,1024]{2,1,0:T(8,128)(2,1)} %bitcast.170), custom_call_target="tpu_custom_call" | custom-call | flops 536870912 | bytes 4194304 | tf_op jit(solution)/shard_map/project/pallas_call | solution.py:759
  184.4 26.8 %middle.1 = (f32[512,1024]{1,0:T(8,128)}, f32[256,1024]{1,0:T(8,128)}, bf16[256,1024]{1,0:T(8,128)(2,1)}, f32[512,1024]{1,0:T(8,128)}, bf16[512,1024]{1,0:T(8,12...) custom-call(s32[2,16]{1,0:T(2,128)} %fusion.36.table, bf16[256,1024]{1,0:T(8,128)(2,1)} %bitcast.173, ...), custom_call_target="tpu_custom_call" | custom-call | flops 12884901888 | bytes 16777216 | tf_op jit(solution)/shard_map/middle/pallas_call | solution.py:905
  218.8 4.1 %branch_back.1 = (f32[256,1024]{1,0:T(8,128)S(1)}, bf16[512,1024]{1,0:T(8,128)(2,1)S(1)}, bf16[16,8,256]{2,1,0:T(8,128)(2,1)S(1)}, bf16[16,288,1024]{2,1,0:T(8,128)(2,1)}) custom-call(s32[2,16]{1,0:T(2,128)S(1)} %copy-done.12, f32[512,1024]{1,0:T(8,128)S(1)} %copy-done.2, bf16[256,1024]{1,0:T(8,128)(2,1)S(1)} %bitcast.165, ...), custom_call_target="tpu_custom_call", output_to_operand_aliasing={{3}: (10, {})} | custom-call | flops 536870912 | bytes 8388608 | tf_op jit(solution)/shard_map/branch_back/pallas_call | solution.py:1008
  224.6 4.3 %attention_back.1 = bf16[16,72,256]{2,1,0:T(8,128)(2,1)} custom-call(s32[2,16]{1,0:T(2,128)} %fusion.36.table, bf16[512,1024]{1,0:T(8,128)(2,1)} %copy-done.4, bf16[16,8,256]{2,1,0:T(8,128)(2,1)} %copy-done.10, bf16[16,304,1024]{2,1,0:T(8,128)(2,1)} %bitcast.172), custom_call_target="tpu_custom_call" | custom-call | flops 536870912 | bytes 2097152 | tf_op jit(solution)/shard_map/attention_back/pallas_call | solution.py:1057
  228.9 22.5 %all_to_all.21.grad_t = bf16[16,72,256]{2,1,0:T(8,128)(2,1)S(1)} all-to-all(bf16[16,72,256]{2,1,0:T(8,128)(2,1)} %attention_back.1), channel_id=1, replica_groups=mesh['head'=2,'z'=4,'x'=2,'core'=2] {'z','x','head'}, dimensions={0} | all-to-all | bytes 1179648 | tf_op jit(solution)/shard_map/all_to_all | solution.py:1341
  252.6 34.4 %attend_backward.1 = bf16[16,272,256]{2,1,0:T(8,128)(2,1)} custom-call(s32[1]{0:T(128)S(1)} %bitcast.169, s32[64]{0:T(128)S(1)} %get-tuple-element.86.inloc, s32[64]{0:T(128)S(1)} %get-tuple-element.85.outloc, bf16[16,72,256]{2,1,0:T(8,128)(2,1)S(1)} %all_to_all.21.grad_t, bf16[4096,64]{1,0:T(8,128)(2,1)S(1)} %copy-done.15, bf16[4096,64]{1,0:T(8,128)(2,1)S(1)} %copy-done.17, ...), custom_call_target="tpu_custom_call" | custom-call | flops 21474836480 | bytes 16777216 | tf_op jit(solution)/shard_map/attend_backward/pallas_call | solution.py:678
  287.1 5.4 %all-to-all-start.3 = ((bf16[16,272,256]{2,1,0:T(8,128)(2,1)}), bf16[16,272,256]{2,1,0:T(8,128)(2,1)}, u32[]{:S(2)}, u32[]{:S(2)}) async-start(bf16[16,272,256]{2,1,0:T(8,128)(2,1)} %attend_backward.1), calls=%async_computation.3 | async-start | bytes 4456448 | tf_op jit(solution)/shard_map/all_to_all | solution.py:1364
  292.5 2.8 collective-permute-start.17
  299.8 54.3 %all-to-all-done.3.got = bf16[16,272,256]{2,1,0:T(8,128)(2,1)} async-done(((bf16[16,272,256]{2,1,0:T(8,128)(2,1)}), bf16[16,272,256]{2,1,0:T(8,128)(2,1)}, u32[]{:S(2)}, u32[]{:S(2)}) %all-to-all-start.3) | async-done | bytes 2228256 | tf_op jit(solution)/shard_map/all_to_all | solution.py:1364
  355.7 3.2 collective-permute-start.21
  359.4 6.4 %finish.1 = (f32[256,1024]{1,0:T(8,128)}, bf16[256,1024]{1,0:T(8,128)(2,1)}) custom-call(bf16[16,272,256]{2,1,0:T(8,128)(2,1)} %all-to-all-done.3.got, bf16[8,192,1024]{2,1,0:T(8,128)(2,1)} %bitcast.207), custom_call_target="tpu_custom_call" | custom-call | flops 1610612736 | bytes 5242880 | tf_op jit(solution)/shard_map/finish/pallas_call | solution.py:1105
  (255 shorter events, 72.7 us)
Async XLA Ops:
  7.3 167.4 %all-gather.5.cloned.1.call-start = ((), (), s32[]{:S(2)}) async-start(), calls=%async_computation.6 | async-start | bytes 10584064 | tf_op jit(solution)/shard_map/all_gather | solution.py:1302
  11.7 2.4 collective-permute-start.13
  15.4 20.1 %collective-permute-start.2 = (bf16[128,1024]{1,0:T(8,128)(2,1)S(1)}, bf16[128,1024]{1,0:T(8,128)(2,1)S(1)}, u32[]{:S(2)}, u32[]{:S(2)}) collective-permute-start(bf16[128,1024]{1,0:T(8,128)(2,1)S(1)} %get-tuple-element.108), channel_id=1, source_target_pairs={{0,8},{8,0},{4,12},{12,4},{1,9},{9,1},{5,13},{13,5},{2,10},{10,2},... | collective-permute-start | bytes 786440 | tf_op jit(solution)/shard_map/ppermute | solution.py:1137
  17.8 17.7 %collective-permute-start.3 = (bf16[128,1024]{1,0:T(8,128)(2,1)S(1)}, bf16[128,1024]{1,0:T(8,128)(2,1)S(1)}, u32[]{:S(2)}, u32[]{:S(2)}) collective-permute-start(bf16[128,1024]{1,0:T(8,128)(2,1)S(1)} %bitcast.191), channel_id=1, source_target_pairs={{0,2},{2,0},{1,3},{3,1},{4,6},{6,4},{5,7},{7,5},{8,10},{10,8},{9,1... | collective-permute-start | bytes 786440 | tf_op jit(solution)/shard_map/ppermute | solution.py:1137
  21.3 61.7 %all-to-all-start = ((bf16[32,40,192]{2,1,0:T(8,128)(2,1)}), bf16[32,40,192]{2,1,0:T(8,128)(2,1)S(1)}, u32[]{:S(2)}, u32[]{:S(2)}) async-start(bf16[32,40,192]{2,1,0:T(8,128)(2,1)} %bitcast.6), calls=%async_computation | async-start | bytes 1310720 | tf_op jit(solution)/shard_map/all_to_all | solution.py:1236
  25.9 333.4 %all-gather.7.cloned.1.call-start = ((), (), s32[]{:S(2)}) async-start(), calls=%async_computation.7 | async-start | bytes 3538944 | tf_op jit(solution)/shard_map/all_gather | solution.py:1317
  38.0 20.0 %collective-permute-start.4 = (bf16[2,128,1024]{2,1,0:T(8,128)(2,1)S(1)}, bf16[2,128,1024]{2,1,0:T(8,128)(2,1)S(1)}, u32[]{:S(2)}, u32[]{:S(2)}) collective-permute-start(bf16[2,128,1024]{2,1,0:T(8,128)(2,1)S(1)} %get-tuple-element.106), channel_id=1, source_target_pairs={{0,4},{4,0},{8,12},{12,8},{1,5},{5,1},{9,13},{13,9},{2,6},{6,2},{1... | collective-permute-start | bytes 1572872 | tf_op jit(solution)/shard_map/ppermute | solution.py:1137
  38.0 16.0 %collective-permute-start.5 = (bf16[128,1024]{1,0:T(8,128)(2,1)}, bf16[128,1024]{1,0:T(8,128)(2,1)S(1)}, u32[]{:S(2)}, u32[]{:S(2)}) collective-permute-start(bf16[128,1024]{1,0:T(8,128)(2,1)} %copy-done.29), channel_id=1, source_target_pairs={{0,16},{16,0},{1,17},{17,1},{2,18},{18,2},{3,19},{19,3},{4,20},{20... | collective-permute-start | bytes 786440 | tf_op jit(solution)/shard_map/ppermute | solution.py:1137
  59.1 19.1 %collective-permute-start.7 = (bf16[2,128,1024]{2,1,0:T(8,128)(2,1)S(1)}, bf16[2,128,1024]{2,1,0:T(8,128)(2,1)S(1)}, u32[]{:S(2)}, u32[]{:S(2)}) collective-permute-start(bf16[2,128,1024]{2,1,0:T(8,128)(2,1)S(1)} %get-tuple-element.104), channel_id=1, source_target_pairs={{0,4},{4,0},{8,12},{12,8},{1,5},{5,1},{9,13},{13,9},{2,6},{6,2},{1... | collective-permute-start | bytes 1572872 | tf_op jit(solution)/shard_map/ppermute | solution.py:1137
  62.8 48.8 %collective-permute-start.6 = (bf16[2,2,128,1024]{3,2,1,0:T(8,128)(2,1)S(1)}, bf16[2,2,128,1024]{3,2,1,0:T(8,128)(2,1)}, u32[]{:S(2)}, u32[]{:S(2)}) collective-permute-start(bf16[2,2,128,1024]{3,2,1,0:T(8,128)(2,1)S(1)} %pad_maximum_fusion), channel_id=1, source_target_pairs={{0,16},{16,0},{1,17},{17,1},{2,18},{18,2},{3,19},{19,3},{4,20},{20... | collective-permute-start | bytes 3145736 | tf_op jit(solution)/shard_map/ppermute | solution.py:1137
  79.3 37.4 %collective-permute-start.8 = (bf16[2,2,128,1024]{3,2,1,0:T(8,128)(2,1)}, bf16[2,2,128,1024]{3,2,1,0:T(8,128)(2,1)}, u32[]{:S(2)}, u32[]{:S(2)}) collective-permute-start(bf16[2,2,128,1024]{3,2,1,0:T(8,128)(2,1)} %pad_maximum_fusion.1), channel_id=1, source_target_pairs={{0,2},{2,0},{1,3},{3,1},{4,6},{6,4},{5,7},{7,5},{8,10},{10,8},{9,1... | collective-permute-start | bytes 3145736 | tf_op jit(solution)/shard_map/ppermute | solution.py:1137
  81.5 37.0 %collective-permute-start.9 = (bf16[2,2,128,1024]{3,2,1,0:T(8,128)(2,1)S(1)}, bf16[2,2,128,1024]{3,2,1,0:T(8,128)(2,1)}, u32[]{:S(2)}, u32[]{:S(2)}) collective-permute-start(bf16[2,2,128,1024]{3,2,1,0:T(8,128)(2,1)S(1)} %pad_maximum_fusion), channel_id=1, source_target_pairs={{0,1},{1,0},{2,3},{3,2},{4,5},{5,4},{6,7},{7,6},{8,9},{9,8},{10,11... | collective-permute-start | bytes 3145736 | tf_op jit(solution)/shard_map/ppermute | solution.py:1137
  83.7 37.0 %collective-permute-start.11 = (bf16[2,2,128,1024]{3,2,1,0:T(8,128)(2,1)}, bf16[2,2,128,1024]{3,2,1,0:T(8,128)(2,1)S(1)}, u32[]{:S(2)}, u32[]{:S(2)}) collective-permute-start(bf16[2,2,128,1024]{3,2,1,0:T(8,128)(2,1)} %pad_maximum_fusion.1), channel_id=1, source_target_pairs={{0,1},{1,0},{2,3},{3,2},{4,5},{5,4},{6,7},{7,6},{8,9},{9,8},{10,11... | collective-permute-start | bytes 3145736 | tf_op jit(solution)/shard_map/ppermute | solution.py:1137
  111.6 8.6 %collective-permute-start.10 = (bf16[2,2,128,1024]{3,2,1,0:T(8,128)(2,1)}, bf16[2,2,128,1024]{3,2,1,0:T(8,128)(2,1)S(1)}, u32[]{:S(2)}, u32[]{:S(2)}) collective-permute-start(bf16[2,2,128,1024]{3,2,1,0:T(8,128)(2,1)} %collective-permute-done.6), channel_id=1, source_target_pairs={{0,1},{1,0},{2,3},{3,2},{4,5},{5,4},{6,7},{7,6},{8,9},{9,8},{10,11... | collective-permute-start | bytes 3145736 | tf_op jit(solution)/shard_map/ppermute | solution.py:1137
  116.7 4.5 %collective-permute-start.12 = (bf16[2,2,128,1024]{3,2,1,0:T(8,128)(2,1)}, bf16[2,2,128,1024]{3,2,1,0:T(8,128)(2,1)S(1)}, u32[]{:S(2)}, u32[]{:S(2)}) collective-permute-start(bf16[2,2,128,1024]{3,2,1,0:T(8,128)(2,1)} %collective-permute-done.8), channel_id=1, source_target_pairs={{0,1},{1,0},{2,3},{3,2},{4,5},{5,4},{6,7},{7,6},{8,9},{9,8},{10,11... | collective-permute-start | bytes 3145736 | tf_op jit(solution)/shard_map/ppermute | solution.py:1137
  171.6 202.2 %reduce-scatter.2.cloned.1.call-start = ((), (), s32[]{:S(2)}) async-start(), calls=%async_computation.5 | async-start | bytes 10027008 | tf_op jit(solution)/shard_map/reduce_scatter | solution.py:1347
  171.8 9.6 %collective-permute-start = (bf16[2,128,1024]{2,1,0:T(8,128)(2,1)S(1)}, bf16[2,128,1024]{2,1,0:T(8,128)(2,1)}, u32[]{:S(2)}, u32[]{:S(2)}) collective-permute-start(bf16[2,128,1024]{2,1,0:T(8,128)(2,1)S(1)} %copy-done.22), channel_id=1, source_target_pairs={{0,1},{1,0},{2,3},{3,2},{4,5},{5,4},{6,7},{7,6},{8,9},{9,8},{10,11... | collective-permute-start | bytes 1572872 | tf_op jit(solution)/shard_map/ppermute | solution.py:1137
  174.0 7.4 %collective-permute-start.1 = (bf16[2,128,1024]{2,1,0:T(8,128)(2,1)S(1)}, bf16[2,128,1024]{2,1,0:T(8,128)(2,1)S(1)}, u32[]{:S(2)}, u32[]{:S(2)}) collective-permute-start(bf16[2,128,1024]{2,1,0:T(8,128)(2,1)S(1)} %copy-done.5), channel_id=1, source_target_pairs={{0,1},{1,0},{2,3},{3,2},{4,5},{5,4},{6,7},{7,6},{8,9},{9,8},{10,11... | collective-permute-start | bytes 1572872 | tf_op jit(solution)/shard_map/ppermute | solution.py:1137
  181.3 2.3 collective-permute-start.16
  213.1 2.3 collective-permute-start.19
  287.1 67.0 %all-to-all-start.3 = ((bf16[16,272,256]{2,1,0:T(8,128)(2,1)}), bf16[16,272,256]{2,1,0:T(8,128)(2,1)}, u32[]{:S(2)}, u32[]{:S(2)}) async-start(bf16[16,272,256]{2,1,0:T(8,128)(2,1)} %attend_backward.1), calls=%async_computation.3 | async-start | bytes 4456448 | tf_op jit(solution)/shard_map/all_to_all | solution.py:1364
  292.5 4.7 %collective-permute-start.17 = (bf16[256,1024]{1,0:T(8,128)(2,1)}, bf16[256,1024]{1,0:T(8,128)(2,1)}, u32[]{:S(2)}, u32[]{:S(2)}) collective-permute-start(bf16[256,1024]{1,0:T(8,128)(2,1)} %get-tuple-element.63), channel_id=1, source_target_pairs={{0,1},{1,0},{2,3},{3,2},{4,5},{5,4},{6,7},{7,6},{8,9},{9,8},{10,11... | collective-permute-start | bytes 1572872 | tf_op jit(solution)/shard_map/ppermute | solution.py:1137
  355.7 10.4 %collective-permute-start.21 = (f32[8,33,192]{2,0,1:T(8,128)S(1)}, f32[8,33,192]{2,0,1:T(8,128)S(1)}, u32[]{:S(2)}, u32[]{:S(2)}) collective-permute-start(f32[8,33,192]{2,0,1:T(8,128)S(1)} %pad_maximum_fusion.6), channel_id=1, source_target_pairs={{0,1},{1,0},{2,3},{3,2},{4,5},{5,4},{6,7},{7,6},{8,9},{9,8},{10,11... | collective-permute-start | bytes 608264 | tf_op jit(solution)/shard_map/ppermute | solution.py:1137
  365.8 4.9 %collective-permute-start.20 = (bf16[256,1024]{1,0:T(8,128)(2,1)}, bf16[256,1024]{1,0:T(8,128)(2,1)}, u32[]{:S(2)}, u32[]{:S(2)}) collective-permute-start(bf16[256,1024]{1,0:T(8,128)(2,1)} %get-tuple-element.81), channel_id=1, source_target_pairs={{0,1},{1,0},{2,3},{3,2},{4,5},{5,4},{6,7},{7,6},{8,9},{9,8},{10,11... | collective-permute-start | bytes 1572872 | tf_op jit(solution)/shard_map/ppermute | solution.py:1137
  (52 other events, 403.9 us)
Sparse Core Ops, SparseCore 0:
  15.5 144.8 all-gather.4
  171.7 38.1 all-gather.6
  224.7 138.5 reduce-scatter.1
where the time goes:
time: 388 us; the launch traced here: 386 us
  waiting for transfers between devices  128 us (33%)
  Pallas kernels  105 us (27%)
  blocking collectives  43.7 us (11%)
  starting transfers between devices  37.4 us (10%)
  local copies, waits for them, and re-layouts  27.4 us (7%)
  other arithmetic  21.2 us (5%)
  between operations  14.9 us (4%)
  matrix products  8.41 us (2%)
    ppermute x23, waiting for transfers between devices, swap(): return lax.ppermute(values, axis, pairs)  73.5 us
    all_to_all x1, waiting for transfers between devices, fast_body(): lax.all_to_all(send_grads, chips, split_axis=0, concat_axis=0, tiled=True)  54.3 us
    pallas_call x1, Pallas kernels, attend_backward(): pl.pallas_call(functools.partial(backward_kernel, head_size, len(pieces),...  34.4 us
    ppermute x23, starting transfers between devices, swap(): return lax.ppermute(values, axis, pairs)  27.1 us
    pallas_call x1, Pallas kernels, middle(): pl.pallas_call(functools.partial(middle_kernel, len(pieces), share), out_...  26.8 us
    pallas_call x1, Pallas kernels, attend_forward(): pl.pallas_call(functools.partial(forward_kernel, head_size), out_shape=(j...  24.4 us
    all_to_all x1, blocking collectives, fast_body(): lax.all_to_all(grad_send, chips, split_axis=0, concat_axis=0, tiled=True)  22.5 us
    all_to_all x1, blocking collectives, fast_body(): lax.all_to_all(attn_send, chips, split_axis=0, concat_axis=0, tiled=True)  21.2 us
  transfers between devices with their start and end apart: 28, of which 12 were waited for; matrix products, arithmetic and copies ran while one was open for 9% of the time, Pallas kernels for 27%

commit v1 on v0

--- a/solution.py
+++ b/solution.py
@@ -476,7 +476,7 @@
     scale = head_size ** (-0.5)
     bound = bound_ref[0]
 
-    @pl.loop(0, runs)
+    @pl.loop(0, runs, unroll=8)
     def _(run):
         rows = qkv[rows_at(inloc[run], RUN), :]
         here = rows_at(run, RUN)
@@ -484,7 +484,7 @@
         ks[here, :] = rows[:, head_size : 2 * head_size]
         vs[here, :] = rows[:, 2 * head_size :]
 
-    @pl.loop(0, tokens // BLOCK)
+    @pl.loop(0, tokens // BLOCK, unroll=4)
     def _(block):
         here = rows_at(block, BLOCK)
         vt[:, here] = vs[here, :].astype(jnp.float32).T.astype(jnp.bfloat16)
@@ -532,7 +532,7 @@
 
     chips, _, span = out.shape
 
-    @pl.loop(0, chips)
+    @pl.loop(0, chips, unroll=8)
     def _(chip):
         out[chip] = mixed[rows_at(chip, span), :].astype(jnp.float32).T.astype(jnp.bfloat16)
 
@@ -577,15 +577,15 @@
     for copy in copies:
         copy.start()
 
-    @pl.loop(0, chips)
+    @pl.loop(0, chips, unroll=8)
     def _(chip):
         mixed[rows_at(chip, span), :] = grad_t[chip, :head_size, :].astype(jnp.float32).T.astype(jnp.bfloat16)
 
-    @pl.loop(0, runs)
+    @pl.loop(0, runs, unroll=8)
     def _(run):
         grads[rows_at(run, RUN), :] = mixed[rows_at(outloc[run], RUN), :]
 
-    @pl.loop(0, tokens // BLOCK)
+    @pl.loop(0, tokens // BLOCK, unroll=4)
     def _(block):
         here = rows_at(block, BLOCK)
         kt[:, here] = ks[here, :].astype(jnp.float32).T.astype(jnp.bfloat16)
@@ -636,15 +636,15 @@
 
     size = 3 * head_size
 
-    @pl.loop(0, runs)
+    @pl.loop(0, runs, unroll=8)
     def _(run):
         moved[rows_at(outloc[run], RUN), :] = wide[rows_at(run, RUN), :]
 
-    @pl.loop(0, chips)
+    @pl.loop(0, chips, unroll=8)
     def _(chip):
         send_out[chip, :size, :] = moved[rows_at(chip, span), :].astype(jnp.float32).T.astype(jnp.bfloat16)
 
-    @pl.loop(0, runs)
+    @pl.loop(0, runs, unroll=8)
     def _(run):
         moved[rows_at(inloc[run], RUN), :] = wide[rows_at(run, RUN), :]
 
@@ -652,7 +652,7 @@
         copy.wait()
     raw[...] = jnp.zeros_like(raw)
 
-    @pl.loop(0, tokens // BLOCK)
+    @pl.loop(0, tokens // BLOCK, unroll=2)
     def _(block):
         here = rows_at(block, BLOCK)
         turned = moved[here, :].astype(jnp.float32).T.astype(jnp.bfloat16)

time: 388 us -> 381 us (0.982)
  Pallas kernels: 105 us -> 96.4 us
    pallas_call x1, Pallas kernels: 24.4 us -> 19.4 us  [attend_forward(): pl.pallas_call(functools.partial(forward_kernel, head_size), out_shape=(j...]
    pallas_call x1, Pallas kernels: 34.4 us -> 30.5 us  [attend_backward(): pl.pallas_call(functools.partial(backward_kernel, head_size, len(pieces),...]
  transfers between devices with their start and end apart: 28 -> 28, of which waited for: 12 -> 12; matrix products, arithmetic and copies ran while one was open for 9% -> 9% of each run, Pallas kernels for 27% -> 25%
where the time goes in v1:
time: 381 us; the launch traced here: 379 us
  waiting for transfers between devices  129 us (34%)
  Pallas kernels  96.4 us (25%)
  blocking collectives  45.9 us (12%)
  starting transfers between devices  36.1 us (9%)
  local copies, waits for them, and re-layouts  27.4 us (7%)
  other arithmetic  21.2 us (6%)
  between operations  14.9 us (4%)
  matrix products  8.41 us (2%)
    ppermute x23, waiting for transfers between devices, swap(): return lax.ppermute(values, axis, pairs)  73.5 us
    all_to_all x1, waiting for transfers between devices, fast_body(): lax.all_to_all(send_grads, chips, split_axis=0, concat_axis=0, tiled=True)  55.1 us
    pallas_call x1, Pallas kernels, attend_backward(): pl.pallas_call(functools.partial(backward_kernel, head_size, len(pieces),...  30.5 us
    pallas_call x1, Pallas kernels, middle(): pl.pallas_call(functools.partial(middle_kernel, len(pieces), share), out_...  26.8 us
    ppermute x23, starting transfers between devices, swap(): return lax.ppermute(values, axis, pairs)  25.8 us
    all_to_all x1, blocking collectives, fast_body(): lax.all_to_all(grad_send, chips, split_axis=0, concat_axis=0, tiled=True)  23.3 us
    all_to_all x1, blocking collectives, fast_body(): lax.all_to_all(attn_send, chips, split_axis=0, concat_axis=0, tiled=True)  22.6 us
    pallas_call x1, Pallas kernels, attend_forward(): pl.pallas_call(functools.partial(forward_kernel, head_size), out_shape=(j...  19.4 us
  transfers between devices with their start and end apart: 28, of which 12 were waited for; matrix products, arithmetic and copies ran while one was open for 9% of the time, Pallas kernels for 25%

profile of v1, /device:TPU:11, one launch (start us, length us, event | category | flops | bytes accessed | tf_op | source)
XLA Modules:
  0.0 379.0 jit_solution(5415855071654897048)
XLA Ops:
  15.4 2.4 collective-permute-start.2
  21.3 4.6 %all-to-all-start = ((bf16[32,40,192]{2,1,0:T(8,128)(2,1)}), bf16[32,40,192]{2,1,0:T(8,128)(2,1)S(1)}, u32[]{:S(2)}, u32[]{:S(2)}) async-start(bf16[32,40,192]{2,1,0:T(8,128)(2,1)} %bitcast.6), calls=%async_computation | async-start | bytes 1310720 | tf_op jit(solution)/shard_map/all_to_all | solution.py:1236
  26.0 9.5 %collective-permute-done.2 = bf16[128,1024]{1,0:T(8,128)(2,1)S(1)} collective-permute-done((bf16[128,1024]{1,0:T(8,128)(2,1)S(1)}, bf16[128,1024]{1,0:T(8,128)(2,1)S(1)}, u32[]{:S(2)}, u32[]{:S(2)}) %collective-permute-start.2) | collective-permute-done | bytes 262176 | tf_op jit(solution)/shard_map/ppermute | solution.py:1137
  38.0 2.6 collective-permute-start.5
  40.9 13.1 %collective-permute-done.5 = bf16[128,1024]{1,0:T(8,128)(2,1)S(1)} collective-permute-done((bf16[128,1024]{1,0:T(8,128)(2,1)}, bf16[128,1024]{1,0:T(8,128)(2,1)S(1)}, u32[]{:S(2)}, u32[]{:S(2)}) %collective-permute-start.5) | collective-permute-done | bytes 262176 | tf_op jit(solution)/shard_map/ppermute | solution.py:1137
  54.0 3.9 %collective-permute-done.4 = bf16[2,128,1024]{2,1,0:T(8,128)(2,1)S(1)} collective-permute-done((bf16[2,128,1024]{2,1,0:T(8,128)(2,1)S(1)}, bf16[2,128,1024]{2,1,0:T(8,128)(2,1)S(1)}, u32[]{:S(2)}, u32[]{:S(2)}) %collective-permute-start.4) | collective-permute-done | bytes 524320 | tf_op jit(solution)/shard_map/ppermute | solution.py:1137
  59.1 2.4 collective-permute-start.7
  62.8 3.0 collective-permute-start.6
  65.8 12.5 %collective-permute-done.7 = bf16[2,128,1024]{2,1,0:T(8,128)(2,1)S(1)} collective-permute-done((bf16[2,128,1024]{2,1,0:T(8,128)(2,1)S(1)}, bf16[2,128,1024]{2,1,0:T(8,128)(2,1)S(1)}, u32[]{:S(2)}, u32[]{:S(2)}) %collective-permute-start.7) | collective-permute-done | bytes 524320 | tf_op jit(solution)/shard_map/ppermute | solution.py:1137
  79.3 2.0 collective-permute-start.8
  83.7 27.8 %collective-permute-done.6 = bf16[2,2,128,1024]{3,2,1,0:T(8,128)(2,1)} collective-permute-done((bf16[2,2,128,1024]{3,2,1,0:T(8,128)(2,1)S(1)}, bf16[2,2,128,1024]{3,2,1,0:T(8,128)(2,1)}, u32[]{:S(2)}, u32[]{:S(2)}) %collective-permute-start.6) | collective-permute-done | bytes 1048608 | tf_op jit(solution)/shard_map/ppermute | solution.py:1137
  122.1 19.4 %attend_forward.1 = (bf16[16,64,256]{2,1,0:T(8,128)(2,1)S(1)}, bf16[4096,64]{1,0:T(8,128)(2,1)S(1)}, bf16[4096,64]{1,0:T(8,128)(2,1)S(1)}, bf16[4096,64]{1,0:T(8...) custom-call(s32[1]{0:T(128)S(1)} %bitcast.168, s32[64]{0:T(128)S(1)} %get-tuple-element.86.inloc, ...), custom_call_target="tpu_custom_call" | custom-call | flops 8589934592 | bytes 8388608 | tf_op jit(solution)/shard_map/attend_forward/pallas_call | solution.py:544
  144.3 22.6 %all_to_all.20.got = bf16[16,64,256]{2,1,0:T(8,128)(2,1)} all-to-all(bf16[16,64,256]{2,1,0:T(8,128)(2,1)S(1)} %get-tuple-element.56), channel_id=1, replica_groups=mesh['head'=2,'z'=4,'x'=2,'core'=2] {'z','x','head'}, dimensions={0} | all-to-all | bytes 1048576 | tf_op jit(solution)/shard_map/all_to_all | solution.py:1314
  170.0 4.9 %project.1 = (f32[512,1024]{1,0:T(8,128)}, bf16[512,1024]{1,0:T(8,128)(2,1)}, bf16[512,512]{1,0:T(8,128)(2,1)}) custom-call(s32[2,16]{1,0:T(2,128)} %fusion.36.table, bf16[16,64,256]{2,1,0:T(8,128)(2,1)} %all_to_all.20.got, bf16[16,304,1024]{2,1,0:T(8,128)(2,1)} %bitcast.170), custom_call_target="tpu_custom_call" | custom-call | flops 536870912 | bytes 4194304 | tf_op jit(solution)/shard_map/project/pallas_call | solution.py:759
  179.8 26.8 %middle.1 = (f32[512,1024]{1,0:T(8,128)}, f32[256,1024]{1,0:T(8,128)}, bf16[256,1024]{1,0:T(8,128)(2,1)}, f32[512,1024]{1,0:T(8,128)}, bf16[512,1024]{1,0:T(8,12...) custom-call(s32[2,16]{1,0:T(2,128)} %fusion.36.table, bf16[256,1024]{1,0:T(8,128)(2,1)} %bitcast.173, ...), custom_call_target="tpu_custom_call" | custom-call | flops 12884901888 | bytes 16777216 | tf_op jit(solution)/shard_map/middle/pallas_call | solution.py:905
  214.2 4.1 %branch_back.1 = (f32[256,1024]{1,0:T(8,128)S(1)}, bf16[512,1024]{1,0:T(8,128)(2,1)S(1)}, bf16[16,8,256]{2,1,0:T(8,128)(2,1)S(1)}, bf16[16,288,1024]{2,1,0:T(8,128)(2,1)}) custom-call(s32[2,16]{1,0:T(2,128)S(1)} %copy-done.12, f32[512,1024]{1,0:T(8,128)S(1)} %copy-done.2, bf16[256,1024]{1,0:T(8,128)(2,1)S(1)} %bitcast.165, ...), custom_call_target="tpu_custom_call", output_to_operand_aliasing={{3}: (10, {})} | custom-call | flops 536870912 | bytes 8388608 | tf_op jit(solution)/shard_map/branch_back/pallas_call | solution.py:1008
  220.0 4.3 %attention_back.1 = bf16[16,72,256]{2,1,0:T(8,128)(2,1)} custom-call(s32[2,16]{1,0:T(2,128)} %fusion.36.table, bf16[512,1024]{1,0:T(8,128)(2,1)} %copy-done.4, bf16[16,8,256]{2,1,0:T(8,128)(2,1)} %copy-done.10, bf16[16,304,1024]{2,1,0:T(8,128)(2,1)} %bitcast.172), custom_call_target="tpu_custom_call" | custom-call | flops 536870912 | bytes 2097152 | tf_op jit(solution)/shard_map/attention_back/pallas_call | solution.py:1057
  224.2 23.3 %all_to_all.21.grad_t = bf16[16,72,256]{2,1,0:T(8,128)(2,1)S(1)} all-to-all(bf16[16,72,256]{2,1,0:T(8,128)(2,1)} %attention_back.1), channel_id=1, replica_groups=mesh['head'=2,'z'=4,'x'=2,'core'=2] {'z','x','head'}, dimensions={0} | all-to-all | bytes 1179648 | tf_op jit(solution)/shard_map/all_to_all | solution.py:1341
  248.7 30.5 %attend_backward.1 = bf16[16,272,256]{2,1,0:T(8,128)(2,1)} custom-call(s32[1]{0:T(128)S(1)} %bitcast.169, s32[64]{0:T(128)S(1)} %get-tuple-element.86.inloc, s32[64]{0:T(128)S(1)} %get-tuple-element.85.outloc, bf16[16,72,256]{2,1,0:T(8,128)(2,1)S(1)} %all_to_all.21.grad_t, bf16[4096,64]{1,0:T(8,128)(2,1)S(1)} %copy-done.15, bf16[4096,64]{1,0:T(8,128)(2,1)S(1)} %copy-done.17, ...), custom_call_target="tpu_custom_call" | custom-call | flops 21474836480 | bytes 16777216 | tf_op jit(solution)/shard_map/attend_backward/pallas_call | solution.py:678
  279.3 5.4 %all-to-all-start.3 = ((bf16[16,272,256]{2,1,0:T(8,128)(2,1)}), bf16[16,272,256]{2,1,0:T(8,128)(2,1)}, u32[]{:S(2)}, u32[]{:S(2)}) async-start(bf16[16,272,256]{2,1,0:T(8,128)(2,1)} %attend_backward.1), calls=%async_computation.3 | async-start | bytes 4456448 | tf_op jit(solution)/shard_map/all_to_all | solution.py:1364
  284.7 2.8 collective-permute-start.17
  292.0 55.1 %all-to-all-done.3.got = bf16[16,272,256]{2,1,0:T(8,128)(2,1)} async-done(((bf16[16,272,256]{2,1,0:T(8,128)(2,1)}), bf16[16,272,256]{2,1,0:T(8,128)(2,1)}, u32[]{:S(2)}, u32[]{:S(2)}) %all-to-all-start.3) | async-done | bytes 2228256 | tf_op jit(solution)/shard_map/all_to_all | solution.py:1364
  348.7 2.8 collective-permute-start.21
  352.0 6.4 %finish.1 = (f32[256,1024]{1,0:T(8,128)}, bf16[256,1024]{1,0:T(8,128)(2,1)}) custom-call(bf16[16,272,256]{2,1,0:T(8,128)(2,1)} %all-to-all-done.3.got, bf16[8,192,1024]{2,1,0:T(8,128)(2,1)} %bitcast.207), custom_call_target="tpu_custom_call" | custom-call | flops 1610612736 | bytes 5242880 | tf_op jit(solution)/shard_map/finish/pallas_call | solution.py:1105
  (255 shorter events, 71.9 us)
Async XLA Ops:
  7.3 162.7 %all-gather.5.cloned.1.call-start = ((), (), s32[]{:S(2)}) async-start(), calls=%async_computation.6 | async-start | bytes 10584064 | tf_op jit(solution)/shard_map/all_gather | solution.py:1302
  11.7 2.4 collective-permute-start.13
  15.4 20.1 %collective-permute-start.2 = (bf16[128,1024]{1,0:T(8,128)(2,1)S(1)}, bf16[128,1024]{1,0:T(8,128)(2,1)S(1)}, u32[]{:S(2)}, u32[]{:S(2)}) collective-permute-start(bf16[128,1024]{1,0:T(8,128)(2,1)S(1)} %get-tuple-element.108), channel_id=1, source_target_pairs={{0,8},{8,0},{4,12},{12,4},{1,9},{9,1},{5,13},{13,5},{2,10},{10,2},... | collective-permute-start | bytes 786440 | tf_op jit(solution)/shard_map/ppermute | solution.py:1137
  17.8 17.7 %collective-permute-start.3 = (bf16[128,1024]{1,0:T(8,128)(2,1)S(1)}, bf16[128,1024]{1,0:T(8,128)(2,1)S(1)}, u32[]{:S(2)}, u32[]{:S(2)}) collective-permute-start(bf16[128,1024]{1,0:T(8,128)(2,1)S(1)} %bitcast.191), channel_id=1, source_target_pairs={{0,2},{2,0},{1,3},{3,1},{4,6},{6,4},{5,7},{7,5},{8,10},{10,8},{9,1... | collective-permute-start | bytes 786440 | tf_op jit(solution)/shard_map/ppermute | solution.py:1137
  21.3 61.7 %all-to-all-start = ((bf16[32,40,192]{2,1,0:T(8,128)(2,1)}), bf16[32,40,192]{2,1,0:T(8,128)(2,1)S(1)}, u32[]{:S(2)}, u32[]{:S(2)}) async-start(bf16[32,40,192]{2,1,0:T(8,128)(2,1)} %bitcast.6), calls=%async_computation | async-start | bytes 1310720 | tf_op jit(solution)/shard_map/all_to_all | solution.py:1236
  25.9 326.1 %all-gather.7.cloned.1.call-start = ((), (), s32[]{:S(2)}) async-start(), calls=%async_computation.7 | async-start | bytes 3538944 | tf_op jit(solution)/shard_map/all_gather | solution.py:1317
  38.0 20.0 %collective-permute-start.4 = (bf16[2,128,1024]{2,1,0:T(8,128)(2,1)S(1)}, bf16[2,128,1024]{2,1,0:T(8,128)(2,1)S(1)}, u32[]{:S(2)}, u32[]{:S(2)}) collective-permute-start(bf16[2,128,1024]{2,1,0:T(8,128)(2,1)S(1)} %get-tuple-element.106), channel_id=1, source_target_pairs={{0,4},{4,0},{8,12},{12,8},{1,5},{5,1},{9,13},{13,9},{2,6},{6,2},{1... | collective-permute-start | bytes 1572872 | tf_op jit(solution)/shard_map/ppermute | solution.py:1137
  38.0 16.0 %collective-permute-start.5 = (bf16[128,1024]{1,0:T(8,128)(2,1)}, bf16[128,1024]{1,0:T(8,128)(2,1)S(1)}, u32[]{:S(2)}, u32[]{:S(2)}) collective-permute-start(bf16[128,1024]{1,0:T(8,128)(2,1)} %copy-done.29), channel_id=1, source_target_pairs={{0,16},{16,0},{1,17},{17,1},{2,18},{18,2},{3,19},{19,3},{4,20},{20... | collective-permute-start | bytes 786440 | tf_op jit(solution)/shard_map/ppermute | solution.py:1137
  59.1 19.1 %collective-permute-start.7 = (bf16[2,128,1024]{2,1,0:T(8,128)(2,1)S(1)}, bf16[2,128,1024]{2,1,0:T(8,128)(2,1)S(1)}, u32[]{:S(2)}, u32[]{:S(2)}) collective-permute-start(bf16[2,128,1024]{2,1,0:T(8,128)(2,1)S(1)} %get-tuple-element.104), channel_id=1, source_target_pairs={{0,4},{4,0},{8,12},{12,8},{1,5},{5,1},{9,13},{13,9},{2,6},{6,2},{1... | collective-permute-start | bytes 1572872 | tf_op jit(solution)/shard_map/ppermute | solution.py:1137
  62.8 48.8 %collective-permute-start.6 = (bf16[2,2,128,1024]{3,2,1,0:T(8,128)(2,1)S(1)}, bf16[2,2,128,1024]{3,2,1,0:T(8,128)(2,1)}, u32[]{:S(2)}, u32[]{:S(2)}) collective-permute-start(bf16[2,2,128,1024]{3,2,1,0:T(8,128)(2,1)S(1)} %pad_maximum_fusion), channel_id=1, source_target_pairs={{0,16},{16,0},{1,17},{17,1},{2,18},{18,2},{3,19},{19,3},{4,20},{20... | collective-permute-start | bytes 3145736 | tf_op jit(solution)/shard_map/ppermute | solution.py:1137
  79.3 37.4 %collective-permute-start.8 = (bf16[2,2,128,1024]{3,2,1,0:T(8,128)(2,1)}, bf16[2,2,128,1024]{3,2,1,0:T(8,128)(2,1)}, u32[]{:S(2)}, u32[]{:S(2)}) collective-permute-start(bf16[2,2,128,1024]{3,2,1,0:T(8,128)(2,1)} %pad_maximum_fusion.1), channel_id=1, source_target_pairs={{0,2},{2,0},{1,3},{3,1},{4,6},{6,4},{5,7},{7,5},{8,10},{10,8},{9,1... | collective-permute-start | bytes 3145736 | tf_op jit(solution)/shard_map/ppermute | solution.py:1137
  81.5 37.0 %collective-permute-start.9 = (bf16[2,2,128,1024]{3,2,1,0:T(8,128)(2,1)S(1)}, bf16[2,2,128,1024]{3,2,1,0:T(8,128)(2,1)}, u32[]{:S(2)}, u32[]{:S(2)}) collective-permute-start(bf16[2,2,128,1024]{3,2,1,0:T(8,128)(2,1)S(1)} %pad_maximum_fusion), channel_id=1, source_target_pairs={{0,1},{1,0},{2,3},{3,2},{4,5},{5,4},{6,7},{7,6},{8,9},{9,8},{10,11... | collective-permute-start | bytes 3145736 | tf_op jit(solution)/shard_map/ppermute | solution.py:1137
  83.7 37.0 %collective-permute-start.11 = (bf16[2,2,128,1024]{3,2,1,0:T(8,128)(2,1)}, bf16[2,2,128,1024]{3,2,1,0:T(8,128)(2,1)S(1)}, u32[]{:S(2)}, u32[]{:S(2)}) collective-permute-start(bf16[2,2,128,1024]{3,2,1,0:T(8,128)(2,1)} %pad_maximum_fusion.1), channel_id=1, source_target_pairs={{0,1},{1,0},{2,3},{3,2},{4,5},{5,4},{6,7},{7,6},{8,9},{9,8},{10,11... | collective-permute-start | bytes 3145736 | tf_op jit(solution)/shard_map/ppermute | solution.py:1137
  111.6 8.6 %collective-permute-start.10 = (bf16[2,2,128,1024]{3,2,1,0:T(8,128)(2,1)}, bf16[2,2,128,1024]{3,2,1,0:T(8,128)(2,1)S(1)}, u32[]{:S(2)}, u32[]{:S(2)}) collective-permute-start(bf16[2,2,128,1024]{3,2,1,0:T(8,128)(2,1)} %collective-permute-done.6), channel_id=1, source_target_pairs={{0,1},{1,0},{2,3},{3,2},{4,5},{5,4},{6,7},{7,6},{8,9},{9,8},{10,11... | collective-permute-start | bytes 3145736 | tf_op jit(solution)/shard_map/ppermute | solution.py:1137
  116.7 4.5 %collective-permute-start.12 = (bf16[2,2,128,1024]{3,2,1,0:T(8,128)(2,1)}, bf16[2,2,128,1024]{3,2,1,0:T(8,128)(2,1)S(1)}, u32[]{:S(2)}, u32[]{:S(2)}) collective-permute-start(bf16[2,2,128,1024]{3,2,1,0:T(8,128)(2,1)} %collective-permute-done.8), channel_id=1, source_target_pairs={{0,1},{1,0},{2,3},{3,2},{4,5},{5,4},{6,7},{7,6},{8,9},{9,8},{10,11... | collective-permute-start | bytes 3145736 | tf_op jit(solution)/shard_map/ppermute | solution.py:1137
  167.9 198.5 %reduce-scatter.2.cloned.1.call-start = ((), (), s32[]{:S(2)}) async-start(), calls=%async_computation.5 | async-start | bytes 10027008 | tf_op jit(solution)/shard_map/reduce_scatter | solution.py:1347
  168.1 8.6 %collective-permute-start = (bf16[2,128,1024]{2,1,0:T(8,128)(2,1)S(1)}, bf16[2,128,1024]{2,1,0:T(8,128)(2,1)}, u32[]{:S(2)}, u32[]{:S(2)}) collective-permute-start(bf16[2,128,1024]{2,1,0:T(8,128)(2,1)S(1)} %copy-done.22), channel_id=1, source_target_pairs={{0,1},{1,0},{2,3},{3,2},{4,5},{5,4},{6,7},{7,6},{8,9},{9,8},{10,11... | collective-permute-start | bytes 1572872 | tf_op jit(solution)/shard_map/ppermute | solution.py:1137
  169.3 7.4 %collective-permute-start.1 = (bf16[2,128,1024]{2,1,0:T(8,128)(2,1)S(1)}, bf16[2,128,1024]{2,1,0:T(8,128)(2,1)S(1)}, u32[]{:S(2)}, u32[]{:S(2)}) collective-permute-start(bf16[2,128,1024]{2,1,0:T(8,128)(2,1)S(1)} %copy-done.5), channel_id=1, source_target_pairs={{0,1},{1,0},{2,3},{3,2},{4,5},{5,4},{6,7},{7,6},{8,9},{9,8},{10,11... | collective-permute-start | bytes 1572872 | tf_op jit(solution)/shard_map/ppermute | solution.py:1137
  176.7 2.3 collective-permute-start.16
  208.5 2.3 collective-permute-start.19
  279.3 67.8 %all-to-all-start.3 = ((bf16[16,272,256]{2,1,0:T(8,128)(2,1)}), bf16[16,272,256]{2,1,0:T(8,128)(2,1)}, u32[]{:S(2)}, u32[]{:S(2)}) async-start(bf16[16,272,256]{2,1,0:T(8,128)(2,1)} %attend_backward.1), calls=%async_computation.3 | async-start | bytes 4456448 | tf_op jit(solution)/shard_map/all_to_all | solution.py:1364
  284.7 4.6 %collective-permute-start.17 = (bf16[256,1024]{1,0:T(8,128)(2,1)}, bf16[256,1024]{1,0:T(8,128)(2,1)}, u32[]{:S(2)}, u32[]{:S(2)}) collective-permute-start(bf16[256,1024]{1,0:T(8,128)(2,1)} %get-tuple-element.63), channel_id=1, source_target_pairs={{0,1},{1,0},{2,3},{3,2},{4,5},{5,4},{6,7},{7,6},{8,9},{9,8},{10,11... | collective-permute-start | bytes 1572872 | tf_op jit(solution)/shard_map/ppermute | solution.py:1137
  348.7 10.0 %collective-permute-start.21 = (f32[8,33,192]{2,0,1:T(8,128)S(1)}, f32[8,33,192]{2,0,1:T(8,128)S(1)}, u32[]{:S(2)}, u32[]{:S(2)}) collective-permute-start(f32[8,33,192]{2,0,1:T(8,128)S(1)} %pad_maximum_fusion.6), channel_id=1, source_target_pairs={{0,1},{1,0},{2,3},{3,2},{4,5},{5,4},{6,7},{7,6},{8,9},{9,8},{10,11... | collective-permute-start | bytes 608264 | tf_op jit(solution)/shard_map/ppermute | solution.py:1137
  358.4 4.9 %collective-permute-start.20 = (bf16[256,1024]{1,0:T(8,128)(2,1)}, bf16[256,1024]{1,0:T(8,128)(2,1)}, u32[]{:S(2)}, u32[]{:S(2)}) collective-permute-start(bf16[256,1024]{1,0:T(8,128)(2,1)} %get-tuple-element.81), channel_id=1, source_target_pairs={{0,1},{1,0},{2,3},{3,2},{4,5},{5,4},{6,7},{7,6},{8,9},{9,8},{10,11... | collective-permute-start | bytes 1572872 | tf_op jit(solution)/shard_map/ppermute | solution.py:1137
  (52 other events, 409.9 us)
Sparse Core Ops, SparseCore 0:
  15.5 148.0 all-gather.4
  168.0 37.9 all-gather.6
  220.0 139.8 reduce-scatter.1

commit v2 on v1

--- a/solution.py
+++ b/solution.py
@@ -716,7 +716,7 @@
     for piece in pieces:
         count = piece.shape[0]
 
-        @pl.loop(0, count)
+        @pl.loop(0, count, unroll=4)
         def _(index, piece=piece, slot=slot):
             chip = table[0, slot + index]
             for rows, target in targets(chip):
@@ -730,7 +730,7 @@
 
 
 def project_kernel(count, table, got, *refs):
-    pieces, (part_out, sent, attn_in, w_out, sem) = refs[:count], refs[count:]
+    pieces, (part_out, sent_a, sent_b, attn_in, w_out, sem) = refs[:count], refs[count:]
     chips, size, span = got.shape
     share = w_out.shape[0] // chips
     rows = span // 2
@@ -748,7 +748,9 @@
     left = attn_in[...].astype(jnp.float32).T.astype(jnp.bfloat16)
     part = dot_nn(left, w_out[...])
     part_out[...] = part
-    sent[...] = part.astype(jnp.bfloat16)
+    own = sent_a.shape[0]
+    sent_a[...] = part[:own].astype(jnp.bfloat16)
+    sent_b[...] = part[own:].astype(jnp.bfloat16)
 
 
 def project(table, got, pieces, share):
@@ -760,12 +762,13 @@
         functools.partial(project_kernel, len(pieces)),
         out_shape=(
             jax.ShapeDtypeStruct((tokens, width), jnp.float32),
-            jax.ShapeDtypeStruct((tokens, width), bf16),
+            jax.ShapeDtypeStruct((tokens // 2, width), bf16),
+            jax.ShapeDtypeStruct((tokens // 2, width), bf16),
             jax.ShapeDtypeStruct((chips // 2 * size, tokens), bf16),
         ),
         in_specs=[pl.BlockSpec(memory_space=SM), pl.BlockSpec(memory_space=VM)]
         + [pl.BlockSpec(memory_space=pltpu.HBM)] * len(pieces),
-        out_specs=[pl.BlockSpec(memory_space=VM)] * 3,
+        out_specs=[pl.BlockSpec(memory_space=VM)] * 4,
         scratch_shapes=[VM((chips * share, width), bf16), pltpu.SemaphoreType.DMA],
         compiler_params=pltpu.CompilerParams(vmem_limit_bytes=58 * 1024 * 1024),
         cost_estimate=pl.CostEstimate(
@@ -777,8 +780,8 @@
 
 def middle_kernel(count, share, table, x_a, x_b, g_a, g_b, part, got_a, got_b, *refs):
     pieces = refs[:count]
-    (resid, base, other, grad_act, grad_sent, fc_sums, vectors, terms) = refs[count : count + 8]
-    (smalls, fc_bias, w_fc, w_proj, g_all, act, act_t, rest, proj_buf, fc_buf, small_sem, load_sem, proj_sem, fc_sem) = refs[count + 8 :]
+    (resid, base, other, grad_act, sent_a, sent_b, fc_sums, vectors, terms) = refs[count : count + 9]
+    (smalls, fc_bias, w_fc, w_proj, g_all, act, act_t, rest, proj_buf, fc_buf, small_sem, load_sem, proj_sem, fc_sem) = refs[count + 9 :]
     f32, bf16 = jnp.float32, jnp.bfloat16
     tokens, width = part.shape
     own = tokens // 2
@@ -889,7 +892,8 @@
             rest[...] += projected[own:]
 
     other[...] = rest[...].astype(bf16)
-    grad_sent[...] = grad_act[...].astype(bf16)
+    sent_a[...] = grad_act[:own, :].astype(bf16)
+    sent_b[...] = grad_act[own:, :].astype(bf16)
     for step in range(steps - 2, steps):
         for copy in copies(step, step % 2):
             copy.wait()
@@ -909,7 +913,8 @@
             shape((tokens // 2, width), f32),
             shape((tokens // 2, width), bf16),
             shape((tokens, width), f32),
-            shape((tokens, width), bf16),
+            shape((tokens // 2, width), bf16),
+            shape((tokens // 2, width), bf16),
             shape((1, hidden), f32),
             shape((8, width), f32),
             shape((chips, rows, width), bf16),
@@ -917,7 +922,7 @@
         in_specs=[pl.BlockSpec(memory_space=SM)]
         + [pl.BlockSpec(memory_space=VM)] * 7
         + [pl.BlockSpec(memory_space=pltpu.HBM)] * len(pieces),
-        out_specs=[pl.BlockSpec(memory_space=VM)] * 7 + [pl.BlockSpec(memory_space=pltpu.HBM)],
+        out_specs=[pl.BlockSpec(memory_space=VM)] * 8 + [pl.BlockSpec(memory_space=pltpu.HBM)],
         scratch_shapes=[
             VM((chips, 16, width), bf16),
             VM((1, hidden), f32),
@@ -1125,6 +1130,41 @@
     )(got, weights)
 
 
+def unpack_kernel(share, core_ref, summed, given, proj, out, merged):
+    f32 = jnp.float32
+    core = core_ref[0]
+    folds, _, width = given.shape
+    each = proj.shape[0]
+    proj[...] = summed[:each, :].astype(f32)
+    out[...] = summed[each : each + share, :].astype(f32)
+    group = each
+    for fold in range(folds):
+        first = pl.multiple_of(each + share + (fold * 2 + core) * share, share)
+        for owner, rows in ((core, summed[pl.ds(first, share), :]), (1 - core, given[fold])):
+            rows = rows.astype(f32)
+            for index in range(width // group):
+                number = fold * (width // group) + index
+                place = ((number // 2 * 2 + owner) * 2 + number % 2) * group
+                merged[:, pl.ds(pl.multiple_of(place, group), group)] = rows[:, index * group : (index + 1) * group]
+
+
+def unpack(core, summed, given, share, each):
+    folds, _, width = given.shape
+    f32 = jnp.float32
+    return pl.pallas_call(
+        functools.partial(unpack_kernel, share),
+        out_shape=(
+            jax.ShapeDtypeStruct((each, width), f32),
+            jax.ShapeDtypeStruct((share, width), f32),
+            jax.ShapeDtypeStruct((share, 2 * folds * width), f32),
+        ),
+        in_specs=[pl.BlockSpec(memory_space=SM)] + [pl.BlockSpec(memory_space=VM)] * 2,
+        out_specs=[pl.BlockSpec(memory_space=VM)] * 3,
+        cost_estimate=pl.CostEstimate(flops=0, bytes_accessed=6 * summed.size, transcendentals=0),
+        name="unpack",
+    )(core, summed, given)
+
+
 PATHS = (("x", "z", "head"), ("head", "z", "x"))
 
 
@@ -1310,14 +1350,13 @@
 
     x_a, x_b = block_input.reshape(-1, width), swap(block_input, "core").reshape(-1, width)
     g_a, g_b = out_grad.reshape(-1, width), swap(out_grad, "core").reshape(-1, width)
-    own = micro * rows
     attn_got = lax.all_to_all(attn_send, chips, split_axis=0, concat_axis=0, tiled=True)
     weight_turned, attn_got = lax.optimization_barrier((head_weight.T, attn_got))
     cubes = cube_orders(nz // 2)
     w_qkv = lax.all_gather(weight_turned, chips, axis=0, axis_index_groups=cubes)
-    part, sent, attn_in = project(table, attn_got, [gathered], share)
-    resid, base, project_other, grad_part, sent_back, fc_sums, vectors, terms = middle(
-        table, x_a, x_b, g_a, g_b, part, swap(sent[own:], "core"), swap(sent[:own], "core"), [gathered], share, hidden_half
+    part, sent_a, sent_b, attn_in = project(table, attn_got, [gathered], share)
+    resid, base, project_other, grad_part, back_a, back_b, fc_sums, vectors, terms = middle(
+        table, x_a, x_b, g_a, g_b, part, swap(sent_b, "core"), swap(sent_a, "core"), [gathered], share, hidden_half
     )
     grad_resid, branch, tails, terms = branch_back(
         table,
@@ -1325,8 +1364,8 @@
         g_a,
         g_b,
         grad_part,
-        swap(sent_back[own:], "core"),
-        swap(sent_back[:own], "core"),
+        swap(back_b, "core"),
+        swap(back_a, "core"),
         vectors,
         fc_sums,
         attn_in,
@@ -1347,16 +1386,11 @@
     summed = lax.psum_scatter(
         terms, every, scatter_dimension=0, tiled=True, axis_index_groups=core_groups(rings)
     )[0]
-    final_proj_w = summed[:proj_rows].astype(f32)
-    final_out_w = summed[proj_rows : proj_rows + out_rows].astype(f32)
     fc_sum = summed[proj_rows + out_rows :].reshape(folds, 2, share, width)
-    fc_keep = lax.dynamic_index_in_dim(fc_sum, ic, 1, keepdims=False)
     fc_give = swap(lax.dynamic_index_in_dim(fc_sum, 1 - ic, 1, keepdims=False), "core")
-
-    def by_owner(values):
-        return values.transpose(1, 0, 2).reshape(share, zx, 2, hidden_share)
-
-    final_fc_w = in_order(by_owner(fc_keep), by_owner(fc_give), ic, 2).reshape(share, 2 * hidden_half).astype(f32)
+    final_proj_w, final_out_w, final_fc_w = unpack(
+        ic.astype(jnp.int32).reshape(1), summed, fc_give, share, hidden_share
+    )
 
     send_grads = attend_backward(
         bound, inloc, outloc, grad_got, queries, keys, values, attn_t, lse, pieces, share

time: 381 us -> 378 us (level)
    unnamed x96 -> x100, local copies, waits for them, and re-layouts: 11.9 us -> 14.9 us
  transfers between devices with their start and end apart: 28 -> 28, of which waited for: 12 -> 12; matrix products, arithmetic and copies ran while one was open for 9% -> 8% of each run, Pallas kernels for 25% -> 26%
where the time goes in v2:
time: 378 us; the launch traced here: 377 us
  waiting for transfers between devices  129 us (34%)
  Pallas kernels  98.4 us (26%)
  blocking collectives  45.8 us (12%)
  starting transfers between devices  36.1 us (10%)
  local copies, waits for them, and re-layouts  26.7 us (7%)
  other arithmetic  17.7 us (5%)
  between operations  14.8 us (4%)
  matrix products  8.41 us (2%)
    ppermute x23, waiting for transfers between devices, swap(): return lax.ppermute(values, axis, pairs)  73.9 us
    all_to_all x1, waiting for transfers between devices, fast_body(): lax.all_to_all(send_grads, chips, split_axis=0, concat_axis=0, tiled=True)  55.1 us
    pallas_call x1, Pallas kernels, attend_backward(): pl.pallas_call(functools.partial(backward_kernel, head_size, len(pieces),...  30.6 us
    pallas_call x1, Pallas kernels, middle(): pl.pallas_call(functools.partial(middle_kernel, len(pieces), share), out_...  26.8 us
    ppermute x23, starting transfers between devices, swap(): return lax.ppermute(values, axis, pairs)  25.8 us
    all_to_all x1, blocking collectives, fast_body(): lax.all_to_all(grad_send, chips, split_axis=0, concat_axis=0, tiled=True)  23.2 us
    all_to_all x1, blocking collectives, fast_body(): lax.all_to_all(attn_send, chips, split_axis=0, concat_axis=0, tiled=True)  22.6 us
    pallas_call x1, Pallas kernels, attend_forward(): pl.pallas_call(functools.partial(forward_kernel, head_size), out_shape=(j...  19.4 us
  transfers between devices with their start and end apart: 28, of which 12 were waited for; matrix products, arithmetic and copies ran while one was open for 8% of the time, Pallas kernels for 26%

profile of v2, /device:TPU:11, one launch (start us, length us, event | category | flops | bytes accessed | tf_op | source)
XLA Modules:
  0.0 377.1 jit_solution(1995028761089911569)
XLA Ops:
  15.4 2.4 collective-permute-start.2
  21.3 4.6 %all-to-all-start = ((bf16[32,40,192]{2,1,0:T(8,128)(2,1)}), bf16[32,40,192]{2,1,0:T(8,128)(2,1)S(1)}, u32[]{:S(2)}, u32[]{:S(2)}) async-start(bf16[32,40,192]{2,1,0:T(8,128)(2,1)} %bitcast.6), calls=%async_computation | async-start | bytes 1310720 | tf_op jit(solution)/shard_map/all_to_all | solution.py:1276
  26.0 9.5 %collective-permute-done.2 = bf16[128,1024]{1,0:T(8,128)(2,1)S(1)} collective-permute-done((bf16[128,1024]{1,0:T(8,128)(2,1)S(1)}, bf16[128,1024]{1,0:T(8,128)(2,1)S(1)}, u32[]{:S(2)}, u32[]{:S(2)}) %collective-permute-start.2) | collective-permute-done | bytes 262176 | tf_op jit(solution)/shard_map/ppermute | solution.py:1177
  38.0 2.6 collective-permute-start.5
  40.9 13.1 %collective-permute-done.5 = bf16[128,1024]{1,0:T(8,128)(2,1)S(1)} collective-permute-done((bf16[128,1024]{1,0:T(8,128)(2,1)}, bf16[128,1024]{1,0:T(8,128)(2,1)S(1)}, u32[]{:S(2)}, u32[]{:S(2)}) %collective-permute-start.5) | collective-permute-done | bytes 262176 | tf_op jit(solution)/shard_map/ppermute | solution.py:1177
  54.0 3.9 %collective-permute-done.4 = bf16[2,128,1024]{2,1,0:T(8,128)(2,1)S(1)} collective-permute-done((bf16[2,128,1024]{2,1,0:T(8,128)(2,1)S(1)}, bf16[2,128,1024]{2,1,0:T(8,128)(2,1)S(1)}, u32[]{:S(2)}, u32[]{:S(2)}) %collective-permute-start.4) | collective-permute-done | bytes 524320 | tf_op jit(solution)/shard_map/ppermute | solution.py:1177
  59.1 2.4 collective-permute-start.7
  62.8 3.0 collective-permute-start.6
  65.8 12.4 %collective-permute-done.7 = bf16[2,128,1024]{2,1,0:T(8,128)(2,1)S(1)} collective-permute-done((bf16[2,128,1024]{2,1,0:T(8,128)(2,1)S(1)}, bf16[2,128,1024]{2,1,0:T(8,128)(2,1)S(1)}, u32[]{:S(2)}, u32[]{:S(2)}) %collective-permute-start.7) | collective-permute-done | bytes 524320 | tf_op jit(solution)/shard_map/ppermute | solution.py:1177
  83.7 27.8 %collective-permute-done.6 = bf16[2,2,128,1024]{3,2,1,0:T(8,128)(2,1)} collective-permute-done((bf16[2,2,128,1024]{3,2,1,0:T(8,128)(2,1)S(1)}, bf16[2,2,128,1024]{3,2,1,0:T(8,128)(2,1)}, u32[]{:S(2)}, u32[]{:S(2)}) %collective-permute-start.6) | collective-permute-done | bytes 1048608 | tf_op jit(solution)/shard_map/ppermute | solution.py:1177
  122.2 19.4 %attend_forward.1 = (bf16[16,64,256]{2,1,0:T(8,128)(2,1)S(1)}, bf16[4096,64]{1,0:T(8,128)(2,1)S(1)}, bf16[4096,64]{1,0:T(8,128)(2,1)S(1)}, bf16[4096,64]{1,0:T(8...) custom-call(s32[1]{0:T(128)S(1)} %bitcast.147, s32[64]{0:T(128)S(1)} %get-tuple-element.96.inloc, ...), custom_call_target="tpu_custom_call" | custom-call | flops 8589934592 | bytes 8388608 | tf_op jit(solution)/shard_map/attend_forward/pallas_call | solution.py:544
  144.3 22.6 %all_to_all.20.got = bf16[16,64,256]{2,1,0:T(8,128)(2,1)} all-to-all(bf16[16,64,256]{2,1,0:T(8,128)(2,1)S(1)} %get-tuple-element.61), channel_id=1, replica_groups=mesh['head'=2,'z'=4,'x'=2,'core'=2] {'z','x','head'}, dimensions={0} | all-to-all | bytes 1048576 | tf_op jit(solution)/shard_map/all_to_all | solution.py:1353
  170.0 4.8 %project.1 = (f32[512,1024]{1,0:T(8,128)}, bf16[256,1024]{1,0:T(8,128)(2,1)}, bf16[256,1024]{1,0:T(8,128)(2,1)}, bf16[512,512]{1,0:T(8,128)(2,1)}) custom-call(s32[2,16]{1,0:T(2,128)} %fusion.32.table, bf16[16,64,256]{2,1,0:T(8,128)(2,1)} %all_to_all.20.got, bf16[16,304,1024]{2,1,0:T(8,128)(2,1)} %bitcast.149), custom_call_target="tpu_custom_call" | custom-call | flops 536870912 | bytes 4194304 | tf_op jit(solution)/shard_map/project/pallas_call | solution.py:761
  178.6 26.8 %middle.1 = (f32[512,1024]{1,0:T(8,128)}, f32[256,1024]{1,0:T(8,128)}, bf16[256,1024]{1,0:T(8,128)(2,1)}, f32[512,1024]{1,0:T(8,128)}, bf16[256,1024]{1,0:T(8,12...) custom-call(s32[2,16]{1,0:T(2,128)} %fusion.32.table, ...), custom_call_target="tpu_custom_call" | custom-call | flops 12884901888 | bytes 16777216 | tf_op jit(solution)/shard_map/middle/pallas_call | solution.py:909
  214.1 4.1 %branch_back.1 = (f32[256,1024]{1,0:T(8,128)S(1)}, bf16[512,1024]{1,0:T(8,128)(2,1)S(1)}, bf16[16,8,256]{2,1,0:T(8,128)(2,1)S(1)}, bf16[16,288,1024]{2,1,0:T(8,128)(2,1)}) custom-call(s32[2,16]{1,0:T(2,128)S(1)} %copy-done.12, f32[512,1024]{1,0:T(8,128)S(1)} %copy-done.2, bf16[256,1024]{1,0:T(8,128)(2,1)S(1)} %bitcast.144, ...), custom_call_target="tpu_custom_call", output_to_operand_aliasing={{3}: (10, {})} | custom-call | flops 536870912 | bytes 8388608 | tf_op jit(solution)/shard_map/branch_back/pallas_call | solution.py:1013
  219.8 4.3 %attention_back.1 = bf16[16,72,256]{2,1,0:T(8,128)(2,1)} custom-call(s32[2,16]{1,0:T(2,128)} %fusion.32.table, bf16[512,1024]{1,0:T(8,128)(2,1)} %copy-done.4, bf16[16,8,256]{2,1,0:T(8,128)(2,1)} %copy-done.10, bf16[16,304,1024]{2,1,0:T(8,128)(2,1)} %bitcast.151), custom_call_target="tpu_custom_call" | custom-call | flops 536870912 | bytes 2097152 | tf_op jit(solution)/shard_map/attention_back/pallas_call | solution.py:1062
  224.1 23.2 %all_to_all.21.grad_t = bf16[16,72,256]{2,1,0:T(8,128)(2,1)S(1)} all-to-all(bf16[16,72,256]{2,1,0:T(8,128)(2,1)} %attention_back.1), channel_id=1, replica_groups=mesh['head'=2,'z'=4,'x'=2,'core'=2] {'z','x','head'}, dimensions={0} | all-to-all | bytes 1179648 | tf_op jit(solution)/shard_map/all_to_all | solution.py:1380
  248.6 30.6 %attend_backward.1 = bf16[16,272,256]{2,1,0:T(8,128)(2,1)} custom-call(s32[1]{0:T(128)S(1)} %bitcast.148, s32[64]{0:T(128)S(1)} %get-tuple-element.96.inloc, s32[64]{0:T(128)S(1)} %get-tuple-element.95.outloc, bf16[16,72,256]{2,1,0:T(8,128)(2,1)S(1)} %all_to_all.21.grad_t, bf16[4096,64]{1,0:T(8,128)(2,1)S(1)} %copy-done.15, bf16[4096,64]{1,0:T(8,128)(2,1)S(1)} %copy-done.17, ...), custom_call_target="tpu_custom_call" | custom-call | flops 21474836480 | bytes 16777216 | tf_op jit(solution)/shard_map/attend_backward/pallas_call | solution.py:678
  279.1 5.4 %all-to-all-start.3 = ((bf16[16,272,256]{2,1,0:T(8,128)(2,1)}), bf16[16,272,256]{2,1,0:T(8,128)(2,1)}, u32[]{:S(2)}, u32[]{:S(2)}) async-start(bf16[16,272,256]{2,1,0:T(8,128)(2,1)} %attend_backward.1), calls=%async_computation.3 | async-start | bytes 4456448 | tf_op jit(solution)/shard_map/all_to_all | solution.py:1398
  284.6 2.8 collective-permute-start.17
  291.8 55.1 %all-to-all-done.3.got = bf16[16,272,256]{2,1,0:T(8,128)(2,1)} async-done(((bf16[16,272,256]{2,1,0:T(8,128)(2,1)}), bf16[16,272,256]{2,1,0:T(8,128)(2,1)}, u32[]{:S(2)}, u32[]{:S(2)}) %all-to-all-start.3) | async-done | bytes 2228256 | tf_op jit(solution)/shard_map/all_to_all | solution.py:1398
  348.5 2.8 collective-permute-start.21
  351.8 6.4 %finish.1 = (f32[256,1024]{1,0:T(8,128)}, bf16[256,1024]{1,0:T(8,128)(2,1)}) custom-call(bf16[16,272,256]{2,1,0:T(8,128)(2,1)} %all-to-all-done.3.got, bf16[8,192,1024]{2,1,0:T(8,128)(2,1)} %bitcast.186), custom_call_target="tpu_custom_call" | custom-call | flops 1610612736 | bytes 5242880 | tf_op jit(solution)/shard_map/finish/pallas_call | solution.py:1110
  368.4 2.2 unpack.1
  (247 shorter events, 70.2 us)
Async XLA Ops:
  7.3 162.7 %all-gather.5.cloned.1.call-start = ((), (), s32[]{:S(2)}) async-start(), calls=%async_computation.6 | async-start | bytes 10584064 | tf_op jit(solution)/shard_map/all_gather | solution.py:1342
  11.7 2.4 collective-permute-start.13
  15.4 20.1 %collective-permute-start.2 = (bf16[128,1024]{1,0:T(8,128)(2,1)S(1)}, bf16[128,1024]{1,0:T(8,128)(2,1)S(1)}, u32[]{:S(2)}, u32[]{:S(2)}) collective-permute-start(bf16[128,1024]{1,0:T(8,128)(2,1)S(1)} %get-tuple-element.112), channel_id=1, source_target_pairs={{0,8},{8,0},{4,12},{12,4},{1,9},{9,1},{5,13},{13,5},{2,10},{10,2},... | collective-permute-start | bytes 786440 | tf_op jit(solution)/shard_map/ppermute | solution.py:1177
  17.8 17.7 %collective-permute-start.3 = (bf16[128,1024]{1,0:T(8,128)(2,1)S(1)}, bf16[128,1024]{1,0:T(8,128)(2,1)S(1)}, u32[]{:S(2)}, u32[]{:S(2)}) collective-permute-start(bf16[128,1024]{1,0:T(8,128)(2,1)S(1)} %bitcast.169), channel_id=1, source_target_pairs={{0,2},{2,0},{1,3},{3,1},{4,6},{6,4},{5,7},{7,5},{8,10},{10,8},{9,1... | collective-permute-start | bytes 786440 | tf_op jit(solution)/shard_map/ppermute | solution.py:1177
  21.3 61.7 %all-to-all-start = ((bf16[32,40,192]{2,1,0:T(8,128)(2,1)}), bf16[32,40,192]{2,1,0:T(8,128)(2,1)S(1)}, u32[]{:S(2)}, u32[]{:S(2)}) async-start(bf16[32,40,192]{2,1,0:T(8,128)(2,1)} %bitcast.6), calls=%async_computation | async-start | bytes 1310720 | tf_op jit(solution)/shard_map/all_to_all | solution.py:1276
  25.9 325.9 %all-gather.7.cloned.1.call-start = ((), (), s32[]{:S(2)}) async-start(), calls=%async_computation.7 | async-start | bytes 3538944 | tf_op jit(solution)/shard_map/all_gather | solution.py:1356
  37.9 20.0 %collective-permute-start.4 = (bf16[2,128,1024]{2,1,0:T(8,128)(2,1)S(1)}, bf16[2,128,1024]{2,1,0:T(8,128)(2,1)S(1)}, u32[]{:S(2)}, u32[]{:S(2)}) collective-permute-start(bf16[2,128,1024]{2,1,0:T(8,128)(2,1)S(1)} %get-tuple-element.110), channel_id=1, source_target_pairs={{0,4},{4,0},{8,12},{12,8},{1,5},{5,1},{9,13},{13,9},{2,6},{6,2},{1... | collective-permute-start | bytes 1572872 | tf_op jit(solution)/shard_map/ppermute | solution.py:1177
  38.0 16.0 %collective-permute-start.5 = (bf16[128,1024]{1,0:T(8,128)(2,1)}, bf16[128,1024]{1,0:T(8,128)(2,1)S(1)}, u32[]{:S(2)}, u32[]{:S(2)}) collective-permute-start(bf16[128,1024]{1,0:T(8,128)(2,1)} %copy-done.29), channel_id=1, source_target_pairs={{0,16},{16,0},{1,17},{17,1},{2,18},{18,2},{3,19},{19,3},{4,20},{20... | collective-permute-start | bytes 786440 | tf_op jit(solution)/shard_map/ppermute | solution.py:1177
  59.1 19.1 %collective-permute-start.7 = (bf16[2,128,1024]{2,1,0:T(8,128)(2,1)S(1)}, bf16[2,128,1024]{2,1,0:T(8,128)(2,1)S(1)}, u32[]{:S(2)}, u32[]{:S(2)}) collective-permute-start(bf16[2,128,1024]{2,1,0:T(8,128)(2,1)S(1)} %get-tuple-element.108), channel_id=1, source_target_pairs={{0,4},{4,0},{8,12},{12,8},{1,5},{5,1},{9,13},{13,9},{2,6},{6,2},{1... | collective-permute-start | bytes 1572872 | tf_op jit(solution)/shard_map/ppermute | solution.py:1177
  62.8 48.8 %collective-permute-start.6 = (bf16[2,2,128,1024]{3,2,1,0:T(8,128)(2,1)S(1)}, bf16[2,2,128,1024]{3,2,1,0:T(8,128)(2,1)}, u32[]{:S(2)}, u32[]{:S(2)}) collective-permute-start(bf16[2,2,128,1024]{3,2,1,0:T(8,128)(2,1)S(1)} %pad_maximum_fusion), channel_id=1, source_target_pairs={{0,16},{16,0},{1,17},{17,1},{2,18},{18,2},{3,19},{19,3},{4,20},{20... | collective-permute-start | bytes 3145736 | tf_op jit(solution)/shard_map/ppermute | solution.py:1177
  79.3 37.4 %collective-permute-start.8 = (bf16[2,2,128,1024]{3,2,1,0:T(8,128)(2,1)}, bf16[2,2,128,1024]{3,2,1,0:T(8,128)(2,1)}, u32[]{:S(2)}, u32[]{:S(2)}) collective-permute-start(bf16[2,2,128,1024]{3,2,1,0:T(8,128)(2,1)} %pad_maximum_fusion.1), channel_id=1, source_target_pairs={{0,2},{2,0},{1,3},{3,1},{4,6},{6,4},{5,7},{7,5},{8,10},{10,8},{9,1... | collective-permute-start | bytes 3145736 | tf_op jit(solution)/shard_map/ppermute | solution.py:1177
  81.5 37.0 %collective-permute-start.9 = (bf16[2,2,128,1024]{3,2,1,0:T(8,128)(2,1)S(1)}, bf16[2,2,128,1024]{3,2,1,0:T(8,128)(2,1)}, u32[]{:S(2)}, u32[]{:S(2)}) collective-permute-start(bf16[2,2,128,1024]{3,2,1,0:T(8,128)(2,1)S(1)} %pad_maximum_fusion), channel_id=1, source_target_pairs={{0,1},{1,0},{2,3},{3,2},{4,5},{5,4},{6,7},{7,6},{8,9},{9,8},{10,11... | collective-permute-start | bytes 3145736 | tf_op jit(solution)/shard_map/ppermute | solution.py:1177
  83.6 37.0 %collective-permute-start.11 = (bf16[2,2,128,1024]{3,2,1,0:T(8,128)(2,1)}, bf16[2,2,128,1024]{3,2,1,0:T(8,128)(2,1)S(1)}, u32[]{:S(2)}, u32[]{:S(2)}) collective-permute-start(bf16[2,2,128,1024]{3,2,1,0:T(8,128)(2,1)} %pad_maximum_fusion.1), channel_id=1, source_target_pairs={{0,1},{1,0},{2,3},{3,2},{4,5},{5,4},{6,7},{7,6},{8,9},{9,8},{10,11... | collective-permute-start | bytes 3145736 | tf_op jit(solution)/shard_map/ppermute | solution.py:1177
  111.6 8.6 %collective-permute-start.10 = (bf16[2,2,128,1024]{3,2,1,0:T(8,128)(2,1)}, bf16[2,2,128,1024]{3,2,1,0:T(8,128)(2,1)S(1)}, u32[]{:S(2)}, u32[]{:S(2)}) collective-permute-start(bf16[2,2,128,1024]{3,2,1,0:T(8,128)(2,1)} %collective-permute-done.6), channel_id=1, source_target_pairs={{0,1},{1,0},{2,3},{3,2},{4,5},{5,4},{6,7},{7,6},{8,9},{9,8},{10,11... | collective-permute-start | bytes 3145736 | tf_op jit(solution)/shard_map/ppermute | solution.py:1177
  116.7 4.5 %collective-permute-start.12 = (bf16[2,2,128,1024]{3,2,1,0:T(8,128)(2,1)}, bf16[2,2,128,1024]{3,2,1,0:T(8,128)(2,1)S(1)}, u32[]{:S(2)}, u32[]{:S(2)}) collective-permute-start(bf16[2,2,128,1024]{3,2,1,0:T(8,128)(2,1)} %collective-permute-done.8), channel_id=1, source_target_pairs={{0,1},{1,0},{2,3},{3,2},{4,5},{5,4},{6,7},{7,6},{8,9},{9,8},{10,11... | collective-permute-start | bytes 3145736 | tf_op jit(solution)/shard_map/ppermute | solution.py:1177
  167.9 197.1 %reduce-scatter.2.cloned.1.call-start = ((), (), s32[]{:S(2)}) async-start(), calls=%async_computation.5 | async-start | bytes 10027008 | tf_op jit(solution)/shard_map/reduce_scatter | solution.py:1386
  168.1 7.3 %collective-permute-start = (bf16[2,128,1024]{2,1,0:T(8,128)(2,1)S(1)}, bf16[2,128,1024]{2,1,0:T(8,128)(2,1)S(1)}, u32[]{:S(2)}, u32[]{:S(2)}) collective-permute-start(bf16[2,128,1024]{2,1,0:T(8,128)(2,1)S(1)} %copy-done.22), channel_id=1, source_target_pairs={{0,1},{1,0},{2,3},{3,2},{4,5},{5,4},{6,7},{7,6},{8,9},{9,8},{10,11... | collective-permute-start | bytes 1572872 | tf_op jit(solution)/shard_map/ppermute | solution.py:1177
  169.3 6.1 %collective-permute-start.1 = (bf16[2,128,1024]{2,1,0:T(8,128)(2,1)S(1)}, bf16[2,128,1024]{2,1,0:T(8,128)(2,1)S(1)}, u32[]{:S(2)}, u32[]{:S(2)}) collective-permute-start(bf16[2,128,1024]{2,1,0:T(8,128)(2,1)S(1)} %copy-done.5), channel_id=1, source_target_pairs={{0,1},{1,0},{2,3},{3,2},{4,5},{5,4},{6,7},{7,6},{8,9},{9,8},{10,11... | collective-permute-start | bytes 1572872 | tf_op jit(solution)/shard_map/ppermute | solution.py:1177
  175.3 2.5 collective-permute-start.16
  205.8 2.5 collective-permute-start.19
  279.1 67.8 %all-to-all-start.3 = ((bf16[16,272,256]{2,1,0:T(8,128)(2,1)}), bf16[16,272,256]{2,1,0:T(8,128)(2,1)}, u32[]{:S(2)}, u32[]{:S(2)}) async-start(bf16[16,272,256]{2,1,0:T(8,128)(2,1)} %attend_backward.1), calls=%async_computation.3 | async-start | bytes 4456448 | tf_op jit(solution)/shard_map/all_to_all | solution.py:1398
  284.6 4.6 %collective-permute-start.17 = (bf16[256,1024]{1,0:T(8,128)(2,1)}, bf16[256,1024]{1,0:T(8,128)(2,1)}, u32[]{:S(2)}, u32[]{:S(2)}) collective-permute-start(bf16[256,1024]{1,0:T(8,128)(2,1)} %get-tuple-element.69), channel_id=1, source_target_pairs={{0,1},{1,0},{2,3},{3,2},{4,5},{5,4},{6,7},{7,6},{8,9},{9,8},{10,11... | collective-permute-start | bytes 1572872 | tf_op jit(solution)/shard_map/ppermute | solution.py:1177
  348.5 10.0 %collective-permute-start.21 = (f32[8,33,192]{2,0,1:T(8,128)S(1)}, f32[8,33,192]{2,0,1:T(8,128)S(1)}, u32[]{:S(2)}, u32[]{:S(2)}) collective-permute-start(f32[8,33,192]{2,0,1:T(8,128)S(1)} %pad_maximum_fusion.6), channel_id=1, source_target_pairs={{0,1},{1,0},{2,3},{3,2},{4,5},{5,4},{6,7},{7,6},{8,9},{9,8},{10,11... | collective-permute-start | bytes 608264 | tf_op jit(solution)/shard_map/ppermute | solution.py:1177
  358.2 4.9 %collective-permute-start.20 = (bf16[256,1024]{1,0:T(8,128)(2,1)}, bf16[256,1024]{1,0:T(8,128)(2,1)}, u32[]{:S(2)}, u32[]{:S(2)}) collective-permute-start(bf16[256,1024]{1,0:T(8,128)(2,1)} %get-tuple-element.88), channel_id=1, source_target_pairs={{0,1},{1,0},{2,3},{3,2},{4,5},{5,4},{6,7},{7,6},{8,9},{9,8},{10,11... | collective-permute-start | bytes 1572872 | tf_op jit(solution)/shard_map/ppermute | solution.py:1177
  (54 other events, 433.4 us)
Sparse Core Ops, SparseCore 0:
  15.5 148.0 all-gather.4
  168.0 37.9 all-gather.6
  219.9 140.0 reduce-scatter.1

commit v3 on v2

--- a/solution.py
+++ b/solution.py
@@ -699,7 +699,7 @@
     )(bound, inloc, outloc, grad_t, qs, ks, vs, attn_t, lse, *pieces)
 
 
-HALF_STEP = 512
+HALF_STEP = 1024
 
 
 def gelu_pair(values):

time: 378 us -> 378 us (level)
  transfers between devices with their start and end apart: 28 -> 28, of which waited for: 12 -> 12; matrix products, arithmetic and copies ran while one was open for 8% -> 8% of each run, Pallas kernels for 26% -> 25%
where the time goes in v3:
time: 378 us; the launch traced here: 376 us
  waiting for transfers between devices  129 us (34%)
  Pallas kernels  97.7 us (26%)
  blocking collectives  45.8 us (12%)
  starting transfers between devices  35.9 us (9%)
  local copies, waits for them, and re-layouts  26.7 us (7%)
  other arithmetic  17.7 us (5%)
  between operations  14.8 us (4%)
  matrix products  8.41 us (2%)
    ppermute x23, waiting for transfers between devices, swap(): return lax.ppermute(values, axis, pairs)  73.9 us
    all_to_all x1, waiting for transfers between devices, fast_body(): lax.all_to_all(send_grads, chips, split_axis=0, concat_axis=0, tiled=True)  55.1 us
    pallas_call x1, Pallas kernels, attend_backward(): pl.pallas_call(functools.partial(backward_kernel, head_size, len(pieces),...  30.6 us
    pallas_call x1, Pallas kernels, middle(): pl.pallas_call(functools.partial(middle_kernel, len(pieces), share), out_...  25.8 us
    ppermute x23, starting transfers between devices, swap(): return lax.ppermute(values, axis, pairs)  25.8 us
    all_to_all x1, blocking collectives, fast_body(): lax.all_to_all(grad_send, chips, split_axis=0, concat_axis=0, tiled=True)  23.2 us
    all_to_all x1, blocking collectives, fast_body(): lax.all_to_all(attn_send, chips, split_axis=0, concat_axis=0, tiled=True)  22.6 us
    pallas_call x1, Pallas kernels, attend_forward(): pl.pallas_call(functools.partial(forward_kernel, head_size), out_shape=(j...  19.4 us
  transfers between devices with their start and end apart: 28, of which 12 were waited for; matrix products, arithmetic and copies ran while one was open for 8% of the time, Pallas kernels for 25%

profile of v3, /device:TPU:11, one launch (start us, length us, event | category | flops | bytes accessed | tf_op | source)
XLA Modules:
  0.0 376.2 jit_solution(7363999332450042437)
XLA Ops:
  15.4 2.4 collective-permute-start.2
  21.3 4.6 %all-to-all-start = ((bf16[32,40,192]{2,1,0:T(8,128)(2,1)}), bf16[32,40,192]{2,1,0:T(8,128)(2,1)S(1)}, u32[]{:S(2)}, u32[]{:S(2)}) async-start(bf16[32,40,192]{2,1,0:T(8,128)(2,1)} %bitcast.6), calls=%async_computation | async-start | bytes 1310720 | tf_op jit(solution)/shard_map/all_to_all | solution.py:1276
  26.0 9.5 %collective-permute-done.2 = bf16[128,1024]{1,0:T(8,128)(2,1)S(1)} collective-permute-done((bf16[128,1024]{1,0:T(8,128)(2,1)S(1)}, bf16[128,1024]{1,0:T(8,128)(2,1)S(1)}, u32[]{:S(2)}, u32[]{:S(2)}) %collective-permute-start.2) | collective-permute-done | bytes 262176 | tf_op jit(solution)/shard_map/ppermute | solution.py:1177
  38.0 2.6 collective-permute-start.5
  40.9 13.1 %collective-permute-done.5 = bf16[128,1024]{1,0:T(8,128)(2,1)S(1)} collective-permute-done((bf16[128,1024]{1,0:T(8,128)(2,1)}, bf16[128,1024]{1,0:T(8,128)(2,1)S(1)}, u32[]{:S(2)}, u32[]{:S(2)}) %collective-permute-start.5) | collective-permute-done | bytes 262176 | tf_op jit(solution)/shard_map/ppermute | solution.py:1177
  54.0 3.9 %collective-permute-done.4 = bf16[2,128,1024]{2,1,0:T(8,128)(2,1)S(1)} collective-permute-done((bf16[2,128,1024]{2,1,0:T(8,128)(2,1)S(1)}, bf16[2,128,1024]{2,1,0:T(8,128)(2,1)S(1)}, u32[]{:S(2)}, u32[]{:S(2)}) %collective-permute-start.4) | collective-permute-done | bytes 524320 | tf_op jit(solution)/shard_map/ppermute | solution.py:1177
  59.1 2.4 collective-permute-start.7
  62.8 3.0 collective-permute-start.6
  65.8 12.4 %collective-permute-done.7 = bf16[2,128,1024]{2,1,0:T(8,128)(2,1)S(1)} collective-permute-done((bf16[2,128,1024]{2,1,0:T(8,128)(2,1)S(1)}, bf16[2,128,1024]{2,1,0:T(8,128)(2,1)S(1)}, u32[]{:S(2)}, u32[]{:S(2)}) %collective-permute-start.7) | collective-permute-done | bytes 524320 | tf_op jit(solution)/shard_map/ppermute | solution.py:1177
  83.7 27.8 %collective-permute-done.6 = bf16[2,2,128,1024]{3,2,1,0:T(8,128)(2,1)} collective-permute-done((bf16[2,2,128,1024]{3,2,1,0:T(8,128)(2,1)S(1)}, bf16[2,2,128,1024]{3,2,1,0:T(8,128)(2,1)}, u32[]{:S(2)}, u32[]{:S(2)}) %collective-permute-start.6) | collective-permute-done | bytes 1048608 | tf_op jit(solution)/shard_map/ppermute | solution.py:1177
  122.2 19.4 %attend_forward.1 = (bf16[16,64,256]{2,1,0:T(8,128)(2,1)S(1)}, bf16[4096,64]{1,0:T(8,128)(2,1)S(1)}, bf16[4096,64]{1,0:T(8,128)(2,1)S(1)}, bf16[4096,64]{1,0:T(8...) custom-call(s32[1]{0:T(128)S(1)} %bitcast.147, s32[64]{0:T(128)S(1)} %get-tuple-element.96.inloc, ...), custom_call_target="tpu_custom_call" | custom-call | flops 8589934592 | bytes 8388608 | tf_op jit(solution)/shard_map/attend_forward/pallas_call | solution.py:544
  144.3 22.6 %all_to_all.20.got = bf16[16,64,256]{2,1,0:T(8,128)(2,1)} all-to-all(bf16[16,64,256]{2,1,0:T(8,128)(2,1)S(1)} %get-tuple-element.61), channel_id=1, replica_groups=mesh['head'=2,'z'=4,'x'=2,'core'=2] {'z','x','head'}, dimensions={0} | all-to-all | bytes 1048576 | tf_op jit(solution)/shard_map/all_to_all | solution.py:1353
  169.8 5.0 %project.1 = (f32[512,1024]{1,0:T(8,128)}, bf16[256,1024]{1,0:T(8,128)(2,1)}, bf16[256,1024]{1,0:T(8,128)(2,1)}, bf16[512,512]{1,0:T(8,128)(2,1)}) custom-call(s32[2,16]{1,0:T(2,128)} %fusion.32.table, bf16[16,64,256]{2,1,0:T(8,128)(2,1)} %all_to_all.20.got, bf16[16,304,1024]{2,1,0:T(8,128)(2,1)} %bitcast.149), custom_call_target="tpu_custom_call" | custom-call | flops 536870912 | bytes 4194304 | tf_op jit(solution)/shard_map/project/pallas_call | solution.py:761
  178.6 25.8 %middle.1 = (f32[512,1024]{1,0:T(8,128)}, f32[256,1024]{1,0:T(8,128)}, bf16[256,1024]{1,0:T(8,128)(2,1)}, f32[512,1024]{1,0:T(8,128)}, bf16[256,1024]{1,0:T(8,12...) custom-call(s32[2,16]{1,0:T(2,128)} %fusion.32.table, ...), custom_call_target="tpu_custom_call" | custom-call | flops 12884901888 | bytes 16777216 | tf_op jit(solution)/shard_map/middle/pallas_call | solution.py:909
  213.1 4.1 %branch_back.1 = (f32[256,1024]{1,0:T(8,128)S(1)}, bf16[512,1024]{1,0:T(8,128)(2,1)S(1)}, bf16[16,8,256]{2,1,0:T(8,128)(2,1)S(1)}, bf16[16,288,1024]{2,1,0:T(8,128)(2,1)}) custom-call(s32[2,16]{1,0:T(2,128)S(1)} %copy-done.12, f32[512,1024]{1,0:T(8,128)S(1)} %copy-done.2, bf16[256,1024]{1,0:T(8,128)(2,1)S(1)} %bitcast.144, ...), custom_call_target="tpu_custom_call", output_to_operand_aliasing={{3}: (10, {})} | custom-call | flops 536870912 | bytes 8388608 | tf_op jit(solution)/shard_map/branch_back/pallas_call | solution.py:1013
  218.8 4.3 %attention_back.1 = bf16[16,72,256]{2,1,0:T(8,128)(2,1)} custom-call(s32[2,16]{1,0:T(2,128)} %fusion.32.table, bf16[512,1024]{1,0:T(8,128)(2,1)} %copy-done.4, bf16[16,8,256]{2,1,0:T(8,128)(2,1)} %copy-done.10, bf16[16,304,1024]{2,1,0:T(8,128)(2,1)} %bitcast.151), custom_call_target="tpu_custom_call" | custom-call | flops 536870912 | bytes 2097152 | tf_op jit(solution)/shard_map/attention_back/pallas_call | solution.py:1062
  223.1 23.2 %all_to_all.21.grad_t = bf16[16,72,256]{2,1,0:T(8,128)(2,1)S(1)} all-to-all(bf16[16,72,256]{2,1,0:T(8,128)(2,1)} %attention_back.1), channel_id=1, replica_groups=mesh['head'=2,'z'=4,'x'=2,'core'=2] {'z','x','head'}, dimensions={0} | all-to-all | bytes 1179648 | tf_op jit(solution)/shard_map/all_to_all | solution.py:1380
  247.6 30.6 %attend_backward.1 = bf16[16,272,256]{2,1,0:T(8,128)(2,1)} custom-call(s32[1]{0:T(128)S(1)} %bitcast.148, s32[64]{0:T(128)S(1)} %get-tuple-element.96.inloc, s32[64]{0:T(128)S(1)} %get-tuple-element.95.outloc, bf16[16,72,256]{2,1,0:T(8,128)(2,1)S(1)} %all_to_all.21.grad_t, bf16[4096,64]{1,0:T(8,128)(2,1)S(1)} %copy-done.15, bf16[4096,64]{1,0:T(8,128)(2,1)S(1)} %copy-done.17, ...), custom_call_target="tpu_custom_call" | custom-call | flops 21474836480 | bytes 16777216 | tf_op jit(solution)/shard_map/attend_backward/pallas_call | solution.py:678
  278.2 5.4 %all-to-all-start.3 = ((bf16[16,272,256]{2,1,0:T(8,128)(2,1)}), bf16[16,272,256]{2,1,0:T(8,128)(2,1)}, u32[]{:S(2)}, u32[]{:S(2)}) async-start(bf16[16,272,256]{2,1,0:T(8,128)(2,1)} %attend_backward.1), calls=%async_computation.3 | async-start | bytes 4456448 | tf_op jit(solution)/shard_map/all_to_all | solution.py:1398
  283.6 2.8 collective-permute-start.17
  290.9 55.1 %all-to-all-done.3.got = bf16[16,272,256]{2,1,0:T(8,128)(2,1)} async-done(((bf16[16,272,256]{2,1,0:T(8,128)(2,1)}), bf16[16,272,256]{2,1,0:T(8,128)(2,1)}, u32[]{:S(2)}, u32[]{:S(2)}) %all-to-all-start.3) | async-done | bytes 2228256 | tf_op jit(solution)/shard_map/all_to_all | solution.py:1398
  347.6 2.8 collective-permute-start.21
  350.9 6.4 %finish.1 = (f32[256,1024]{1,0:T(8,128)}, bf16[256,1024]{1,0:T(8,128)(2,1)}) custom-call(bf16[16,272,256]{2,1,0:T(8,128)(2,1)} %all-to-all-done.3.got, bf16[8,192,1024]{2,1,0:T(8,128)(2,1)} %bitcast.186), custom_call_target="tpu_custom_call" | custom-call | flops 1610612736 | bytes 5242880 | tf_op jit(solution)/shard_map/finish/pallas_call | solution.py:1110
  367.5 2.2 unpack.1
  (247 shorter events, 70.0 us)
Async XLA Ops:
  7.3 162.5 %all-gather.5.cloned.1.call-start = ((), (), s32[]{:S(2)}) async-start(), calls=%async_computation.6 | async-start | bytes 10584064 | tf_op jit(solution)/shard_map/all_gather | solution.py:1342
  11.7 2.4 collective-permute-start.13
  15.4 20.1 %collective-permute-start.2 = (bf16[128,1024]{1,0:T(8,128)(2,1)S(1)}, bf16[128,1024]{1,0:T(8,128)(2,1)S(1)}, u32[]{:S(2)}, u32[]{:S(2)}) collective-permute-start(bf16[128,1024]{1,0:T(8,128)(2,1)S(1)} %get-tuple-element.112), channel_id=1, source_target_pairs={{0,8},{8,0},{4,12},{12,4},{1,9},{9,1},{5,13},{13,5},{2,10},{10,2},... | collective-permute-start | bytes 786440 | tf_op jit(solution)/shard_map/ppermute | solution.py:1177
  17.8 17.7 %collective-permute-start.3 = (bf16[128,1024]{1,0:T(8,128)(2,1)S(1)}, bf16[128,1024]{1,0:T(8,128)(2,1)S(1)}, u32[]{:S(2)}, u32[]{:S(2)}) collective-permute-start(bf16[128,1024]{1,0:T(8,128)(2,1)S(1)} %bitcast.169), channel_id=1, source_target_pairs={{0,2},{2,0},{1,3},{3,1},{4,6},{6,4},{5,7},{7,5},{8,10},{10,8},{9,1... | collective-permute-start | bytes 786440 | tf_op jit(solution)/shard_map/ppermute | solution.py:1177
  21.3 61.7 %all-to-all-start = ((bf16[32,40,192]{2,1,0:T(8,128)(2,1)}), bf16[32,40,192]{2,1,0:T(8,128)(2,1)S(1)}, u32[]{:S(2)}, u32[]{:S(2)}) async-start(bf16[32,40,192]{2,1,0:T(8,128)(2,1)} %bitcast.6), calls=%async_computation | async-start | bytes 1310720 | tf_op jit(solution)/shard_map/all_to_all | solution.py:1276
  25.9 325.0 %all-gather.7.cloned.1.call-start = ((), (), s32[]{:S(2)}) async-start(), calls=%async_computation.7 | async-start | bytes 3538944 | tf_op jit(solution)/shard_map/all_gather | solution.py:1356
  37.9 20.0 %collective-permute-start.4 = (bf16[2,128,1024]{2,1,0:T(8,128)(2,1)S(1)}, bf16[2,128,1024]{2,1,0:T(8,128)(2,1)S(1)}, u32[]{:S(2)}, u32[]{:S(2)}) collective-permute-start(bf16[2,128,1024]{2,1,0:T(8,128)(2,1)S(1)} %get-tuple-element.110), channel_id=1, source_target_pairs={{0,4},{4,0},{8,12},{12,8},{1,5},{5,1},{9,13},{13,9},{2,6},{6,2},{1... | collective-permute-start | bytes 1572872 | tf_op jit(solution)/shard_map/ppermute | solution.py:1177
  38.0 16.0 %collective-permute-start.5 = (bf16[128,1024]{1,0:T(8,128)(2,1)}, bf16[128,1024]{1,0:T(8,128)(2,1)S(1)}, u32[]{:S(2)}, u32[]{:S(2)}) collective-permute-start(bf16[128,1024]{1,0:T(8,128)(2,1)} %copy-done.29), channel_id=1, source_target_pairs={{0,16},{16,0},{1,17},{17,1},{2,18},{18,2},{3,19},{19,3},{4,20},{20... | collective-permute-start | bytes 786440 | tf_op jit(solution)/shard_map/ppermute | solution.py:1177
  59.1 19.1 %collective-permute-start.7 = (bf16[2,128,1024]{2,1,0:T(8,128)(2,1)S(1)}, bf16[2,128,1024]{2,1,0:T(8,128)(2,1)S(1)}, u32[]{:S(2)}, u32[]{:S(2)}) collective-permute-start(bf16[2,128,1024]{2,1,0:T(8,128)(2,1)S(1)} %get-tuple-element.108), channel_id=1, source_target_pairs={{0,4},{4,0},{8,12},{12,8},{1,5},{5,1},{9,13},{13,9},{2,6},{6,2},{1... | collective-permute-start | bytes 1572872 | tf_op jit(solution)/shard_map/ppermute | solution.py:1177
  62.8 48.8 %collective-permute-start.6 = (bf16[2,2,128,1024]{3,2,1,0:T(8,128)(2,1)S(1)}, bf16[2,2,128,1024]{3,2,1,0:T(8,128)(2,1)}, u32[]{:S(2)}, u32[]{:S(2)}) collective-permute-start(bf16[2,2,128,1024]{3,2,1,0:T(8,128)(2,1)S(1)} %pad_maximum_fusion), channel_id=1, source_target_pairs={{0,16},{16,0},{1,17},{17,1},{2,18},{18,2},{3,19},{19,3},{4,20},{20... | collective-permute-start | bytes 3145736 | tf_op jit(solution)/shard_map/ppermute | solution.py:1177
  79.3 37.4 %collective-permute-start.8 = (bf16[2,2,128,1024]{3,2,1,0:T(8,128)(2,1)}, bf16[2,2,128,1024]{3,2,1,0:T(8,128)(2,1)}, u32[]{:S(2)}, u32[]{:S(2)}) collective-permute-start(bf16[2,2,128,1024]{3,2,1,0:T(8,128)(2,1)} %pad_maximum_fusion.1), channel_id=1, source_target_pairs={{0,2},{2,0},{1,3},{3,1},{4,6},{6,4},{5,7},{7,5},{8,10},{10,8},{9,1... | collective-permute-start | bytes 3145736 | tf_op jit(solution)/shard_map/ppermute | solution.py:1177
  81.5 37.0 %collective-permute-start.9 = (bf16[2,2,128,1024]{3,2,1,0:T(8,128)(2,1)S(1)}, bf16[2,2,128,1024]{3,2,1,0:T(8,128)(2,1)}, u32[]{:S(2)}, u32[]{:S(2)}) collective-permute-start(bf16[2,2,128,1024]{3,2,1,0:T(8,128)(2,1)S(1)} %pad_maximum_fusion), channel_id=1, source_target_pairs={{0,1},{1,0},{2,3},{3,2},{4,5},{5,4},{6,7},{7,6},{8,9},{9,8},{10,11... | collective-permute-start | bytes 3145736 | tf_op jit(solution)/shard_map/ppermute | solution.py:1177
  83.6 37.0 %collective-permute-start.11 = (bf16[2,2,128,1024]{3,2,1,0:T(8,128)(2,1)}, bf16[2,2,128,1024]{3,2,1,0:T(8,128)(2,1)S(1)}, u32[]{:S(2)}, u32[]{:S(2)}) collective-permute-start(bf16[2,2,128,1024]{3,2,1,0:T(8,128)(2,1)} %pad_maximum_fusion.1), channel_id=1, source_target_pairs={{0,1},{1,0},{2,3},{3,2},{4,5},{5,4},{6,7},{7,6},{8,9},{9,8},{10,11... | collective-permute-start | bytes 3145736 | tf_op jit(solution)/shard_map/ppermute | solution.py:1177
  111.6 8.6 %collective-permute-start.10 = (bf16[2,2,128,1024]{3,2,1,0:T(8,128)(2,1)}, bf16[2,2,128,1024]{3,2,1,0:T(8,128)(2,1)S(1)}, u32[]{:S(2)}, u32[]{:S(2)}) collective-permute-start(bf16[2,2,128,1024]{3,2,1,0:T(8,128)(2,1)} %collective-permute-done.6), channel_id=1, source_target_pairs={{0,1},{1,0},{2,3},{3,2},{4,5},{5,4},{6,7},{7,6},{8,9},{9,8},{10,11... | collective-permute-start | bytes 3145736 | tf_op jit(solution)/shard_map/ppermute | solution.py:1177
  116.7 4.5 %collective-permute-start.12 = (bf16[2,2,128,1024]{3,2,1,0:T(8,128)(2,1)}, bf16[2,2,128,1024]{3,2,1,0:T(8,128)(2,1)S(1)}, u32[]{:S(2)}, u32[]{:S(2)}) collective-permute-start(bf16[2,2,128,1024]{3,2,1,0:T(8,128)(2,1)} %collective-permute-done.8), channel_id=1, source_target_pairs={{0,1},{1,0},{2,3},{3,2},{4,5},{5,4},{6,7},{7,6},{8,9},{9,8},{10,11... | collective-permute-start | bytes 3145736 | tf_op jit(solution)/shard_map/ppermute | solution.py:1177
  167.9 196.2 %reduce-scatter.2.cloned.1.call-start = ((), (), s32[]{:S(2)}) async-start(), calls=%async_computation.5 | async-start | bytes 10027008 | tf_op jit(solution)/shard_map/reduce_scatter | solution.py:1386
  167.9 7.5 %collective-permute-start = (bf16[2,128,1024]{2,1,0:T(8,128)(2,1)S(1)}, bf16[2,128,1024]{2,1,0:T(8,128)(2,1)S(1)}, u32[]{:S(2)}, u32[]{:S(2)}) collective-permute-start(bf16[2,128,1024]{2,1,0:T(8,128)(2,1)S(1)} %copy-done.22), channel_id=1, source_target_pairs={{0,1},{1,0},{2,3},{3,2},{4,5},{5,4},{6,7},{7,6},{8,9},{9,8},{10,11... | collective-permute-start | bytes 1572872 | tf_op jit(solution)/shard_map/ppermute | solution.py:1177
  169.1 6.3 %collective-permute-start.1 = (bf16[2,128,1024]{2,1,0:T(8,128)(2,1)S(1)}, bf16[2,128,1024]{2,1,0:T(8,128)(2,1)S(1)}, u32[]{:S(2)}, u32[]{:S(2)}) collective-permute-start(bf16[2,128,1024]{2,1,0:T(8,128)(2,1)S(1)} %copy-done.5), channel_id=1, source_target_pairs={{0,1},{1,0},{2,3},{3,2},{4,5},{5,4},{6,7},{7,6},{8,9},{9,8},{10,11... | collective-permute-start | bytes 1572872 | tf_op jit(solution)/shard_map/ppermute | solution.py:1177
  175.3 2.5 collective-permute-start.16
  204.9 2.5 collective-permute-start.19
  278.2 67.8 %all-to-all-start.3 = ((bf16[16,272,256]{2,1,0:T(8,128)(2,1)}), bf16[16,272,256]{2,1,0:T(8,128)(2,1)}, u32[]{:S(2)}, u32[]{:S(2)}) async-start(bf16[16,272,256]{2,1,0:T(8,128)(2,1)} %attend_backward.1), calls=%async_computation.3 | async-start | bytes 4456448 | tf_op jit(solution)/shard_map/all_to_all | solution.py:1398
  283.6 4.6 %collective-permute-start.17 = (bf16[256,1024]{1,0:T(8,128)(2,1)}, bf16[256,1024]{1,0:T(8,128)(2,1)}, u32[]{:S(2)}, u32[]{:S(2)}) collective-permute-start(bf16[256,1024]{1,0:T(8,128)(2,1)} %get-tuple-element.69), channel_id=1, source_target_pairs={{0,1},{1,0},{2,3},{3,2},{4,5},{5,4},{6,7},{7,6},{8,9},{9,8},{10,11... | collective-permute-start | bytes 1572872 | tf_op jit(solution)/shard_map/ppermute | solution.py:1177
  347.6 10.0 %collective-permute-start.21 = (f32[8,33,192]{2,0,1:T(8,128)S(1)}, f32[8,33,192]{2,0,1:T(8,128)S(1)}, u32[]{:S(2)}, u32[]{:S(2)}) collective-permute-start(f32[8,33,192]{2,0,1:T(8,128)S(1)} %pad_maximum_fusion.6), channel_id=1, source_target_pairs={{0,1},{1,0},{2,3},{3,2},{4,5},{5,4},{6,7},{7,6},{8,9},{9,8},{10,11... | collective-permute-start | bytes 608264 | tf_op jit(solution)/shard_map/ppermute | solution.py:1177
  357.3 4.9 %collective-permute-start.20 = (bf16[256,1024]{1,0:T(8,128)(2,1)}, bf16[256,1024]{1,0:T(8,128)(2,1)}, u32[]{:S(2)}, u32[]{:S(2)}) collective-permute-start(bf16[256,1024]{1,0:T(8,128)(2,1)} %get-tuple-element.88), channel_id=1, source_target_pairs={{0,1},{1,0},{2,3},{3,2},{4,5},{5,4},{6,7},{7,6},{8,9},{9,8},{10,11... | collective-permute-start | bytes 1572872 | tf_op jit(solution)/shard_map/ppermute | solution.py:1177
  (54 other events, 429.9 us)
Sparse Core Ops, SparseCore 0:
  15.5 148.0 all-gather.4
  168.0 37.9 all-gather.6
  218.9 139.6 reduce-scatter.1

commit v4 on v3

--- a/solution.py
+++ b/solution.py
@@ -448,7 +448,7 @@
 
 
 RUN = 64
-BLOCK = 512
+BLOCK = 1024
 NEG = -1000000000.0
 VM = pltpu.VMEM
 SM = pltpu.SMEM
@@ -468,6 +468,11 @@
 
 def first_block(start, bound):
     return jnp.where(start >= bound, bound // BLOCK, 0)
+
+
+def clear_block(block, bound):
+    last = (block + 1) * BLOCK - 1
+    return jnp.where(last >= bound, jnp.minimum((bound + BLOCK - 1) // BLOCK, block), 0)
 
 
 def forward_kernel(head_size, bound_ref, inloc, outloc, qkv, out, qs, ks, vs, attn_t, lse, vt, mixed):
@@ -497,9 +502,11 @@
         query_pos = start + lax.broadcasted_iota(jnp.int32, (1, BLOCK), 1)
         floor = jnp.where(query_pos >= bound, bound, 0)
 
-        def scores_of(index, diagonal):
+        def scores_of(index, diagonal, bounded=True):
             keys = ks[rows_at(index, BLOCK), :]
             scores = dot_nt(keys, queries)
+            if not bounded:
+                return scores
             key_pos = index * BLOCK + lax.broadcasted_iota(jnp.int32, (BLOCK, BLOCK), 0)
             visible = key_pos >= floor
             if diagonal:
@@ -512,9 +519,9 @@
         total = jnp.sum(weights, axis=0, keepdims=True)
         accum = dot_nn(vt[:, here], weights.astype(jnp.bfloat16))
 
-        def step(index, state):
+        def step(bounded, index, state):
             highest, total, accum = state
-            scores = scores_of(index, False)
+            scores = scores_of(index, False, bounded)
             higher = jnp.maximum(highest, jnp.max(scores, axis=0, keepdims=True))
             weights = jnp.exp(scores - higher)
             factor = jnp.exp(highest - higher)
@@ -522,7 +529,9 @@
             accum = accum * factor + dot_nn(vt[:, rows_at(index, BLOCK)], weights.astype(jnp.bfloat16))
             return higher, total, accum
 
-        highest, total, accum = lax.fori_loop(first_block(start, bound), block, step, (highest, total, accum))
+        first, clear = first_block(start, bound), clear_block(block, bound)
+        state = lax.fori_loop(first, clear, functools.partial(step, True), (highest, total, accum))
+        highest, total, accum = lax.fori_loop(clear, block, functools.partial(step, False), state)
         result = accum / total
         attn_t[:, here] = result.astype(jnp.bfloat16)
         lse[:, here] = highest + jnp.log(total)
@@ -601,14 +610,16 @@
         query_pos = start + lax.broadcasted_iota(jnp.int32, (1, BLOCK), 1)
         floor = jnp.where(query_pos >= bound, bound, 0)
 
-        def one(index, diagonal):
+        def one(index, diagonal, bounded=True):
             there = rows_at(index, BLOCK)
             scores = dot_nt(ks[there, :], queries)
-            key_pos = index * BLOCK + lax.broadcasted_iota(jnp.int32, (BLOCK, BLOCK), 0)
-            visible = key_pos >= floor
-            if diagonal:
-                visible = visible & (key_pos <= query_pos)
-            probs = jnp.where(visible, jnp.exp(scores - log_total), 0.0)
+            probs = jnp.exp(scores - log_total)
+            if bounded:
+                key_pos = index * BLOCK + lax.broadcasted_iota(jnp.int32, (BLOCK, BLOCK), 0)
+                visible = key_pos >= floor
+                if diagonal:
+                    visible = visible & (key_pos <= query_pos)
+                probs = jnp.where(visible, probs, 0.0)
             grad_probs = dot_nt(vs[there, :], grad)
             grad_scores = (probs * (grad_probs - delta)).astype(jnp.bfloat16)
             return (
@@ -622,13 +633,15 @@
         dv[there, :] = grad_v
         dk[there, :] = grad_k
 
-        def step(index, grad_q):
-            grad_v, grad_k, term, there = one(index, False)
+        def step(bounded, index, grad_q):
+            grad_v, grad_k, term, there = one(index, False, bounded)
             dv[there, :] += grad_v
             dk[there, :] += grad_k
             return grad_q + term
 
-        grad_q = lax.fori_loop(first_block(start, bound), block, step, grad_q)
+        first, clear = first_block(start, bound), clear_block(block, bound)
+        grad_q = lax.fori_loop(first, clear, functools.partial(step, True), grad_q)
+        grad_q = lax.fori_loop(clear, block, functools.partial(step, False), grad_q)
         wide[here, :head_size] = (grad_q.T * scale).astype(jnp.bfloat16)
 
     wide[:, head_size : 2 * head_size] = dk[...].astype(jnp.bfloat16)
@@ -652,7 +665,7 @@
         copy.wait()
     raw[...] = jnp.zeros_like(raw)
 
-    @pl.loop(0, tokens // BLOCK, unroll=2)
+    @pl.loop(0, tokens // BLOCK)
     def _(block):
         here = rows_at(block, BLOCK)
         turned = moved[here, :].astype(jnp.float32).T.astype(jnp.bfloat16)

time: 378 us -> 382 us (1.011); the launches traced: 376 us -> 376 us
  Pallas kernels: 97.7 us -> 92.9 us
  transfers between devices with their start and end apart: 28 -> 28, of which waited for: 12 -> 12; matrix products, arithmetic and copies ran while one was open for 8% -> 8% of each run, Pallas kernels for 25% -> 24%
where the time goes in v4:
time: 382 us; the launch traced here: 376 us
  waiting for transfers between devices  128 us (34%)
  Pallas kernels  92.9 us (24%)
  blocking collectives  48.1 us (13%)
  starting transfers between devices  38.8 us (10%)
  local copies, waits for them, and re-layouts  26.7 us (7%)
  other arithmetic  17.7 us (5%)
  between operations  15 us (4%)
  matrix products  8.4 us (2%)
    ppermute x23, waiting for transfers between devices, swap(): return lax.ppermute(values, axis, pairs)  73.7 us
    all_to_all x1, waiting for transfers between devices, fast_body(): lax.all_to_all(send_grads, chips, split_axis=0, concat_axis=0, tiled=True)  54.4 us
    pallas_call x1, Pallas kernels, attend_backward(): pl.pallas_call(functools.partial(backward_kernel, head_size, len(pieces),...  28.9 us
    pallas_call x1, Pallas kernels, middle(): pl.pallas_call(functools.partial(middle_kernel, len(pieces), share), out_...  25.8 us
    ppermute x23, starting transfers between devices, swap(): return lax.ppermute(values, axis, pairs)  25.7 us
    all_to_all x1, blocking collectives, fast_body(): lax.all_to_all(attn_send, chips, split_axis=0, concat_axis=0, tiled=True)  24.9 us
    all_to_all x1, blocking collectives, fast_body(): lax.all_to_all(grad_send, chips, split_axis=0, concat_axis=0, tiled=True)  23.3 us
    pallas_call x1, Pallas kernels, attend_forward(): pl.pallas_call(functools.partial(forward_kernel, head_size), out_shape=(j...  16.2 us
  transfers between devices with their start and end apart: 28, of which 12 were waited for; matrix products, arithmetic and copies ran while one was open for 8% of the time, Pallas kernels for 24%

profile of v4, /device:TPU:11, one launch (start us, length us, event | category | flops | bytes accessed | tf_op | source)
XLA Modules:
  0.0 375.9 jit_solution(10880164104693524466)
XLA Ops:
  15.4 2.4 collective-permute-start.2
  21.3 4.6 %all-to-all-start = ((bf16[32,40,192]{2,1,0:T(8,128)(2,1)}), bf16[32,40,192]{2,1,0:T(8,128)(2,1)S(1)}, u32[]{:S(2)}, u32[]{:S(2)}) async-start(bf16[32,40,192]{2,1,0:T(8,128)(2,1)} %bitcast.6), calls=%async_computation | async-start | bytes 1310720 | tf_op jit(solution)/shard_map/all_to_all | solution.py:1289
  26.1 9.4 %collective-permute-done.2 = bf16[128,1024]{1,0:T(8,128)(2,1)S(1)} collective-permute-done((bf16[128,1024]{1,0:T(8,128)(2,1)S(1)}, bf16[128,1024]{1,0:T(8,128)(2,1)S(1)}, u32[]{:S(2)}, u32[]{:S(2)}) %collective-permute-start.2) | collective-permute-done | bytes 262176 | tf_op jit(solution)/shard_map/ppermute | solution.py:1190
  38.0 2.6 collective-permute-start.5
  40.9 13.1 %collective-permute-done.5 = bf16[128,1024]{1,0:T(8,128)(2,1)S(1)} collective-permute-done((bf16[128,1024]{1,0:T(8,128)(2,1)}, bf16[128,1024]{1,0:T(8,128)(2,1)S(1)}, u32[]{:S(2)}, u32[]{:S(2)}) %collective-permute-start.5) | collective-permute-done | bytes 262176 | tf_op jit(solution)/shard_map/ppermute | solution.py:1190
  54.0 3.9 %collective-permute-done.4 = bf16[2,128,1024]{2,1,0:T(8,128)(2,1)S(1)} collective-permute-done((bf16[2,128,1024]{2,1,0:T(8,128)(2,1)S(1)}, bf16[2,128,1024]{2,1,0:T(8,128)(2,1)S(1)}, u32[]{:S(2)}, u32[]{:S(2)}) %collective-permute-start.4) | collective-permute-done | bytes 524320 | tf_op jit(solution)/shard_map/ppermute | solution.py:1190
  59.1 2.4 collective-permute-start.7
  62.8 3.0 collective-permute-start.6
  65.8 12.4 %collective-permute-done.7 = bf16[2,128,1024]{2,1,0:T(8,128)(2,1)S(1)} collective-permute-done((bf16[2,128,1024]{2,1,0:T(8,128)(2,1)S(1)}, bf16[2,128,1024]{2,1,0:T(8,128)(2,1)S(1)}, u32[]{:S(2)}, u32[]{:S(2)}) %collective-permute-start.7) | collective-permute-done | bytes 524320 | tf_op jit(solution)/shard_map/ppermute | solution.py:1190
  83.7 27.8 %collective-permute-done.6 = bf16[2,2,128,1024]{3,2,1,0:T(8,128)(2,1)} collective-permute-done((bf16[2,2,128,1024]{3,2,1,0:T(8,128)(2,1)S(1)}, bf16[2,2,128,1024]{3,2,1,0:T(8,128)(2,1)}, u32[]{:S(2)}, u32[]{:S(2)}) %collective-permute-start.6) | collective-permute-done | bytes 1048608 | tf_op jit(solution)/shard_map/ppermute | solution.py:1190
  122.2 16.2 %attend_forward.1 = (bf16[16,64,256]{2,1,0:T(8,128)(2,1)S(1)}, bf16[4096,64]{1,0:T(8,128)(2,1)S(1)}, bf16[4096,64]{1,0:T(8,128)(2,1)S(1)}, bf16[4096,64]{1,0:T(8...) custom-call(s32[1]{0:T(128)S(1)} %bitcast.147, s32[64]{0:T(128)S(1)} %get-tuple-element.96.inloc, ...), custom_call_target="tpu_custom_call" | custom-call | flops 8589934592 | bytes 8388608 | tf_op jit(solution)/shard_map/attend_forward/pallas_call | solution.py:553
  141.2 24.9 %all_to_all.20.got = bf16[16,64,256]{2,1,0:T(8,128)(2,1)} all-to-all(bf16[16,64,256]{2,1,0:T(8,128)(2,1)S(1)} %get-tuple-element.61), channel_id=1, replica_groups=mesh['head'=2,'z'=4,'x'=2,'core'=2] {'z','x','head'}, dimensions={0} | all-to-all | bytes 1048576 | tf_op jit(solution)/shard_map/all_to_all | solution.py:1366
  169.0 5.0 %project.1 = (f32[512,1024]{1,0:T(8,128)}, bf16[256,1024]{1,0:T(8,128)(2,1)}, bf16[256,1024]{1,0:T(8,128)(2,1)}, bf16[512,512]{1,0:T(8,128)(2,1)}) custom-call(s32[2,16]{1,0:T(2,128)} %fusion.32.table, bf16[16,64,256]{2,1,0:T(8,128)(2,1)} %all_to_all.20.got, bf16[16,304,1024]{2,1,0:T(8,128)(2,1)} %bitcast.149), custom_call_target="tpu_custom_call" | custom-call | flops 536870912 | bytes 4194304 | tf_op jit(solution)/shard_map/project/pallas_call | solution.py:774
  177.8 25.8 %middle.1 = (f32[512,1024]{1,0:T(8,128)}, f32[256,1024]{1,0:T(8,128)}, bf16[256,1024]{1,0:T(8,128)(2,1)}, f32[512,1024]{1,0:T(8,128)}, bf16[256,1024]{1,0:T(8,12...) custom-call(s32[2,16]{1,0:T(2,128)} %fusion.32.table, ...), custom_call_target="tpu_custom_call" | custom-call | flops 12884901888 | bytes 16777216 | tf_op jit(solution)/shard_map/middle/pallas_call | solution.py:922
  212.3 4.1 %branch_back.1 = (f32[256,1024]{1,0:T(8,128)S(1)}, bf16[512,1024]{1,0:T(8,128)(2,1)S(1)}, bf16[16,8,256]{2,1,0:T(8,128)(2,1)S(1)}, bf16[16,288,1024]{2,1,0:T(8,128)(2,1)}) custom-call(s32[2,16]{1,0:T(2,128)S(1)} %copy-done.12, f32[512,1024]{1,0:T(8,128)S(1)} %copy-done.2, bf16[256,1024]{1,0:T(8,128)(2,1)S(1)} %bitcast.144, ...), custom_call_target="tpu_custom_call", output_to_operand_aliasing={{3}: (10, {})} | custom-call | flops 536870912 | bytes 8388608 | tf_op jit(solution)/shard_map/branch_back/pallas_call | solution.py:1026
  218.0 4.3 %attention_back.1 = bf16[16,72,256]{2,1,0:T(8,128)(2,1)} custom-call(s32[2,16]{1,0:T(2,128)} %fusion.32.table, bf16[512,1024]{1,0:T(8,128)(2,1)} %copy-done.4, bf16[16,8,256]{2,1,0:T(8,128)(2,1)} %copy-done.10, bf16[16,304,1024]{2,1,0:T(8,128)(2,1)} %bitcast.151), custom_call_target="tpu_custom_call" | custom-call | flops 536870912 | bytes 2097152 | tf_op jit(solution)/shard_map/attention_back/pallas_call | solution.py:1075
  222.3 23.3 %all_to_all.21.grad_t = bf16[16,72,256]{2,1,0:T(8,128)(2,1)S(1)} all-to-all(bf16[16,72,256]{2,1,0:T(8,128)(2,1)} %attention_back.1), channel_id=1, replica_groups=mesh['head'=2,'z'=4,'x'=2,'core'=2] {'z','x','head'}, dimensions={0} | all-to-all | bytes 1179648 | tf_op jit(solution)/shard_map/all_to_all | solution.py:1393
  246.8 28.9 %attend_backward.1 = bf16[16,272,256]{2,1,0:T(8,128)(2,1)} custom-call(s32[1]{0:T(128)S(1)} %bitcast.148, s32[64]{0:T(128)S(1)} %get-tuple-element.96.inloc, s32[64]{0:T(128)S(1)} %get-tuple-element.95.outloc, bf16[16,72,256]{2,1,0:T(8,128)(2,1)S(1)} %all_to_all.21.grad_t, bf16[4096,64]{1,0:T(8,128)(2,1)S(1)} %copy-done.15, bf16[4096,64]{1,0:T(8,128)(2,1)S(1)} %copy-done.17, ...), custom_call_target="tpu_custom_call" | custom-call | flops 21474836480 | bytes 16777216 | tf_op jit(solution)/shard_map/attend_backward/pallas_call | solution.py:691
  275.7 8.2 %all-to-all-start.3 = ((bf16[16,272,256]{2,1,0:T(8,128)(2,1)}), bf16[16,272,256]{2,1,0:T(8,128)(2,1)}, u32[]{:S(2)}, u32[]{:S(2)}) async-start(bf16[16,272,256]{2,1,0:T(8,128)(2,1)} %attend_backward.1), calls=%async_computation.3 | async-start | bytes 4456448 | tf_op jit(solution)/shard_map/all_to_all | solution.py:1411
  283.9 2.4 collective-permute-start.17
  290.8 54.4 %all-to-all-done.3.got = bf16[16,272,256]{2,1,0:T(8,128)(2,1)} async-done(((bf16[16,272,256]{2,1,0:T(8,128)(2,1)}), bf16[16,272,256]{2,1,0:T(8,128)(2,1)}, u32[]{:S(2)}, u32[]{:S(2)}) %all-to-all-start.3) | async-done | bytes 2228256 | tf_op jit(solution)/shard_map/all_to_all | solution.py:1411
  346.8 3.1 collective-permute-start.21
  350.4 6.4 %finish.1 = (f32[256,1024]{1,0:T(8,128)}, bf16[256,1024]{1,0:T(8,128)(2,1)}) custom-call(bf16[16,272,256]{2,1,0:T(8,128)(2,1)} %all-to-all-done.3.got, bf16[8,192,1024]{2,1,0:T(8,128)(2,1)} %bitcast.186), custom_call_target="tpu_custom_call" | custom-call | flops 1610612736 | bytes 5242880 | tf_op jit(solution)/shard_map/finish/pallas_call | solution.py:1123
  367.0 2.2 unpack.1
  (247 shorter events, 70.2 us)
Async XLA Ops:
  7.3 161.7 %all-gather.5.cloned.1.call-start = ((), (), s32[]{:S(2)}) async-start(), calls=%async_computation.6 | async-start | bytes 10584064 | tf_op jit(solution)/shard_map/all_gather | solution.py:1355
  11.7 2.4 collective-permute-start.13
  15.4 20.1 %collective-permute-start.2 = (bf16[128,1024]{1,0:T(8,128)(2,1)S(1)}, bf16[128,1024]{1,0:T(8,128)(2,1)S(1)}, u32[]{:S(2)}, u32[]{:S(2)}) collective-permute-start(bf16[128,1024]{1,0:T(8,128)(2,1)S(1)} %get-tuple-element.112), channel_id=1, source_target_pairs={{0,8},{8,0},{4,12},{12,4},{1,9},{9,1},{5,13},{13,5},{2,10},{10,2},... | collective-permute-start | bytes 786440 | tf_op jit(solution)/shard_map/ppermute | solution.py:1190
  17.8 17.7 %collective-permute-start.3 = (bf16[128,1024]{1,0:T(8,128)(2,1)S(1)}, bf16[128,1024]{1,0:T(8,128)(2,1)S(1)}, u32[]{:S(2)}, u32[]{:S(2)}) collective-permute-start(bf16[128,1024]{1,0:T(8,128)(2,1)S(1)} %bitcast.169), channel_id=1, source_target_pairs={{0,2},{2,0},{1,3},{3,1},{4,6},{6,4},{5,7},{7,5},{8,10},{10,8},{9,1... | collective-permute-start | bytes 786440 | tf_op jit(solution)/shard_map/ppermute | solution.py:1190
  21.3 61.7 %all-to-all-start = ((bf16[32,40,192]{2,1,0:T(8,128)(2,1)}), bf16[32,40,192]{2,1,0:T(8,128)(2,1)S(1)}, u32[]{:S(2)}, u32[]{:S(2)}) async-start(bf16[32,40,192]{2,1,0:T(8,128)(2,1)} %bitcast.6), calls=%async_computation | async-start | bytes 1310720 | tf_op jit(solution)/shard_map/all_to_all | solution.py:1289
  25.9 324.5 %all-gather.7.cloned.1.call-start = ((), (), s32[]{:S(2)}) async-start(), calls=%async_computation.7 | async-start | bytes 3538944 | tf_op jit(solution)/shard_map/all_gather | solution.py:1369
  37.9 20.0 %collective-permute-start.4 = (bf16[2,128,1024]{2,1,0:T(8,128)(2,1)S(1)}, bf16[2,128,1024]{2,1,0:T(8,128)(2,1)S(1)}, u32[]{:S(2)}, u32[]{:S(2)}) collective-permute-start(bf16[2,128,1024]{2,1,0:T(8,128)(2,1)S(1)} %get-tuple-element.110), channel_id=1, source_target_pairs={{0,4},{4,0},{8,12},{12,8},{1,5},{5,1},{9,13},{13,9},{2,6},{6,2},{1... | collective-permute-start | bytes 1572872 | tf_op jit(solution)/shard_map/ppermute | solution.py:1190
  38.0 16.0 %collective-permute-start.5 = (bf16[128,1024]{1,0:T(8,128)(2,1)}, bf16[128,1024]{1,0:T(8,128)(2,1)S(1)}, u32[]{:S(2)}, u32[]{:S(2)}) collective-permute-start(bf16[128,1024]{1,0:T(8,128)(2,1)} %copy-done.29), channel_id=1, source_target_pairs={{0,16},{16,0},{1,17},{17,1},{2,18},{18,2},{3,19},{19,3},{4,20},{20... | collective-permute-start | bytes 786440 | tf_op jit(solution)/shard_map/ppermute | solution.py:1190
  59.1 19.1 %collective-permute-start.7 = (bf16[2,128,1024]{2,1,0:T(8,128)(2,1)S(1)}, bf16[2,128,1024]{2,1,0:T(8,128)(2,1)S(1)}, u32[]{:S(2)}, u32[]{:S(2)}) collective-permute-start(bf16[2,128,1024]{2,1,0:T(8,128)(2,1)S(1)} %get-tuple-element.108), channel_id=1, source_target_pairs={{0,4},{4,0},{8,12},{12,8},{1,5},{5,1},{9,13},{13,9},{2,6},{6,2},{1... | collective-permute-start | bytes 1572872 | tf_op jit(solution)/shard_map/ppermute | solution.py:1190
  62.8 48.8 %collective-permute-start.6 = (bf16[2,2,128,1024]{3,2,1,0:T(8,128)(2,1)S(1)}, bf16[2,2,128,1024]{3,2,1,0:T(8,128)(2,1)}, u32[]{:S(2)}, u32[]{:S(2)}) collective-permute-start(bf16[2,2,128,1024]{3,2,1,0:T(8,128)(2,1)S(1)} %pad_maximum_fusion), channel_id=1, source_target_pairs={{0,16},{16,0},{1,17},{17,1},{2,18},{18,2},{3,19},{19,3},{4,20},{20... | collective-permute-start | bytes 3145736 | tf_op jit(solution)/shard_map/ppermute | solution.py:1190
  79.3 37.4 %collective-permute-start.8 = (bf16[2,2,128,1024]{3,2,1,0:T(8,128)(2,1)}, bf16[2,2,128,1024]{3,2,1,0:T(8,128)(2,1)}, u32[]{:S(2)}, u32[]{:S(2)}) collective-permute-start(bf16[2,2,128,1024]{3,2,1,0:T(8,128)(2,1)} %pad_maximum_fusion.1), channel_id=1, source_target_pairs={{0,2},{2,0},{1,3},{3,1},{4,6},{6,4},{5,7},{7,5},{8,10},{10,8},{9,1... | collective-permute-start | bytes 3145736 | tf_op jit(solution)/shard_map/ppermute | solution.py:1190
  81.5 37.0 %collective-permute-start.9 = (bf16[2,2,128,1024]{3,2,1,0:T(8,128)(2,1)S(1)}, bf16[2,2,128,1024]{3,2,1,0:T(8,128)(2,1)}, u32[]{:S(2)}, u32[]{:S(2)}) collective-permute-start(bf16[2,2,128,1024]{3,2,1,0:T(8,128)(2,1)S(1)} %pad_maximum_fusion), channel_id=1, source_target_pairs={{0,1},{1,0},{2,3},{3,2},{4,5},{5,4},{6,7},{7,6},{8,9},{9,8},{10,11... | collective-permute-start | bytes 3145736 | tf_op jit(solution)/shard_map/ppermute | solution.py:1190
  83.6 37.0 %collective-permute-start.11 = (bf16[2,2,128,1024]{3,2,1,0:T(8,128)(2,1)}, bf16[2,2,128,1024]{3,2,1,0:T(8,128)(2,1)S(1)}, u32[]{:S(2)}, u32[]{:S(2)}) collective-permute-start(bf16[2,2,128,1024]{3,2,1,0:T(8,128)(2,1)} %pad_maximum_fusion.1), channel_id=1, source_target_pairs={{0,1},{1,0},{2,3},{3,2},{4,5},{5,4},{6,7},{7,6},{8,9},{9,8},{10,11... | collective-permute-start | bytes 3145736 | tf_op jit(solution)/shard_map/ppermute | solution.py:1190
  111.6 8.6 %collective-permute-start.10 = (bf16[2,2,128,1024]{3,2,1,0:T(8,128)(2,1)}, bf16[2,2,128,1024]{3,2,1,0:T(8,128)(2,1)S(1)}, u32[]{:S(2)}, u32[]{:S(2)}) collective-permute-start(bf16[2,2,128,1024]{3,2,1,0:T(8,128)(2,1)} %collective-permute-done.6), channel_id=1, source_target_pairs={{0,1},{1,0},{2,3},{3,2},{4,5},{5,4},{6,7},{7,6},{8,9},{9,8},{10,11... | collective-permute-start | bytes 3145736 | tf_op jit(solution)/shard_map/ppermute | solution.py:1190
  116.7 4.5 %collective-permute-start.12 = (bf16[2,2,128,1024]{3,2,1,0:T(8,128)(2,1)}, bf16[2,2,128,1024]{3,2,1,0:T(8,128)(2,1)S(1)}, u32[]{:S(2)}, u32[]{:S(2)}) collective-permute-start(bf16[2,2,128,1024]{3,2,1,0:T(8,128)(2,1)} %collective-permute-done.8), channel_id=1, source_target_pairs={{0,1},{1,0},{2,3},{3,2},{4,5},{5,4},{6,7},{7,6},{8,9},{9,8},{10,11... | collective-permute-start | bytes 3145736 | tf_op jit(solution)/shard_map/ppermute | solution.py:1190
  167.0 196.6 %reduce-scatter.2.cloned.1.call-start = ((), (), s32[]{:S(2)}) async-start(), calls=%async_computation.5 | async-start | bytes 10027008 | tf_op jit(solution)/shard_map/reduce_scatter | solution.py:1399
  167.1 7.5 %collective-permute-start = (bf16[2,128,1024]{2,1,0:T(8,128)(2,1)S(1)}, bf16[2,128,1024]{2,1,0:T(8,128)(2,1)S(1)}, u32[]{:S(2)}, u32[]{:S(2)}) collective-permute-start(bf16[2,128,1024]{2,1,0:T(8,128)(2,1)S(1)} %copy-done.22), channel_id=1, source_target_pairs={{0,1},{1,0},{2,3},{3,2},{4,5},{5,4},{6,7},{7,6},{8,9},{9,8},{10,11... | collective-permute-start | bytes 1572872 | tf_op jit(solution)/shard_map/ppermute | solution.py:1190
  168.3 6.3 %collective-permute-start.1 = (bf16[2,128,1024]{2,1,0:T(8,128)(2,1)S(1)}, bf16[2,128,1024]{2,1,0:T(8,128)(2,1)S(1)}, u32[]{:S(2)}, u32[]{:S(2)}) collective-permute-start(bf16[2,128,1024]{2,1,0:T(8,128)(2,1)S(1)} %copy-done.5), channel_id=1, source_target_pairs={{0,1},{1,0},{2,3},{3,2},{4,5},{5,4},{6,7},{7,6},{8,9},{9,8},{10,11... | collective-permute-start | bytes 1572872 | tf_op jit(solution)/shard_map/ppermute | solution.py:1190
  174.5 2.5 collective-permute-start.16
  204.1 2.5 collective-permute-start.19
  275.7 69.5 %all-to-all-start.3 = ((bf16[16,272,256]{2,1,0:T(8,128)(2,1)}), bf16[16,272,256]{2,1,0:T(8,128)(2,1)}, u32[]{:S(2)}, u32[]{:S(2)}) async-start(bf16[16,272,256]{2,1,0:T(8,128)(2,1)} %attend_backward.1), calls=%async_computation.3 | async-start | bytes 4456448 | tf_op jit(solution)/shard_map/all_to_all | solution.py:1411
  283.9 4.2 %collective-permute-start.17 = (bf16[256,1024]{1,0:T(8,128)(2,1)}, bf16[256,1024]{1,0:T(8,128)(2,1)}, u32[]{:S(2)}, u32[]{:S(2)}) collective-permute-start(bf16[256,1024]{1,0:T(8,128)(2,1)} %get-tuple-element.69), channel_id=1, source_target_pairs={{0,1},{1,0},{2,3},{3,2},{4,5},{5,4},{6,7},{7,6},{8,9},{9,8},{10,11... | collective-permute-start | bytes 1572872 | tf_op jit(solution)/shard_map/ppermute | solution.py:1190
  346.8 10.3 %collective-permute-start.21 = (f32[8,33,192]{2,0,1:T(8,128)S(1)}, f32[8,33,192]{2,0,1:T(8,128)S(1)}, u32[]{:S(2)}, u32[]{:S(2)}) collective-permute-start(f32[8,33,192]{2,0,1:T(8,128)S(1)} %pad_maximum_fusion.6), channel_id=1, source_target_pairs={{0,1},{1,0},{2,3},{3,2},{4,5},{5,4},{6,7},{7,6},{8,9},{9,8},{10,11... | collective-permute-start | bytes 608264 | tf_op jit(solution)/shard_map/ppermute | solution.py:1190
  356.9 4.9 %collective-permute-start.20 = (bf16[256,1024]{1,0:T(8,128)(2,1)}, bf16[256,1024]{1,0:T(8,128)(2,1)}, u32[]{:S(2)}, u32[]{:S(2)}) collective-permute-start(bf16[256,1024]{1,0:T(8,128)(2,1)} %get-tuple-element.88), channel_id=1, source_target_pairs={{0,1},{1,0},{2,3},{3,2},{4,5},{5,4},{6,7},{7,6},{8,9},{9,8},{10,11... | collective-permute-start | bytes 1572872 | tf_op jit(solution)/shard_map/ppermute | solution.py:1190
  (54 other events, 441.6 us)
Sparse Core Ops, SparseCore 0:
  15.5 148.6 all-gather.4
  167.1 38.9 all-gather.6
  218.1 139.3 reduce-scatter.1
